TPU v7x, 32 devices: a whole 2x2x4 slice. The times are simulated.
32 devices in a mesh: dp: 8 (over y, x, core), tensor: 4 (over z).
Axes of the slice: x: 2, y: 2, z: 4, core: 2. Of those that a mesh axis runs over, the one named last changes fastest.
Arguments:
- tokens: bfloat16 [8192, 1024], P(('dp', 'tensor')), may hold values from -6 to 6
- encoder_states: bfloat16 [16384, 1024], P('dp'), may hold values from -6 to 6
- tok_lengths: int32 [8, 4], P('dp'), may hold values from 1 to 512, 1024 in all within a row
- enc_lengths: int32 [8, 4], P('dp'), may hold values from 1 to 1024, 2048 in all within a row
- pad_mask: int32 [8192], P('dp'), may hold values 0 or 1
- first_gain: float32 [1024], replicated, may hold values from 0.5 to 1.5
- first_shift: float32 [1024], replicated, may hold values from -1.5 to 1.5
- causal_query: bfloat16 [1024, 1024], P(None, 'tensor'), may hold values from -0.1875 to 0.1875
- causal_key: bfloat16 [1024, 1024], P(None, 'tensor'), may hold values from -0.1875 to 0.1875
- causal_value: bfloat16 [1024, 1024], P(None, 'tensor'), may hold values from -0.1875 to 0.1875
- causal_out: bfloat16 [1024, 1024], P('tensor'), may hold values from -1.5 to 1.5
- second_gain: float32 [1024], replicated, may hold values from 0.5 to 1.5
- second_shift: float32 [1024], replicated, may hold values from -1.5 to 1.5
- cross_query: bfloat16 [1024, 1024], P(None, 'tensor'), may hold values from -0.1875 to 0.1875
- cross_key: bfloat16 [1024, 1024], P(None, 'tensor'), may hold values from -0.1875 to 0.1875
- cross_value: bfloat16 [1024, 1024], P(None, 'tensor'), may hold values from -0.1875 to 0.1875
- cross_out: bfloat16 [1024, 1024], P('tensor'), may hold values from -1.5 to 1.5
- third_gain: float32 [1024], replicated, may hold values from 0.5 to 1.5
- third_shift: float32 [1024], replicated, may hold values from -1.5 to 1.5
- expand_weight: bfloat16 [1024, 4096], P(None, 'tensor'), may hold values from -0.1875 to 0.1875
- reduce_weight: bfloat16 [4096, 1024], P('tensor'), may hold values from -0.125 to 0.125
- cotangent: bfloat16 [8192, 1024], P(('dp', 'tensor')), may hold values from -6 to 6
Outputs:
- output: bfloat16 [8192, 1024], P(('dp', 'tensor'))
- tokens_grad: bfloat16 [8192, 1024], P(('dp', 'tensor'))
- encoder_grad: bfloat16 [16384, 1024], P(('dp', 'tensor'))
- first_gain_grad: float32 [1024], replicated
- first_shift_grad: float32 [1024], replicated
- causal_query_grad: float32 [1024, 1024], P(None, 'tensor')
- causal_key_grad: float32 [1024, 1024], P(None, 'tensor')
- causal_value_grad: float32 [1024, 1024], P(None, 'tensor')
- causal_out_grad: float32 [1024, 1024], P('tensor')
- second_gain_grad: float32 [1024], replicated
- second_shift_grad: float32 [1024], replicated
- cross_query_grad: float32 [1024, 1024], P(None, 'tensor')
- cross_key_grad: float32 [1024, 1024], P(None, 'tensor')
- cross_value_grad: float32 [1024, 1024], P(None, 'tensor')
- cross_out_grad: float32 [1024, 1024], P('tensor')
- third_gain_grad: float32 [1024], replicated
- third_shift_grad: float32 [1024], replicated
- expand_weight_grad: float32 [1024, 4096], P(None, 'tensor')
- reduce_weight_grad: float32 [4096, 1024], P('tensor')
Inputs may be any that keep to these rules, and one draw needn't show every extreme that they name: `tok_lengths`: each row sums to 1024; its largest entry is exactly 512. `enc_lengths`: each row sums to 2048; its largest entry is exactly 1024.
All inputs are finite; a program needn't handle non-finite values. No bound on the sum of `pad_mask` on one device may be relied on, other than what follows from the above.
Results may differ from a plain program's by a relative error of at most 0.03.
Values may be sent and summed in bfloat16 or wider, within the bound.
A program may use at most 192 MiB of HBM per device.

v0:
```python
import jax
import jax.numpy as jnp
from jax import lax
from jax.sharding import PartitionSpec as P

HEAD_DIM = 64


eps = 1e-05
tanh_coeff = 0.7978845608
cubic_coeff = 0.044715


def smooth_gate(values):
    inner = jnp.tanh(tanh_coeff * (values + cubic_coeff * values * values * values))
    return 0.5 * values * (1.0 + inner)


def smooth_slope(values):
    inner = jnp.tanh(tanh_coeff * (values + cubic_coeff * values * values * values))
    return 0.5 * (1.0 + inner) + 0.5 * values * (1.0 - inner * inner) * tanh_coeff * (
        1.0 + 3.0 * cubic_coeff * values * values
    )


def segment_ids(lengths, count):
    ends = jnp.cumsum(lengths, dtype=jnp.int32)
    places = jnp.arange(count, dtype=jnp.int32)
    return jnp.sum((places[:, None] >= ends[None, :]).astype(jnp.int32), axis=1)


def normalize(rows, gain, shift):
    centred = rows - jnp.mean(rows, axis=1, keepdims=True)
    inverse = lax.rsqrt(jnp.mean(centred * centred, axis=1, keepdims=True) + eps)
    unit = centred * inverse
    return (unit * gain + shift, unit, inverse)


def normalize_back(grad_out, unit, inverse, gain):
    scaled = grad_out * gain
    inner = (
        scaled
        - jnp.mean(scaled, axis=1, keepdims=True)
        - unit * jnp.mean(scaled * unit, axis=1, keepdims=True)
    )
    return (inner * inverse, jnp.sum(grad_out * unit, axis=0), jnp.sum(grad_out, axis=0))


def along_rows(left, right):
    return lax.dot_general(
        left, right, (((0,), (0,)), ((), ())), preferred_element_type=jnp.float32
    )


def against(left, weight):
    return lax.dot_general(
        left, weight, (((1,), (1,)), ((), ())), preferred_element_type=jnp.float32
    )


def spread_normed(rows):
    return lax.all_gather(rows, "tensor", axis=0, tiled=True)


def spread_grads(rows):
    return lax.all_gather(rows, "tensor", axis=0, tiled=True)


def sum_branch(left, weight, rows):

    def term(start, count):
        return jnp.dot(left, weight, preferred_element_type=jnp.float32)

    return lax.psum_scatter(
        term(jnp.int32(0), lax.axis_size("tensor") * rows).astype(jnp.bfloat16),
        "tensor",
        scatter_dimension=0,
        tiled=True,
    ).astype(jnp.float32)


def sum_inputs(pairs, rows):

    def term(start, count):
        total = jnp.zeros((count, pairs[0][1].shape[0]), jnp.float32)
        for left, weight in pairs:
            total = total + against(left, weight)
        return total

    return lax.psum_scatter(
        term(jnp.int32(0), lax.axis_size("tensor") * rows).astype(jnp.bfloat16),
        "tensor",
        scatter_dimension=0,
        tiled=True,
    ).astype(jnp.float32)


def attend_forward(queries, keys, values, allowed_fn, heads, scale):
    count = queries.shape[0]
    block = min(512, count)
    blocks = count // block
    width = queries.shape[1] // heads
    query_blocks = queries.reshape(blocks, block, heads, width)
    key_heads = keys.reshape(keys.shape[0], heads, width)
    value_heads = values.reshape(values.shape[0], heads, width)
    starts = jnp.arange(blocks, dtype=jnp.int32) * block

    def one_block(pair):
        query_block, start = pair
        raw = jnp.einsum("qhd,khd->hqk", query_block, key_heads, preferred_element_type=jnp.float32)
        scores = jnp.where(allowed_fn(start, block)[None], raw * scale, -1e30)
        top = jnp.max(scores, axis=2, keepdims=True)
        expo = jnp.exp(scores - top)
        total = jnp.sum(expo, axis=2, keepdims=True)
        probs = (expo / total).astype(jnp.bfloat16)
        mixed = jnp.einsum("hqk,khd->qhd", probs, value_heads, preferred_element_type=jnp.float32)
        return (mixed.astype(jnp.bfloat16), top + jnp.log(total))

    mixed, logsum = lax.map(one_block, (query_blocks, starts))
    return (mixed.reshape(count, heads * width), logsum)


def attend_backward(queries, keys, values, grad_mixed, logsum, allowed_fn, heads, scale):
    count = queries.shape[0]
    block = min(512, count)
    blocks = count // block
    width = queries.shape[1] // heads
    query_blocks = queries.reshape(blocks, block, heads, width)
    grad_blocks = grad_mixed.reshape(blocks, block, heads, width)
    key_heads = keys.reshape(keys.shape[0], heads, width)
    value_heads = values.reshape(values.shape[0], heads, width)
    starts = jnp.arange(blocks, dtype=jnp.int32) * block

    def one_block(carry, item):
        grad_keys, grad_values = carry
        query_block, grad_block, logsum_block, start = item
        raw = jnp.einsum("qhd,khd->hqk", query_block, key_heads, preferred_element_type=jnp.float32)
        scores = jnp.where(allowed_fn(start, block)[None], raw * scale, -1e30)
        probs = jnp.exp(scores - logsum_block)
        grad_probs = jnp.einsum(
            "qhd,khd->hqk", grad_block, value_heads, preferred_element_type=jnp.float32
        )
        inner = jnp.sum(probs * grad_probs, axis=2, keepdims=True)
        grad_raw = (probs * (grad_probs - inner) * scale).astype(jnp.bfloat16)
        grad_query = jnp.einsum(
            "hqk,khd->qhd", grad_raw, key_heads, preferred_element_type=jnp.float32
        )
        grad_keys = grad_keys + jnp.einsum(
            "hqk,qhd->khd", grad_raw, query_block, preferred_element_type=jnp.float32
        )
        grad_values = grad_values + jnp.einsum(
            "hqk,qhd->khd",
            probs.astype(jnp.bfloat16),
            grad_block,
            preferred_element_type=jnp.float32,
        )
        return ((grad_keys, grad_values), grad_query)

    empty = jnp.zeros(key_heads.shape, jnp.float32)
    (grad_keys, grad_values), grad_query = lax.scan(
        one_block, (empty, empty), (query_blocks, grad_blocks, logsum, starts)
    )
    return (
        grad_query.reshape(count, heads * width).astype(jnp.bfloat16),
        grad_keys.reshape(keys.shape[0], heads * width).astype(jnp.bfloat16),
        grad_values.reshape(keys.shape[0], heads * width).astype(jnp.bfloat16),
    )


def on_device(
    tokens,
    encoder_states,
    tok_lengths,
    enc_lengths,
    pad_mask,
    first_gain,
    first_shift,
    causal_query,
    causal_key,
    causal_value,
    causal_out,
    second_gain,
    second_shift,
    cross_query,
    cross_key,
    cross_value,
    cross_out,
    third_gain,
    third_shift,
    expand_weight,
    reduce_weight,
    cotangent,
):
    share = tokens.shape[0]
    length = pad_mask.shape[0]
    frames = encoder_states.shape[0]
    heads = causal_query.shape[1] // HEAD_DIM
    scale = HEAD_DIM ** (-0.5)
    token_seg = segment_ids(tok_lengths[0], length)
    frame_seg = segment_ids(enc_lengths[0], frames)
    places = jnp.arange(length, dtype=jnp.int32)

    def causal_allowed(start, block):
        rows_here = start + jnp.arange(block, dtype=jnp.int32)
        seg_here = lax.dynamic_slice_in_dim(token_seg, start, block, 0)
        return (
            (seg_here[:, None] == token_seg[None, :])
            & (places[None, :] <= rows_here[:, None])
            & ((pad_mask[None, :] == 1) | (places[None, :] == rows_here[:, None]))
        )

    def cross_allowed(start, block):
        seg_here = lax.dynamic_slice_in_dim(token_seg, start, block, 0)
        return seg_here[:, None] == frame_seg[None, :]

    residual = tokens.astype(jnp.float32)
    first_out, first_unit, first_inv = normalize(residual, first_gain, first_shift)
    first_all = spread_normed(first_out.astype(jnp.bfloat16))
    query = jnp.dot(first_all, causal_query, preferred_element_type=jnp.float32).astype(
        jnp.bfloat16
    )
    keyed = jnp.dot(first_all, causal_key, preferred_element_type=jnp.float32).astype(jnp.bfloat16)
    valued = jnp.dot(first_all, causal_value, preferred_element_type=jnp.float32).astype(
        jnp.bfloat16
    )
    mixed, self_logsum = attend_forward(query, keyed, valued, causal_allowed, heads, scale)
    after_self = residual + sum_branch(mixed, causal_out, share)
    second_out, second_unit, second_inv = normalize(after_self, second_gain, second_shift)
    second_all = spread_normed(second_out.astype(jnp.bfloat16))
    cquery = jnp.dot(second_all, cross_query, preferred_element_type=jnp.float32).astype(
        jnp.bfloat16
    )
    ckeyed = jnp.dot(encoder_states, cross_key, preferred_element_type=jnp.float32).astype(
        jnp.bfloat16
    )
    cvalued = jnp.dot(encoder_states, cross_value, preferred_element_type=jnp.float32).astype(
        jnp.bfloat16
    )
    cmixed, cross_logsum = attend_forward(cquery, ckeyed, cvalued, cross_allowed, heads, scale)
    after_cross = after_self + sum_branch(cmixed, cross_out, share)
    third_out, third_unit, third_inv = normalize(after_cross, third_gain, third_shift)
    third_all = spread_normed(third_out.astype(jnp.bfloat16))
    pre_act = jnp.dot(third_all, expand_weight, preferred_element_type=jnp.float32)
    hidden = smooth_gate(pre_act).astype(jnp.bfloat16)
    output = (after_cross + sum_branch(hidden, reduce_weight, share)).astype(jnp.bfloat16)
    grad_res = cotangent.astype(jnp.float32)
    grad_top = spread_grads(grad_res.astype(jnp.bfloat16))
    reduce_grad = along_rows(hidden, grad_top)
    grad_hidden = against(grad_top, reduce_weight)
    grad_expand_in = (grad_hidden * smooth_slope(pre_act)).astype(jnp.bfloat16)
    expand_grad = along_rows(third_all, grad_expand_in)
    third_in = sum_inputs(((grad_expand_in, expand_weight),), share)
    back_rows, third_gain_grad, third_shift_grad = normalize_back(
        third_in, third_unit, third_inv, third_gain
    )
    grad_res = grad_res + back_rows
    grad_top = spread_grads(grad_res.astype(jnp.bfloat16))
    cross_out_grad = along_rows(cmixed, grad_top)
    grad_cmixed = against(grad_top, cross_out).astype(jnp.bfloat16)
    grad_cquery, grad_ckey, grad_cvalue = attend_backward(
        cquery, ckeyed, cvalued, grad_cmixed, cross_logsum, cross_allowed, heads, scale
    )
    cross_query_grad = along_rows(second_all, grad_cquery)
    cross_key_grad = along_rows(encoder_states, grad_ckey)
    cross_value_grad = along_rows(encoder_states, grad_cvalue)
    encoder_grad = lax.psum_scatter(
        (against(grad_ckey, cross_key) + against(grad_cvalue, cross_value)).astype(jnp.bfloat16),
        "tensor",
        scatter_dimension=0,
        tiled=True,
    )
    second_in = sum_inputs(((grad_cquery, cross_query),), share)
    back_rows, second_gain_grad, second_shift_grad = normalize_back(
        second_in, second_unit, second_inv, second_gain
    )
    grad_res = grad_res + back_rows
    grad_top = spread_grads(grad_res.astype(jnp.bfloat16))
    causal_out_grad = along_rows(mixed, grad_top)
    grad_mixed = against(grad_top, causal_out).astype(jnp.bfloat16)
    grad_query, grad_key, grad_value = attend_backward(
        query, keyed, valued, grad_mixed, self_logsum, causal_allowed, heads, scale
    )
    causal_query_grad = along_rows(first_all, grad_query)
    causal_key_grad = along_rows(first_all, grad_key)
    causal_value_grad = along_rows(first_all, grad_value)
    first_in = sum_inputs(
        ((grad_query, causal_query), (grad_key, causal_key), (grad_value, causal_value)), share
    )
    back_rows, first_gain_grad, first_shift_grad = normalize_back(
        first_in, first_unit, first_inv, first_gain
    )
    tokens_grad = (grad_res + back_rows).astype(jnp.bfloat16)
    (
        causal_query_grad,
        causal_key_grad,
        causal_value_grad,
        causal_out_grad,
        cross_query_grad,
        cross_key_grad,
        cross_value_grad,
        cross_out_grad,
        expand_grad,
        reduce_grad,
    ) = lax.psum(
        (
            causal_query_grad,
            causal_key_grad,
            causal_value_grad,
            causal_out_grad,
            cross_query_grad,
            cross_key_grad,
            cross_value_grad,
            cross_out_grad,
            expand_grad,
            reduce_grad,
        ),
        "dp",
    )
    (
        first_gain_grad,
        first_shift_grad,
        second_gain_grad,
        second_shift_grad,
        third_gain_grad,
        third_shift_grad,
    ) = lax.psum(
        (
            first_gain_grad,
            first_shift_grad,
            second_gain_grad,
            second_shift_grad,
            third_gain_grad,
            third_shift_grad,
        ),
        ("dp", "tensor"),
    )
    return (
        output,
        tokens_grad,
        encoder_grad,
        first_gain_grad,
        first_shift_grad,
        causal_query_grad,
        causal_key_grad,
        causal_value_grad,
        causal_out_grad,
        second_gain_grad,
        second_shift_grad,
        cross_query_grad,
        cross_key_grad,
        cross_value_grad,
        cross_out_grad,
        third_gain_grad,
        third_shift_grad,
        expand_grad,
        reduce_grad,
    )


def solution(mesh):
    in_specs = (
        P(("dp", "tensor"), None),
        P("dp", None),
        P("dp", None),
        P("dp", None),
        P("dp"),
        P(),
        P(),
        P(None, "tensor"),
        P(None, "tensor"),
        P(None, "tensor"),
        P("tensor", None),
        P(),
        P(),
        P(None, "tensor"),
        P(None, "tensor"),
        P(None, "tensor"),
        P("tensor", None),
        P(),
        P(),
        P(None, "tensor"),
        P("tensor", None),
        P(("dp", "tensor"), None),
    )
    out_specs = (
        P(("dp", "tensor"), None),
        P(("dp", "tensor"), None),
        P(("dp", "tensor"), None),
        P(),
        P(),
        P(None, "tensor"),
        P(None, "tensor"),
        P(None, "tensor"),
        P("tensor", None),
        P(),
        P(),
        P(None, "tensor"),
        P(None, "tensor"),
        P(None, "tensor"),
        P("tensor", None),
        P(),
        P(),
        P(None, "tensor"),
        P("tensor", None),
    )
    return jax.shard_map(
        on_device, mesh=mesh, in_specs=in_specs, out_specs=out_specs, check_vma=False
    )
```

profile of v0, /device:TPU:1, one launch (start us, length us, event | category | flops | bytes accessed | tf_op | source)
XLA Modules:
  0.0 1276.3 jit_solution(7370262960131817720)
XLA Ops:
  13.6 47.2 %all-gather.7.cloned.1.call-done = bf16[1024,1024]{1,0:T(8,128)(2,1)} async-done(((bf16[256,1024]{1,0:T(8,128)(2,1)}), bf16[1024,1024]{1,0:T(8,128)(2,1)}) %all-gather.7.cloned.1.call-update) | async-done | bytes 2097168 | tf_op jit(solution)/shard_map/all_gather | solution.py:62
  60.8 3.2 convolution_convert_fusion.12
  67.4 3.2 convolution_convert_fusion.10
  70.6 3.2 convolution_convert_fusion.11
  74.5 27.2 %while.58 = (s32[]{:T(128)}, bf16[2,512,4,64]{1,3,2,0:T(8,128)(2,1)S(1)}, f32[2,4,512,1]{2,1,3,0:T(4,128)}, s32[2]{0:T(128)S(1)}, s32[1024]{0:T(1024)S(1)}, /*in...) while((s32[]{:T(128)}, ...), condition=%wide.region_7.8_spmd.clone.clone, body=%wide.region_4.0_spmd.clone.clone.sunk | while | flops 565313024 | bytes 28922048 | solution.py:119
  78.7 2.8 fusion.357
  83.8 3.7 fusion.359
  92.3 2.8 fusion.357
  97.4 3.7 fusion.359
  103.1 3.1 convolution_convert_fusion.6
  106.3 42.5 %reduce-scatter.8.cloned.1.call-done = bf16[256,1024]{1,0:T(8,128)(2,1)} async-done(((bf16[1024,1024]{1,0:T(8,128)(2,1)}), bf16[256,1024]{1,0:T(8,128)(2,1)}) %reduce-scatter.8.cloned.1.call-update) | async-done | bytes 524304 | tf_op jit(solution)/shard_map/reduce_scatter | solution.py:74
  154.3 3.8 convolution_convert_fusion.1
  160.3 38.9 %all-gather.9.cloned.1.call-done = bf16[1024,1024]{1,0:T(8,128)(2,1)} async-done(((bf16[256,1024]{1,0:T(8,128)(2,1)}), bf16[1024,1024]{1,0:T(8,128)(2,1)}) %all-gather.9.cloned.1.call-update) | async-done | bytes 2097168 | tf_op jit(solution)/shard_map/all_gather | solution.py:62
  199.2 3.2 convolution_convert_fusion.9
  202.4 2.8 reshape.531
  208.3 35.3 %while.57 = (s32[]{:T(128)}, bf16[2,512,4,64]{1,3,2,0:T(8,128)(2,1)}, f32[2,4,512,1]{2,1,3,0:T(4,128)S(1)}, s32[2]{0:T(128)S(1)}, s32[1024]{0:T(1024)S(1)}, /*in...) while((s32[]{:T(128)}, ...), condition=%wide.region_16.17_spmd, body=%wide.region_13.16_spmd.sunk | while | flops 1125251072 | bytes 65616140 | solution.py:119
  211.5 4.4 fusion.351
  216.0 4.3 fusion.352
  220.4 4.8 fusion.353
  229.2 4.4 fusion.351
  233.7 4.3 fusion.352
  238.0 4.8 fusion.353
  246.1 3.1 convolution_convert_fusion.5
  249.2 9.8 all-gather.11.cloned.1.call-start
  259.0 32.8 %reduce-scatter.10.cloned.1.call-done = bf16[256,1024]{1,0:T(8,128)(2,1)} async-done(((bf16[1024,1024]{1,0:T(8,128)(2,1)}), bf16[256,1024]{1,0:T(8,128)(2,1)}) %reduce-scatter.10.cloned.1.call-update) | async-done | bytes 524304 | tf_op jit(solution)/shard_map/reduce_scatter | solution.py:74
  296.1 44.9 %all-gather.11.cloned.1.call-done = bf16[1024,1024]{1,0:T(8,128)(2,1)} async-done(((bf16[256,1024]{1,0:T(8,128)(2,1)}), bf16[1024,1024]{1,0:T(8,128)(2,1)}) %all-gather.11.cloned.1.call-update) | async-done | bytes 2097168 | tf_op jit(solution)/shard_map/all_gather | solution.py:62
  341.1 5.9 fusion.228
  347.0 40.2 %all-gather.13.cloned.1.call-done = bf16[1024,1024]{1,0:T(8,128)(2,1)} async-done(((bf16[256,1024]{1,0:T(8,128)(2,1)}), bf16[1024,1024]{1,0:T(8,128)(2,1)}) %all-gather.13.cloned.1.call-update) | async-done | bytes 2097168 | tf_op jit(solution)/shard_map/all_gather | solution.py:66
  387.2 7.7 fusion.188
  396.2 3.7 convolution_convert_fusion.3
  400.0 6.9 convolution_convert_fusion.4
  407.0 35.5 %reduce-scatter.14.cloned.1.call-done = bf16[256,1024]{1,0:T(8,128)(2,1)} async-done(((bf16[1024,1024]{1,0:T(8,128)(2,1)}), bf16[256,1024]{1,0:T(8,128)(2,1)}) %reduce-scatter.14.cloned.1.call-update) | async-done | bytes 524304 | tf_op jit(solution)/shard_map/reduce_scatter | solution.py:90
  444.7 43.5 %reduce-scatter.12.cloned.1.call-done = bf16[256,1024]{1,0:T(8,128)(2,1)} async-done(((bf16[1024,1024]{1,0:T(8,128)(2,1)}), bf16[256,1024]{1,0:T(8,128)(2,1)}) %reduce-scatter.12.cloned.1.call-update) | async-done | bytes 524304 | tf_op jit(solution)/shard_map/reduce_scatter | solution.py:74
  488.2 3.0 fusion.225
  491.3 45.5 %all-gather.15.cloned.1.call-done = bf16[1024,1024]{1,0:T(8,128)(2,1)} async-done(((bf16[256,1024]{1,0:T(8,128)(2,1)}), bf16[1024,1024]{1,0:T(8,128)(2,1)}) %all-gather.15.cloned.1.call-update) | async-done | bytes 2097168 | tf_op jit(solution)/shard_map/all_gather | solution.py:66
  536.8 3.2 convolution_convert_fusion.8
  544.2 144.3 %while.59 = (s32[]{:T(128)}, f32[2048,4,64]{0,2,1:T(8,128)}, f32[2048,4,64]{0,2,1:T(8,128)}, bf16[2,512,4,64]{1,3,2,0:T(8,128)(2,1)}, bf16[2,512,4,64]{1,3,2,0:T...) while((s32[]{:T(128)}, f32[2048,4,64]{0,2,1:T(8,128)}, ...), condition=%wide.region_26.27_spmd.clone, body=%wide.region_24.26_spmd.clone.sunk | while | flops 2796560384 | bytes 273226016 | solution.py:160
  547.9 3.4 fusion.371
  551.3 6.4 fusion.373
  557.7 8.1 fusion.370
  565.8 24.0 %fusion.374 = bf16[2,512,4,64]{1,3,2,0:T(8,128)(2,1)} fusion(bf16[2,512,4,64]{1,3,2,0:T(8,128)(2,1)} %get-tuple-element.1085, s32[]{:T(128)S(6)} %copy.121, bf16[2048,4,64]{0,2,1:T(8,128)(2,1)S(1)} %get-tuple-element.1105, f32[4,512,2048]{2,1,0:T(8,128)} %fusion.370, f32[4,512,2048]{2,1,0:T(8,128)} %copy-done.2, ...), kind=kOutput, calls=%fused_computation.66.clone.1 | convolution fusion | flops 583012352 | bytes 70795264 | tf_op jit(solution)/shard_map/while/body/eval_jaxpr/hqk,khd->qhd/dot_general | solution.py:145
  589.8 25.5 %fusion.372 = f32[2048,4,64]{0,2,1:T(8,128)} fusion(f32[4,512,2048]{2,1,0:T(8,128)} %fusion.370, f32[4,512,2048]{2,1,0:T(8,128)} %copy-done.2, f32[4,512]{1,0:T(4,128)S(1)} %dynamic-slice_bitcast_fusion.4, pred[512,2048]{1,0:T(8,128)(4,1)S(1)} %broadcast_compare_fusion.10, f32[2048,4,64]{0,2,1:T(8,128)} %get-tuple-element.1083, pred[]{:T(512)S(6)} %compare.6, ...), kind=kOutput, calls=%fused_computation.63.clone.1 | convolution fusion | flops 584060928 | bytes 73678856 | tf_op jit(solution)/shard_map/while/body/eval_jaxpr/hqk,qhd->khd/dot_general | solution.py:148
  618.5 3.4 fusion.371
  621.9 8.3 fusion.373
  630.2 8.1 fusion.370
  638.3 24.0 %fusion.374 = bf16[2,512,4,64]{1,3,2,0:T(8,128)(2,1)} fusion(bf16[2,512,4,64]{1,3,2,0:T(8,128)(2,1)} %get-tuple-element.1085, s32[]{:T(128)S(6)} %copy.121, bf16[2048,4,64]{0,2,1:T(8,128)(2,1)S(1)} %get-tuple-element.1105, f32[4,512,2048]{2,1,0:T(8,128)} %fusion.370, f32[4,512,2048]{2,1,0:T(8,128)} %copy-done.2, ...), kind=kOutput, calls=%fused_computation.66.clone.1 | convolution fusion | flops 583012352 | bytes 70795264 | tf_op jit(solution)/shard_map/while/body/eval_jaxpr/hqk,khd->qhd/dot_general | solution.py:145
  662.3 26.1 %fusion.372 = f32[2048,4,64]{0,2,1:T(8,128)} fusion(f32[4,512,2048]{2,1,0:T(8,128)} %fusion.370, f32[4,512,2048]{2,1,0:T(8,128)} %copy-done.2, f32[4,512]{1,0:T(4,128)S(1)} %dynamic-slice_bitcast_fusion.4, pred[512,2048]{1,0:T(8,128)(4,1)S(1)} %broadcast_compare_fusion.10, f32[2048,4,64]{0,2,1:T(8,128)} %get-tuple-element.1083, pred[]{:T(512)S(6)} %compare.6, ...), kind=kOutput, calls=%fused_computation.63.clone.1 | convolution fusion | flops 584060928 | bytes 73678856 | tf_op jit(solution)/shard_map/while/body/eval_jaxpr/hqk,qhd->khd/dot_general | solution.py:148
  690.3 3.4 convolution_convert_fusion.2
  693.8 42.5 %reduce-scatter.16.cloned.1.call-done = bf16[256,1024]{1,0:T(8,128)(2,1)} async-done(((bf16[1024,1024]{1,0:T(8,128)(2,1)}), bf16[256,1024]{1,0:T(8,128)(2,1)}) %reduce-scatter.16.cloned.1.call-update) | async-done | bytes 524304 | tf_op jit(solution)/shard_map/reduce_scatter | solution.py:90
  740.8 45.5 %all-gather.17.cloned.1.call-done = bf16[1024,1024]{1,0:T(8,128)(2,1)} async-done(((bf16[256,1024]{1,0:T(8,128)(2,1)}), bf16[1024,1024]{1,0:T(8,128)(2,1)}) %all-gather.17.cloned.1.call-update) | async-done | bytes 2097168 | tf_op jit(solution)/shard_map/all_gather | solution.py:66
  789.7 105.7 %while.60 = (s32[]{:T(128)}, f32[1024,4,64]{0,2,1:T(8,128)}, f32[1024,4,64]{0,2,1:T(8,128)}, bf16[2,512,4,64]{1,3,2,0:T(8,128)(2,1)S(1)}, bf16[2,512,4,64]{1,3,2...) while((s32[]{:T(128)}, f32[1024,4,64]{0,2,1:T(8,128)}, ...), condition=%wide.region_32.33_spmd.clone.clone, body=%wide.region_30.32_spmd.clone.clone.sunk | while | flops 1400905216 | bytes 144781648 | solution.py:160
  800.4 5.9 fusion.385
  806.3 17.2 %fusion.390 = bf16[2,512,4,64]{1,3,2,0:T(8,128)(2,1)S(1)} fusion(bf16[2,512,4,64]{1,3,2,0:T(8,128)(2,1)S(1)} %get-tuple-element.1130, s32[]{:T(128)S(6)} %copy.133, bf16[1024,4,64]{0,2,1:T(8,128)(2,1)} %get-tuple-element.1150, f32[4,512,1024]{2,1,0:T(8,128)} %fusion.385, f32[4,512,1024]{2,1,0:T(8,128)} %copy-done.3, ...), kind=kOutput, calls=%fused_computation.118.clone.1 | convolution fusion | flops 291507200 | bytes 35667972 | tf_op jit(solution)/shard_map/while/body/eval_jaxpr/hqk,khd->qhd/dot_general | solution.py:145
  823.4 19.0 %fusion.388 = f32[1024,4,64]{0,2,1:T(8,128)} fusion(f32[4,512,1024]{2,1,0:T(8,128)} %fusion.385, f32[4,512,1024]{2,1,0:T(8,128)} %copy-done.3, f32[4,512]{1,0:T(4,128)S(1)} %dynamic-slice_bitcast_fusion.5, pred[512,1024]{1,0:T(8,128)(4,1)S(1)} %fusion.387, f32[1024,4,64]{0,2,1:T(8,128)} %get-tuple-element.1128, pred[]{:T(512)S(6)} %compare.7, ...), kind=kOutput, calls=%fused_computation.115.clone.1 | convolution fusion | flops 292031488 | bytes 36978692 | tf_op jit(solution)/shard_map/while/body/eval_jaxpr/hqk,qhd->khd/dot_general | solution.py:148
  853.0 5.9 fusion.385
  858.9 17.2 %fusion.390 = bf16[2,512,4,64]{1,3,2,0:T(8,128)(2,1)S(1)} fusion(bf16[2,512,4,64]{1,3,2,0:T(8,128)(2,1)S(1)} %get-tuple-element.1130, s32[]{:T(128)S(6)} %copy.133, bf16[1024,4,64]{0,2,1:T(8,128)(2,1)} %get-tuple-element.1150, f32[4,512,1024]{2,1,0:T(8,128)} %fusion.385, f32[4,512,1024]{2,1,0:T(8,128)} %copy-done.3, ...), kind=kOutput, calls=%fused_computation.118.clone.1 | convolution fusion | flops 291507200 | bytes 35667972 | tf_op jit(solution)/shard_map/while/body/eval_jaxpr/hqk,khd->qhd/dot_general | solution.py:145
  876.1 19.2 %fusion.388 = f32[1024,4,64]{0,2,1:T(8,128)} fusion(f32[4,512,1024]{2,1,0:T(8,128)} %fusion.385, f32[4,512,1024]{2,1,0:T(8,128)} %copy-done.3, f32[4,512]{1,0:T(4,128)S(1)} %dynamic-slice_bitcast_fusion.5, pred[512,1024]{1,0:T(8,128)(4,1)S(1)} %fusion.387, f32[1024,4,64]{0,2,1:T(8,128)} %get-tuple-element.1128, pred[]{:T(512)S(6)} %compare.7, ...), kind=kOutput, calls=%fused_computation.115.clone.1 | convolution fusion | flops 292031488 | bytes 36978692 | tf_op jit(solution)/shard_map/while/body/eval_jaxpr/hqk,qhd->khd/dot_general | solution.py:148
  901.4 6.8 fusion.238
  908.2 4.8 fusion.222
  932.5 3.4 add_convert_fusion
  935.9 7.9 reduce-scatter.18.cloned.1.call-done
  945.5 41.4 %all-reduce = (f32[1024]{0:T(1024)}, f32[1024]{0:T(1024)}, f32[1024]{0:T(1024)}, f32[1024]{0:T(1024)}, f32[1024]{0:T(1024)}, /*index=5*/f32[1024]{0:T(1024)}) all-reduce(f32[1024]{0:T(1024)S(1)} %get-tuple-element.610, f32[1024]{0:T(1024)S(1)} %get-tuple-element.617, ...), channel_id=1, replica_groups=mesh['dp'=8,'tensor'=4] {'dp','tensor'}, use_global_device_ids=true, to_apply=%region_38.39 | all-reduce | flops 6144 | bytes 49152 | tf_op jit(solution)/shard_map/psum | solution.py:326
  989.2 185.7 %all-reduce.4.cloned.1.call-done = (f32[1024,256]{1,0:T(8,128)}, f32[1024,256]{1,0:T(8,128)}, f32[1024,256]{1,0:T(8,128)}, f32[256,1024]{1,0:T(8,128)}, f32[1024...) async-done(((f32[1024,256]{1,0:T(8,128)}, f32[1024,256]{1,0:T(8,128)}, ...) | async-done | bytes 16777232 | tf_op jit(solution)/shard_map/psum | solution.py:304
  1180.1 74.9 %reduce-scatter.20.cloned.1.call-done = bf16[512,1024]{1,0:T(8,128)(2,1)} async-done(((bf16[2048,1024]{1,0:T(8,128)(2,1)}), bf16[512,1024]{1,0:T(8,128)(2,1)}) %reduce-scatter.20.cloned.1.call-update) | async-done | bytes 1048592 | tf_op jit(solution)/shard_map/reduce_scatter | solution.py:266
  (312 shorter events, 130.0 us)
Async XLA Ops:
  7.2 333.9 %copy-start = (bf16[1024,1024]{1,0:T(8,128)(2,1)S(1)}, bf16[1024,1024]{1,0:T(8,128)(2,1)}, u32[]{:S(2)}) copy-start(bf16[1024,1024]{1,0:T(8,128)(2,1)} %param.49) | copy-start | bytes 6291460
  7.2 53.6 %all-gather.7.cloned.1.call-start = ((), (), s32[]{:S(2)}) async-start(), calls=%async_computation.7 | async-start | bytes 2621440 | tf_op jit(solution)/shard_map/all_gather | solution.py:62
  12.7 136.2 %reduce-scatter.8.cloned.1.call-start = ((), (), s32[]{:S(2)}) async-start(), calls=%async_computation.8 | async-start | bytes 2621440 | tf_op jit(solution)/shard_map/reduce_scatter | solution.py:74
  66.1 8.4 copy-start.46
  101.7 47.2 %copy-start.4 = (bf16[256,1024]{1,0:T(8,128)(2,1)S(1)}, bf16[256,1024]{1,0:T(8,128)(2,1)}, u32[]{:S(2)}) copy-start(bf16[256,1024]{1,0:T(8,128)(2,1)} %param.30) | copy-start | bytes 1572868
  102.2 49.3 %copy-start.50 = (f32[1024]{0:T(1024)S(1)}, f32[1024]{0:T(1024)}, u32[]{:S(2)}) copy-start(f32[1024]{0:T(1024)} %param.41) | copy-start | bytes 12292
  102.2 49.2 %copy-start.62 = (f32[1024]{0:T(1024)S(1)}, f32[1024]{0:T(1024)}, u32[]{:S(2)}) copy-start(f32[1024]{0:T(1024)} %param.42) | copy-start | bytes 12292
  103.1 50.8 %copy-start.67 = (s32[1,4]{1,0:T(1,128)S(1)}, s32[1,4]{1,0:T(1,128)}, u32[]{:S(2)}) copy-start(s32[1,4]{1,0:T(1,128)} %param.33) | copy-start | bytes 52
  106.3 92.9 %all-gather.9.cloned.1.call-start = ((), (), s32[]{:S(2)}) async-start(), calls=%async_computation.9 | async-start | bytes 2621440 | tf_op jit(solution)/shard_map/all_gather | solution.py:62
  150.1 4.0 copy-start.54
  153.6 138.2 %reduce-scatter.10.cloned.1.call-start = ((), (), s32[]{:S(2)}) async-start(), calls=%async_computation.10 | async-start | bytes 2621440 | tf_op jit(solution)/shard_map/reduce_scatter | solution.py:74
  154.2 3.8 copy-start.40
  154.3 3.8 copy-start.64
  216.0 4.4 copy-start.9
  216.0 4.4 copy-start.31
  233.7 4.4 copy-start.9
  233.7 4.4 copy-start.31
  246.1 48.4 %copy-start.48 = (f32[1024]{0:T(1024)S(1)}, f32[1024]{0:T(1024)}, u32[]{:S(2)}) copy-start(f32[1024]{0:T(1024)} %param.47) | copy-start | bytes 12292
  246.1 48.4 %copy-start.63 = (f32[1024]{0:T(1024)S(1)}, f32[1024]{0:T(1024)}, u32[]{:S(2)}) copy-start(f32[1024]{0:T(1024)} %param.48) | copy-start | bytes 12292
  249.2 91.8 %all-gather.11.cloned.1.call-start = ((), (), s32[]{:S(2)}) async-start(), calls=%async_computation.11 | async-start | bytes 2621440 | tf_op jit(solution)/shard_map/all_gather | solution.py:62
  295.5 91.7 %all-gather.13.cloned.1.call-start = ((), (), s32[]{:S(2)}) async-start(), calls=%async_computation.13 | async-start | bytes 2621440 | tf_op jit(solution)/shard_map/all_gather | solution.py:66
  296.1 146.5 %reduce-scatter.14.cloned.1.call-start = ((), (), s32[]{:S(2)}) async-start(), calls=%async_computation.14 | async-start | bytes 2621440 | tf_op jit(solution)/shard_map/reduce_scatter | solution.py:90
  400.0 42.6 %copy-start.8 = (f32[256,1024]{1,0:T(8,128)S(1)}, f32[256,1024]{1,0:T(8,128)}, u32[]{:S(2)}) copy-start(f32[256,1024]{1,0:T(8,128)} %copy-done.7) | copy-start | bytes 3145732
  400.0 88.2 %copy-start.28 = (bf16[256,1024]{1,0:T(8,128)(2,1)S(1)}, bf16[256,1024]{1,0:T(8,128)(2,1)}, u32[]{:S(2)}) copy-start(bf16[256,1024]{1,0:T(8,128)(2,1)} %param.51) | copy-start | bytes 1572868
  400.0 88.2 %reduce-scatter.12.cloned.1.call-start = ((), (), s32[]{:S(2)}) async-start(), calls=%async_computation.12 | async-start | bytes 2621440 | tf_op jit(solution)/shard_map/reduce_scatter | solution.py:74
  407.0 129.8 %all-gather.15.cloned.1.call-start = ((), (), s32[]{:S(2)}) async-start(), calls=%async_computation.15 | async-start | bytes 2621440 | tf_op jit(solution)/shard_map/all_gather | solution.py:66
  491.2 245.1 %reduce-scatter.16.cloned.1.call-start = ((), (), s32[]{:S(2)}) async-start(), calls=%async_computation.16 | async-start | bytes 2621440 | tf_op jit(solution)/shard_map/reduce_scatter | solution.py:90
  491.3 52.9 %copy-start.10 = (bf16[2048,4,64]{0,2,1:T(8,128)(2,1)S(1)}, bf16[2048,4,64]{0,2,1:T(8,128)(2,1)}, u32[]{:S(2)}) copy-start(bf16[2048,4,64]{0,2,1:T(8,128)(2,1)} %get-tuple-element.1211) | copy-start | bytes 3145732
  551.3 6.4 copy-start.2
  621.9 8.3 copy-start.2
  688.5 47.8 %copy-start.5 = (bf16[256,1024]{1,0:T(8,128)(2,1)S(1)}, bf16[256,1024]{1,0:T(8,128)(2,1)}, u32[]{:S(2)}) copy-start(bf16[256,1024]{1,0:T(8,128)(2,1)} %param.30) | copy-start | bytes 1572868
  688.5 47.8 %copy-start.11 = (bf16[256,1024]{1,0:T(8,128)(2,1)S(1)}, bf16[256,1024]{1,0:T(8,128)(2,1)}, u32[]{:S(2)}) copy-start(bf16[256,1024]{1,0:T(8,128)(2,1)} %reduce-scatter.8.cloned.1.call-done) | copy-start | bytes 1572868
  688.5 47.8 %copy-start.51 = (f32[1024]{0:T(1024)S(1)}, f32[1024]{0:T(1024)}, u32[]{:S(2)}) copy-start(f32[1024]{0:T(1024)} %param.41) | copy-start | bytes 12292
  688.5 47.7 %copy-start.55 = (f32[256]{0:T(256)S(1)}, f32[256]{0:T(256)}, u32[]{:S(2)}) copy-start(f32[256]{0:T(256)} %copy-done.54) | copy-start | bytes 3076
  688.6 47.7 %copy-start.61 = (f32[256]{0:T(256)S(1)}, f32[256]{0:T(256)}, u32[]{:S(2)}) copy-start(f32[256]{0:T(256)} %copy-done.60) | copy-start | bytes 3076
  690.2 47.7 %copy-start.25 = (f32[256,1024]{1,0:T(8,128)S(1)}, f32[256,1024]{1,0:T(8,128)}, u32[]{:S(2)}) copy-start(f32[256,1024]{1,0:T(8,128)} %get-tuple-element.721) | copy-start | bytes 3145732
  690.3 50.3 %copy-start.18 = (bf16[32,8,2,512]{3,1,2,0:T(8,128)(2,1)}, bf16[32,8,2,512]{3,1,2,0:T(8,128)(2,1)S(1)}, u32[]{:S(2)}) copy-start(bf16[32,8,2,512]{3,1,2,0:T(8,128)(2,1)S(1)} %copy.91) | copy-start | bytes 1572868
  693.7 92.6 %copy-start.45 = (bf16[256,1024]{1,0:T(8,128)(2,1)S(1)}, bf16[256,1024]{1,0:T(8,128)(2,1)}, u32[]{:S(2)}) copy-start(bf16[256,1024]{1,0:T(8,128)(2,1)} %param.40) | copy-start | bytes 1572868
  693.7 92.6 %all-gather.17.cloned.1.call-start = ((), (), s32[]{:S(2)}) async-start(), calls=%async_computation.17 | async-start | bytes 2621440 | tf_op jit(solution)/shard_map/all_gather | solution.py:66
  740.7 203.2 %reduce-scatter.18.cloned.1.call-start = ((), (), s32[]{:S(2)}) async-start(), calls=%async_computation.18 | async-start | bytes 2621440 | tf_op jit(solution)/shard_map/reduce_scatter | solution.py:90
  740.8 49.0 %copy-start.47 = (s32[1024]{0:T(1024)S(1)}, s32[1024]{0:T(1024)}, u32[]{:S(2)}) copy-start(s32[1024]{0:T(1024)} %param.34) | copy-start | bytes 12292
  800.4 5.9 copy-start.34
  853.0 5.9 copy-start.34
  901.3 273.6 %all-reduce.4.cloned.1.call-start = ((), (), s32[]{:S(2)}) async-start(), calls=%async_computation.20 | async-start | bytes 33554432 | tf_op jit(solution)/shard_map/psum | solution.py:304
  901.3 6.8 copy-start.66
  901.3 6.8 copy-start.68
  908.1 4.8 copy-start.30
  908.1 5.0 copy-start.29
  914.7 5.7 copy-start.20
  920.4 3.9 copy-start.6
  929.6 325.3 %reduce-scatter.20.cloned.1.call-start = ((), (), s32[]{:S(2)}) async-start(), calls=%async_computation.19 | async-start | bytes 5242880 | tf_op jit(solution)/shard_map/reduce_scatter | solution.py:266
  935.9 8.0 copy-start.49
  935.9 8.0 copy-start.53
  935.9 8.0 copy-start.57
  935.9 9.6 copy-start.58
  935.9 9.6 copy-start.59
  935.9 51.0 %copy-start.24 = (f32[256,1024]{1,0:T(8,128)S(1)}, f32[256,1024]{1,0:T(8,128)}, u32[]{:S(2)}) copy-start(f32[256,1024]{1,0:T(8,128)} %get-tuple-element.719) | copy-start | bytes 3145732
  1174.9 80.1 %copy-start.39 = (f32[1024,256]{1,0:T(8,128)S(1)}, f32[1024,256]{1,0:T(8,128)}, u32[]{:S(2)}) copy-start(f32[1024,256]{1,0:T(8,128)} %get-tuple-element.1162) | copy-start | bytes 3145732
  1177.5 83.2 %copy-start.38 = (f32[256,1024]{1,0:T(8,128)S(1)}, f32[256,1024]{1,0:T(8,128)}, u32[]{:S(2)}) copy-start(f32[256,1024]{1,0:T(8,128)} %get-tuple-element.1165) | copy-start | bytes 3145732
  1255.0 6.7 copy-start.37
  1255.9 6.7 copy-start.36
  1258.3 5.3 copy-start.23
  1263.6 3.7 copy-start.22
  1263.6 5.7 copy-start.1
  (28 other events, 59.4 us)
Sparse Core Ops, SparseCore 0:
  12.8 48.0 all-gather.6
  106.4 42.3 reduce-scatter.7
  153.8 45.4 all-gather.8
  249.3 42.4 reduce-scatter.9
  295.6 45.4 all-gather.10
  342.5 44.6 all-gather.12
  400.1 42.4 reduce-scatter.13
  444.9 43.1 reduce-scatter.11
  491.3 45.3 all-gather.14
  693.9 42.3 reduce-scatter.15
  740.8 45.4 all-gather.16
  901.4 42.4 reduce-scatter.17
  951.4 223.4 all-reduce.3
  1178.3 76.6 reduce-scatter.19
where the time goes:
time: 1290 us; the launch traced here: 1280 us
  waiting for transfers between devices  728 us (56%)
  matrix products  357 us (28%)
  local copies, waits for them, and re-layouts  54.8 us (4%)
  other arithmetic  52.1 us (4%)
  blocking collectives  41.4 us (3%)
  loops' own time  16.7 us (1%)
  between operations  15.2 us (1%)
    psum x1, waiting for transfers between devices, on_device(): lax.psum((causal_query_grad, causal_key_grad, causal_value_grad, causal_o...  186 us
    all_gather x3, waiting for transfers between devices, spread_grads(): return lax.all_gather(rows, 'tensor', axis=0, tiled=True)  131 us
    all_gather x3, waiting for transfers between devices, spread_normed(): return lax.all_gather(rows, 'tensor', axis=0, tiled=True)  131 us
    reduce_scatter x3, waiting for transfers between devices, sum_branch(): lax.psum_scatter(term(jnp.int32(0), lax.axis_size('tensor') * rows).astyp...  119 us
    dot_general x4, matrix products, one_block(): jnp.einsum('hqk,qhd->khd', grad_raw, query_block, preferred_element_type=...  89.7 us
    reduce_scatter x3, waiting for transfers between devices, sum_inputs(): lax.psum_scatter(term(jnp.int32(0), lax.axis_size('tensor') * rows).astyp...  85.9 us
    dot_general x4, matrix products, one_block(): jnp.einsum('hqk,khd->qhd', grad_raw, key_heads, preferred_element_type=jn...  82.3 us
    reduce_scatter x1, waiting for transfers between devices, on_device(): lax.psum_scatter((against(grad_ckey, cross_key) + against(grad_cvalue, cr...  74.9 us
  transfers between devices with their start and end apart: 14, of which 14 were waited for; matrix products, arithmetic and copies ran while one was open for 5% of the time, Pallas kernels for 0%

commit v1 on v0

--- a/solution.py
+++ b/solution.py
@@ -1,6 +1,10 @@
+import functools
+
 import jax
 import jax.numpy as jnp
 from jax import lax
+from jax.experimental import pallas as pl
+from jax.experimental.pallas import tpu as pltpu
 from jax.sharding import PartitionSpec as P
 
 HEAD_DIM = 64
@@ -95,76 +99,164 @@
     ).astype(jnp.float32)
 
 
-def attend_forward(queries, keys, values, allowed_fn, heads, scale):
-    count = queries.shape[0]
-    block = min(512, count)
-    blocks = count // block
-    width = queries.shape[1] // heads
-    query_blocks = queries.reshape(blocks, block, heads, width)
-    key_heads = keys.reshape(keys.shape[0], heads, width)
-    value_heads = values.reshape(values.shape[0], heads, width)
-    starts = jnp.arange(blocks, dtype=jnp.int32) * block
-
-    def one_block(pair):
-        query_block, start = pair
-        raw = jnp.einsum("qhd,khd->hqk", query_block, key_heads, preferred_element_type=jnp.float32)
-        scores = jnp.where(allowed_fn(start, block)[None], raw * scale, -1e30)
-        top = jnp.max(scores, axis=2, keepdims=True)
-        expo = jnp.exp(scores - top)
-        total = jnp.sum(expo, axis=2, keepdims=True)
-        probs = (expo / total).astype(jnp.bfloat16)
-        mixed = jnp.einsum("hqk,khd->qhd", probs, value_heads, preferred_element_type=jnp.float32)
-        return (mixed.astype(jnp.bfloat16), top + jnp.log(total))
-
-    mixed, logsum = lax.map(one_block, (query_blocks, starts))
-    return (mixed.reshape(count, heads * width), logsum)
-
-
-def attend_backward(queries, keys, values, grad_mixed, logsum, allowed_fn, heads, scale):
-    count = queries.shape[0]
-    block = min(512, count)
-    blocks = count // block
-    width = queries.shape[1] // heads
-    query_blocks = queries.reshape(blocks, block, heads, width)
-    grad_blocks = grad_mixed.reshape(blocks, block, heads, width)
-    key_heads = keys.reshape(keys.shape[0], heads, width)
-    value_heads = values.reshape(values.shape[0], heads, width)
-    starts = jnp.arange(blocks, dtype=jnp.int32) * block
-
-    def one_block(carry, item):
-        grad_keys, grad_values = carry
-        query_block, grad_block, logsum_block, start = item
-        raw = jnp.einsum("qhd,khd->hqk", query_block, key_heads, preferred_element_type=jnp.float32)
-        scores = jnp.where(allowed_fn(start, block)[None], raw * scale, -1e30)
-        probs = jnp.exp(scores - logsum_block)
-        grad_probs = jnp.einsum(
-            "qhd,khd->hqk", grad_block, value_heads, preferred_element_type=jnp.float32
-        )
-        inner = jnp.sum(probs * grad_probs, axis=2, keepdims=True)
-        grad_raw = (probs * (grad_probs - inner) * scale).astype(jnp.bfloat16)
-        grad_query = jnp.einsum(
-            "hqk,khd->qhd", grad_raw, key_heads, preferred_element_type=jnp.float32
-        )
-        grad_keys = grad_keys + jnp.einsum(
-            "hqk,qhd->khd", grad_raw, query_block, preferred_element_type=jnp.float32
-        )
-        grad_values = grad_values + jnp.einsum(
-            "hqk,qhd->khd",
-            probs.astype(jnp.bfloat16),
-            grad_block,
-            preferred_element_type=jnp.float32,
-        )
-        return ((grad_keys, grad_values), grad_query)
-
-    empty = jnp.zeros(key_heads.shape, jnp.float32)
-    (grad_keys, grad_values), grad_query = lax.scan(
-        one_block, (empty, empty), (query_blocks, grad_blocks, logsum, starts)
-    )
-    return (
-        grad_query.reshape(count, heads * width).astype(jnp.bfloat16),
-        grad_keys.reshape(keys.shape[0], heads * width).astype(jnp.bfloat16),
-        grad_values.reshape(keys.shape[0], heads * width).astype(jnp.bfloat16),
-    )
+BF=jnp.bfloat16
+F32=jnp.float32
+
+def head_mask(rows, width, h):
+    lane = lax.broadcasted_iota(jnp.int32, (rows, width), 1)
+    return (lane // HEAD_DIM) == h
+
+def dot(a,b,ca,cb):
+    return lax.dot_general(a,b,(((ca,),(cb,)),((),())),preferred_element_type=F32)
+
+def fwd_kernel(causal, heads, bq, bk, lo_ref, hi_ref, q_ref, k_ref, v_ref, rs_ref, ks_ref, o_ref, lse_ref, acc):
+    count, width = q_ref.shape
+    def one(qb, _):
+        q0 = pl.multiple_of(qb*bq, bq)
+        qv = q_ref[pl.ds(q0,bq),:] * BF(HEAD_DIM**-0.5)
+        rseg = rs_ref[pl.ds(q0,bq),0:1]
+        qm = [jnp.where(head_mask(bq,width,h), qv, BF(0)) for h in range(heads)]
+        acc[...] = jnp.zeros_like(acc)
+        lane = lax.broadcasted_iota(jnp.int32,(bq,128),1)
+        def inner(kb, carry):
+            k0 = pl.multiple_of(kb*bk, bk)
+            kv = k_ref[pl.ds(k0,bk),:]
+            vv = v_ref[pl.ds(k0,bk),:]
+            kseg = ks_ref[0:1,pl.ds(k0,bk)]
+            if causal:
+                kpad = ks_ref[1:2,pl.ds(k0,bk)]
+                ri = lax.broadcasted_iota(jnp.int32,(bq,bk),0)+q0
+                ci = lax.broadcasted_iota(jnp.int32,(bq,bk),1)+k0
+                ok = ((rseg==kpad)&(ci<=ri))|(ci==ri)
+            else:
+                ok = rseg==kseg
+            ms, ls = carry
+            new_m, new_l = [], []
+            parts=None
+            alphas=[]
+            for h in range(heads):
+                s = dot(qm[h],kv,1,1)
+                s = jnp.where(ok,s,-1e30)
+                m = jnp.maximum(ms[h], jnp.max(s,axis=1,keepdims=True))
+                p = jnp.exp(s-m)
+                al = jnp.exp(ms[h]-m)
+                new_m.append(m); new_l.append(ls[h]*al+jnp.sum(p,axis=1,keepdims=True))
+                vm = jnp.where(head_mask(bk,width,h),vv,BF(0))
+                t = dot(p.astype(BF),vm,1,0)
+                parts = t if parts is None else parts+t
+                alphas.append(al)
+            lane2 = lax.broadcasted_iota(jnp.int32,(bq,width),1)//HEAD_DIM
+            sc = alphas[heads-1]
+            for h in range(heads-1):
+                sc = jnp.where(lane2==h, alphas[h], sc)
+            acc[...] = acc[...]*sc + parts
+            return (tuple(new_m),tuple(new_l))
+        init = (tuple(jnp.full((bq,1),-1e30,F32) for _ in range(heads)), tuple(jnp.zeros((bq,1),F32) for _ in range(heads)))
+        ms, ls = lax.fori_loop(lo_ref[qb], hi_ref[qb], inner, init)
+        lane2 = lax.broadcasted_iota(jnp.int32,(bq,width),1)//HEAD_DIM
+        inv = [1.0/l for l in ls]
+        sc = inv[heads-1]
+        for h in range(heads-1):
+            sc = jnp.where(lane2==h, inv[h], sc)
+        o_ref[pl.ds(q0,bq),:] = (acc[...]*sc).astype(BF)
+        st = jnp.zeros((bq,128),F32)
+        for h in range(heads):
+            st = jnp.where(lane==h, ms[h]+jnp.log(ls[h]), st)
+        stt = jnp.transpose(st)
+        lse_ref[:,pl.ds(q0,bq)] = stt[0:8,:]
+        return 0
+    lax.fori_loop(0,count//bq,one,0)
+
+def attend_fwd(q,k,v,rseg,kseg,lo,hi,causal,bq=256,bk=256):
+    count,width=q.shape
+    heads=width//HEAD_DIM
+    vm=pl.BlockSpec(memory_space=pltpu.VMEM); sm=pl.BlockSpec(memory_space=pltpu.SMEM)
+    return pl.pallas_call(functools.partial(fwd_kernel,causal,heads,bq,bk),
+        out_shape=(jax.ShapeDtypeStruct((count,width),BF),jax.ShapeDtypeStruct((8,count),F32)),
+        in_specs=[sm,sm,vm,vm,vm,vm,vm],out_specs=(vm,vm),
+        scratch_shapes=[pltpu.VMEM((bq,width),F32)],
+        compiler_params=pltpu.CompilerParams(vmem_limit_bytes=40<<20),
+        name="attend_fwd",
+    )(lo,hi,q,k,v,rseg,kseg)
+
+def bwd_kernel(causal, heads, bq, bk, lo_ref, hi_ref, q_ref, k_ref, v_ref, o_ref, do_ref, lse_ref, rs_ref, ks_ref,
+               dq_ref, dk_ref, dv_ref, dka, dva, qm, dom, dqa):
+    count,width=q_ref.shape
+    dka[...]=jnp.zeros_like(dka); dva[...]=jnp.zeros_like(dva)
+    def one(qb,_):
+        q0=pl.multiple_of(qb*bq,bq)
+        qv=q_ref[pl.ds(q0,bq),:]*BF(HEAD_DIM**-0.5)
+        dov=do_ref[pl.ds(q0,bq),:]
+        prod=dov.astype(F32)*o_ref[pl.ds(q0,bq),:].astype(F32)
+        row=lax.broadcasted_iota(jnp.int32,(8,width),0); col=lax.broadcasted_iota(jnp.int32,(8,width),1)//HEAD_DIM
+        sel=(row==col).astype(F32)
+        delta=lax.dot_general(sel,prod,(((1,),(1,)),((),())),precision=lax.Precision.HIGHEST,preferred_element_type=F32)
+        for h in range(heads):
+            hm=head_mask(bq,width,h)
+            qm[pl.ds(h*bq,bq),:]=jnp.where(hm,qv,BF(0))
+            dom[pl.ds(h*bq,bq),:]=jnp.where(hm,dov,BF(0))
+        dqa[...]=jnp.zeros_like(dqa)
+        rseg=rs_ref[0:1,pl.ds(q0,bq)]
+        lse=lse_ref[:,pl.ds(q0,bq)]
+        def inner(kb,_):
+            k0=pl.multiple_of(kb*bk,bk)
+            kv=k_ref[pl.ds(k0,bk),:]; vv=v_ref[pl.ds(k0,bk),:]
+            if causal:
+                kpad=ks_ref[pl.ds(k0,bk),1:2]
+                ri=lax.broadcasted_iota(jnp.int32,(bk,bq),1)+q0
+                ci=lax.broadcasted_iota(jnp.int32,(bk,bq),0)+k0
+                ok=((rseg==kpad)&(ci<=ri))|(ci==ri)
+            else:
+                ok=rseg==ks_ref[pl.ds(k0,bk),0:1]
+            ps=[];dss=[]
+            dq=None
+            for h in range(heads):
+                st=dot(kv,qm[pl.ds(h*bq,bq),:],1,1)
+                p=jnp.where(ok,jnp.exp(st-lse[h:h+1,:]),0.0)
+                dp=dot(vv,dom[pl.ds(h*bq,bq),:],1,1)
+                ds=(p*(dp-delta[h:h+1,:])).astype(BF)
+                ps.append(p.astype(BF)); dss.append(ds)
+                km=jnp.where(head_mask(bk,width,h),kv,BF(0))
+                t=dot(ds,km,0,0)
+                dq=t if dq is None else dq+t
+            dqa[...]+=dq
+            pcat=jnp.concatenate(ps,axis=1); dcat=jnp.concatenate(dss,axis=1)
+            dva[pl.ds(k0,bk),:]+=dot(pcat,dom[...],1,0)
+            dka[pl.ds(k0,bk),:]+=dot(dcat,qm[...],1,0)
+            return 0
+        lax.fori_loop(lo_ref[qb],hi_ref[qb],inner,0)
+        dq_ref[pl.ds(q0,bq),:]=(dqa[...]*(HEAD_DIM**-0.5)).astype(BF)
+        return 0
+    lax.fori_loop(0,count//bq,one,0)
+    dk_ref[...]=dka[...].astype(BF)
+    dv_ref[...]=dva[...].astype(BF)
+
+def attend_bwd(q,k,v,o,do,lse,rseg,kseg,lo,hi,causal,bq=256,bk=256):
+    count,width=q.shape; keys=k.shape[0]
+    heads=width//HEAD_DIM
+    vm=pl.BlockSpec(memory_space=pltpu.VMEM); sm=pl.BlockSpec(memory_space=pltpu.SMEM)
+    return pl.pallas_call(functools.partial(bwd_kernel,causal,heads,bq,bk),
+        out_shape=(jax.ShapeDtypeStruct((count,width),BF),jax.ShapeDtypeStruct((keys,width),BF),jax.ShapeDtypeStruct((keys,width),BF)),
+        in_specs=[sm,sm]+[vm]*8,out_specs=(vm,vm,vm),
+        scratch_shapes=[pltpu.VMEM((keys,width),F32),pltpu.VMEM((keys,width),F32),pltpu.VMEM((heads*bq,width),BF),pltpu.VMEM((heads*bq,width),BF),pltpu.VMEM((bq,width),F32)],
+        compiler_params=pltpu.CompilerParams(vmem_limit_bytes=40<<20),
+        name="attend_bwd",
+    )(lo,hi,q,k,v,o,do,lse,rseg,kseg)
+
+def ranges(tok_lengths, enc_lengths, pad, count, frames, bq, bk):
+    tend=jnp.cumsum(tok_lengths,dtype=jnp.int32); eend=jnp.cumsum(enc_lengths,dtype=jnp.int32)
+    places=jnp.arange(count,dtype=jnp.int32)
+    tseg=jnp.sum((places[:,None]>=tend[None,:]).astype(jnp.int32),axis=1)
+    eseg=jnp.sum((jnp.arange(frames,dtype=jnp.int32)[:,None]>=eend[None,:]).astype(jnp.int32),axis=1)
+    starts=jnp.arange(count//bq,dtype=jnp.int32)*bq
+    first=tseg[::bq]; last=tseg[bq-1::bq]
+    onehot=lambda s:(s[:,None]==jnp.arange(tend.shape[0])[None,:]).astype(jnp.int32)
+    pick=lambda arr,s: jnp.sum(onehot(s)*arr[None,:],axis=1)
+    tstart=tend-tok_lengths; estart=eend-enc_lengths
+    slo=pick(tstart,first)//bk; shi=(starts+bq+bk-1)//bk
+    clo=pick(estart,first)//bk; chi=(pick(eend,last)+bk-1)//bk
+    kpad=jnp.where(pad==1,tseg,-1)
+    return tseg,eseg,kpad,slo,shi,clo,chi
 
 
 def on_device(
@@ -196,23 +288,12 @@
     frames = encoder_states.shape[0]
     heads = causal_query.shape[1] // HEAD_DIM
     scale = HEAD_DIM ** (-0.5)
-    token_seg = segment_ids(tok_lengths[0], length)
-    frame_seg = segment_ids(enc_lengths[0], frames)
-    places = jnp.arange(length, dtype=jnp.int32)
-
-    def causal_allowed(start, block):
-        rows_here = start + jnp.arange(block, dtype=jnp.int32)
-        seg_here = lax.dynamic_slice_in_dim(token_seg, start, block, 0)
-        return (
-            (seg_here[:, None] == token_seg[None, :])
-            & (places[None, :] <= rows_here[:, None])
-            & ((pad_mask[None, :] == 1) | (places[None, :] == rows_here[:, None]))
-        )
-
-    def cross_allowed(start, block):
-        seg_here = lax.dynamic_slice_in_dim(token_seg, start, block, 0)
-        return seg_here[:, None] == frame_seg[None, :]
-
+    token_seg, frame_seg, key_seg, self_lo, self_hi, cross_lo, cross_hi = ranges(
+        tok_lengths[0], enc_lengths[0], pad_mask, length, frames, 256, 512
+    )
+    self_keys = jnp.stack([token_seg, key_seg] + [token_seg] * 6)
+    cross_keys = jnp.stack([frame_seg] * 8)
+    seg_col, seg_row = token_seg[:, None], token_seg[None, :]
     residual = tokens.astype(jnp.float32)
     first_out, first_unit, first_inv = normalize(residual, first_gain, first_shift)
     first_all = spread_normed(first_out.astype(jnp.bfloat16))
@@ -223,7 +304,9 @@
     valued = jnp.dot(first_all, causal_value, preferred_element_type=jnp.float32).astype(
         jnp.bfloat16
     )
-    mixed, self_logsum = attend_forward(query, keyed, valued, causal_allowed, heads, scale)
+    mixed, self_logsum = attend_fwd(
+        query, keyed, valued, seg_col, self_keys, self_lo, self_hi, True, 256, 512
+    )
     after_self = residual + sum_branch(mixed, causal_out, share)
     second_out, second_unit, second_inv = normalize(after_self, second_gain, second_shift)
     second_all = spread_normed(second_out.astype(jnp.bfloat16))
@@ -236,7 +319,9 @@
     cvalued = jnp.dot(encoder_states, cross_value, preferred_element_type=jnp.float32).astype(
         jnp.bfloat16
     )
-    cmixed, cross_logsum = attend_forward(cquery, ckeyed, cvalued, cross_allowed, heads, scale)
+    cmixed, cross_logsum = attend_fwd(
+        cquery, ckeyed, cvalued, seg_col, cross_keys, cross_lo, cross_hi, False, 256, 512
+    )
     after_cross = after_self + sum_branch(cmixed, cross_out, share)
     third_out, third_unit, third_inv = normalize(after_cross, third_gain, third_shift)
     third_all = spread_normed(third_out.astype(jnp.bfloat16))
@@ -257,8 +342,9 @@
     grad_top = spread_grads(grad_res.astype(jnp.bfloat16))
     cross_out_grad = along_rows(cmixed, grad_top)
     grad_cmixed = against(grad_top, cross_out).astype(jnp.bfloat16)
-    grad_cquery, grad_ckey, grad_cvalue = attend_backward(
-        cquery, ckeyed, cvalued, grad_cmixed, cross_logsum, cross_allowed, heads, scale
+    grad_cquery, grad_ckey, grad_cvalue = attend_bwd(
+        cquery, ckeyed, cvalued, cmixed, grad_cmixed, cross_logsum, seg_row, cross_keys.T,
+        cross_lo, cross_hi, False, 256, 512,
     )
     cross_query_grad = along_rows(second_all, grad_cquery)
     cross_key_grad = along_rows(encoder_states, grad_ckey)
@@ -277,8 +363,9 @@
     grad_top = spread_grads(grad_res.astype(jnp.bfloat16))
     causal_out_grad = along_rows(mixed, grad_top)
     grad_mixed = against(grad_top, causal_out).astype(jnp.bfloat16)
-    grad_query, grad_key, grad_value = attend_backward(
-        query, keyed, valued, grad_mixed, self_logsum, causal_allowed, heads, scale
+    grad_query, grad_key, grad_value = attend_bwd(
+        query, keyed, valued, mixed, grad_mixed, self_logsum, seg_row, self_keys.T,
+        self_lo, self_hi, True, 256, 512,
     )
     causal_query_grad = along_rows(first_all, grad_query)
     causal_key_grad = along_rows(first_all, grad_key)

time: 1290 us -> 1010 us (0.78)
  matrix products: 357 us -> 82.8 us
  Pallas kernels: 0 us -> 50.9 us
  waiting for transfers between devices: 728 us -> 759 us
  local copies, waits for them, and re-layouts: 54.8 us -> 25.6 us
  other arithmetic: 52.1 us -> 29 us
  loops' own time: 16.7 us -> 0 us
    dot_general x28 -> x0, matrix products: 263 us -> none  [the longest x4 89.7 us: one_block(): jnp.einsum('hqk,qhd->khd', grad_raw, query_block, preferred_element_type=...]
    pallas_call x0 -> x4, Pallas kernels: none -> 50.9 us  [the longest x2 27.9 us: attend_bwd(): pl.pallas_call(functools.partial(bwd_kernel, causal, heads, bq, bk), out_...]
    reduce_scatter x3, waiting for transfers between devices: 119 us -> 139 us  [sum_branch(): lax.psum_scatter(term(jnp.int32(0), lax.axis_size('tensor') * rows).astyp...]
    another operation x4 -> x0, loops' own time: 16.7 us -> none  [the longest x2 8.74 us: attend_backward(): lax.scan(one_block, (empty, empty), (query_blocks, grad_blocks, logsum, s...]
    reduce_scatter x3, waiting for transfers between devices: 85.9 us -> 102 us  [sum_inputs(): lax.psum_scatter(term(jnp.int32(0), lax.axis_size('tensor') * rows).astyp...]
    reduce_sum x6 -> x4, other arithmetic: 13.5 us -> 0.54 us  [the longest x2 0.37 us: ranges(): pick = lambda arr, s: jnp.sum(onehot(s) * arr[None, :], axis=1)]
    unnamed x141 -> x152, local copies, waits for them, and re-layouts: 29.1 us -> 24.7 us
  transfers between devices with their start and end apart: 14 -> 14, of which waited for: 14 -> 14; matrix products, arithmetic and copies ran while one was open for 5% -> 6% of each run, Pallas kernels for 0% -> 0%
where the time goes in v1:
time: 1010 us
  waiting for transfers between devices  759 us (75%)
  matrix products  82.8 us (8%)
  Pallas kernels  50.9 us (5%)
  blocking collectives  41.4 us (4%)
  other arithmetic  29 us (3%)
  local copies, waits for them, and re-layouts  25.6 us (3%)
  between operations  14.9 us (1%)
    psum x1, waiting for transfers between devices, on_device(): lax.psum((causal_query_grad, causal_key_grad, causal_value_grad, causal_o...  186 us
    reduce_scatter x3, waiting for transfers between devices, sum_branch(): lax.psum_scatter(term(jnp.int32(0), lax.axis_size('tensor') * rows).astyp...  139 us
    all_gather x3, waiting for transfers between devices, spread_grads(): return lax.all_gather(rows, 'tensor', axis=0, tiled=True)  131 us
    all_gather x3, waiting for transfers between devices, spread_normed(): return lax.all_gather(rows, 'tensor', axis=0, tiled=True)  127 us
    reduce_scatter x3, waiting for transfers between devices, sum_inputs(): lax.psum_scatter(term(jnp.int32(0), lax.axis_size('tensor') * rows).astyp...  102 us
    reduce_scatter x1, waiting for transfers between devices, on_device(): lax.psum_scatter((against(grad_ckey, cross_key) + against(grad_cvalue, cr...  74.8 us
    psum x1, blocking collectives, on_device(): lax.psum((first_gain_grad, first_shift_grad, second_gain_grad, second_shi...  41.4 us
    pallas_call x2, Pallas kernels, attend_bwd(): pl.pallas_call(functools.partial(bwd_kernel, causal, heads, bq, bk), out_...  27.9 us
  transfers between devices with their start and end apart: 14, of which 14 were waited for; matrix products, arithmetic and copies ran while one was open for 6% of the time, Pallas kernels for 0%

profile of v1, /device:TPU:1, one launch (start us, length us, event | category | flops | bytes accessed | tf_op | source)
XLA Modules:
  0.0 1006.0 jit_solution(15753716593753721894)
XLA Ops:
  7.3 1.3 convert_reduce_fusion.3
  8.6 1.3 fusion.26
  9.9 2.2 fusion.21
  15.9 44.4 %all-gather.7.cloned.1.call-done = bf16[1024,1024]{1,0:T(8,128)(2,1)} async-done(((bf16[256,1024]{1,0:T(8,128)(2,1)}), bf16[1024,1024]{1,0:T(8,128)(2,1)}) %all-gather.7.cloned.1.call-update) | async-done | bytes 2097168 | tf_op jit(solution)/shard_map/all_gather | solution.py:66
  60.3 2.5 convolution_convert_fusion.12.q_ref
  64.9 9.3 attend_fwd.2
  74.2 2.0 convolution_convert_fusion.6
  76.3 45.6 %reduce-scatter.8.cloned.1.call-done = bf16[256,1024]{1,0:T(8,128)(2,1)} async-done(((bf16[1024,1024]{1,0:T(8,128)(2,1)}), bf16[256,1024]{1,0:T(8,128)(2,1)}) %reduce-scatter.8.cloned.1.call-update) | async-done | bytes 524304 | tf_op jit(solution)/shard_map/reduce_scatter | solution.py:78
  123.2 1.3 multiply_reduce_fusion.1
  124.6 2.1 add_convert_fusion.4
  127.4 4.7 convolution_convert_fusion.1.k_ref
  132.1 2.3 convolution_convert_fusion.v_ref
  134.4 37.9 %all-gather.9.cloned.1.call-done = bf16[1024,1024]{1,0:T(8,128)(2,1)} async-done(((bf16[256,1024]{1,0:T(8,128)(2,1)}), bf16[1024,1024]{1,0:T(8,128)(2,1)}) %all-gather.9.cloned.1.call-update) | async-done | bytes 2097168 | tf_op jit(solution)/shard_map/all_gather | solution.py:66
  172.3 2.5 convolution_convert_fusion.9.q_ref
  174.9 13.7 %attend_fwd.3 = (bf16[1024,256]{1,0:T(8,128)(2,1)S(1)}, f32[8,1024]{1,0:T(8,128)S(1)}) custom-call(s32[4]{0:T(128)S(1)} %and_select_fusion.1.lo_ref, s32[4]{0:T(128)S(1)} %and_select_fusion.hi_ref, bf16[1024,256]{1,0:T(8,128)(2,1)S(1)} %convolution_convert_fusion.9.q_ref, bf16[2048,256]{1,0:T(8,128)(2,1)S(1)} %copy-done.4, bf16[2048,256]{1,0:T(8,128)(2,1)S(1)} %copy-done.6, ...), custom_call_target="tpu_custom_call" | custom-call | tf_op jit(solution)/shard_map/attend_fwd/pallas_call | solution.py:174
  188.7 2.0 convolution_convert_fusion.5
  190.8 49.3 %reduce-scatter.10.cloned.1.call-done = bf16[256,1024]{1,0:T(8,128)(2,1)} async-done(((bf16[1024,1024]{1,0:T(8,128)(2,1)}), bf16[256,1024]{1,0:T(8,128)(2,1)}) %reduce-scatter.10.cloned.1.call-update) | async-done | bytes 524304 | tf_op jit(solution)/shard_map/reduce_scatter | solution.py:78
  240.1 1.6 fusion.47
  244.9 44.4 %all-gather.11.cloned.1.call-done = bf16[1024,1024]{1,0:T(8,128)(2,1)} async-done(((bf16[256,1024]{1,0:T(8,128)(2,1)}), bf16[1024,1024]{1,0:T(8,128)(2,1)}) %all-gather.11.cloned.1.call-update) | async-done | bytes 2097168 | tf_op jit(solution)/shard_map/all_gather | solution.py:66
  289.4 5.9 fusion.48
  295.3 40.2 %all-gather.13.cloned.1.call-done = bf16[1024,1024]{1,0:T(8,128)(2,1)} async-done(((bf16[256,1024]{1,0:T(8,128)(2,1)}), bf16[1024,1024]{1,0:T(8,128)(2,1)}) %all-gather.13.cloned.1.call-update) | async-done | bytes 2097168 | tf_op jit(solution)/shard_map/all_gather | solution.py:70
  335.5 7.7 fusion.6
  343.2 1.4 copy-done.70
  344.6 3.7 convolution_convert_fusion.3
  348.4 7.0 convolution_convert_fusion.4
  355.4 35.5 %reduce-scatter.14.cloned.1.call-done = bf16[256,1024]{1,0:T(8,128)(2,1)} async-done(((bf16[1024,1024]{1,0:T(8,128)(2,1)}), bf16[256,1024]{1,0:T(8,128)(2,1)}) %reduce-scatter.14.cloned.1.call-update) | async-done | bytes 524304 | tf_op jit(solution)/shard_map/reduce_scatter | solution.py:94
  390.9 1.6 fusion.36
  392.5 44.0 %reduce-scatter.12.cloned.1.call-done = bf16[256,1024]{1,0:T(8,128)(2,1)} async-done(((bf16[1024,1024]{1,0:T(8,128)(2,1)}), bf16[256,1024]{1,0:T(8,128)(2,1)}) %reduce-scatter.12.cloned.1.call-update) | async-done | bytes 524304 | tf_op jit(solution)/shard_map/reduce_scatter | solution.py:78
  436.5 3.0 fusion.45
  439.8 45.4 %all-gather.15.cloned.1.call-done = bf16[1024,1024]{1,0:T(8,128)(2,1)} async-done(((bf16[256,1024]{1,0:T(8,128)(2,1)}), bf16[1024,1024]{1,0:T(8,128)(2,1)}) %all-gather.15.cloned.1.call-update) | async-done | bytes 2097168 | tf_op jit(solution)/shard_map/all_gather | solution.py:70
  485.2 2.5 convolution_convert_fusion.8.do_ref
  488.0 17.2 %attend_bwd.2 = (bf16[1024,256]{1,0:T(8,128)(2,1)S(1)}, bf16[2048,256]{1,0:T(8,128)(2,1)S(1)}, bf16[2048,256]{1,0:T(8,128)(2,1)S(1)}) custom-call(s32[4]{0:T(128)S(1)} %and_select_fusion.1.lo_ref, s32[4]{0:T(128)S(1)} %and_select_fusion.hi_ref, bf16[1024,256]{1,0:T(8,128)(2,1)S(1)} %copy-done.9, bf16[2048,256]{1,0:T(8,128)(2,1)S(1)} %copy-done.5, ...), custom_call_target="tpu_custom_call" | custom-call | tf_op jit(solution)/shard_map/attend_bwd/pallas_call | solution.py:238
  508.0 2.1 convolution_convert_fusion.2
  510.1 51.7 %reduce-scatter.16.cloned.1.call-done = bf16[256,1024]{1,0:T(8,128)(2,1)} async-done(((bf16[1024,1024]{1,0:T(8,128)(2,1)}), bf16[256,1024]{1,0:T(8,128)(2,1)}) %reduce-scatter.16.cloned.1.call-update) | async-done | bytes 524304 | tf_op jit(solution)/shard_map/reduce_scatter | solution.py:94
  561.8 1.6 fusion.37
  563.5 2.7 fusion.43
  566.5 45.3 %all-gather.17.cloned.1.call-done = bf16[1024,1024]{1,0:T(8,128)(2,1)} async-done(((bf16[256,1024]{1,0:T(8,128)(2,1)}), bf16[1024,1024]{1,0:T(8,128)(2,1)}) %all-gather.17.cloned.1.call-update) | async-done | bytes 2097168 | tf_op jit(solution)/shard_map/all_gather | solution.py:70
  611.8 2.5 convolution_convert_fusion.7.do_ref
  614.3 10.7 %attend_bwd.3 = (bf16[1024,256]{1,0:T(8,128)(2,1)S(1)}, bf16[1024,256]{1,0:T(8,128)(2,1)S(1)}, bf16[1024,256]{1,0:T(8,128)(2,1)S(1)}) custom-call(s32[4]{0:T(128)S(1)} %and_select_fusion.3.lo_ref, s32[4]{0:T(128)S(1)} %and_select_fusion.2.hi_ref, bf16[1024,256]{1,0:T(8,128)(2,1)S(1)} %copy-done.11, bf16[1024,256]{1,0:T(8,128)(2,1)S(1)} %copy-done.13, ...), custom_call_target="tpu_custom_call" | custom-call | tf_op jit(solution)/shard_map/attend_bwd/pallas_call | solution.py:238
  626.6 2.1 add_convert_fusion.1
  629.1 6.1 fusion.58
  635.2 4.8 fusion.42
  640.0 1.7 fusion.56
  641.7 1.7 fusion.57
  643.6 2.3 convolution_bitcast_fusion.1
  645.9 2.3 convolution_bitcast_fusion
  648.1 1.7 fusion.52
  649.9 1.7 fusion.53
  651.6 1.7 fusion.54
  653.3 1.7 fusion.55
  656.1 1.3 fusion.51
  657.4 3.4 add_convert_fusion
  660.8 14.4 %reduce-scatter.18.cloned.1.call-done = bf16[256,1024]{1,0:T(8,128)(2,1)} async-done(((bf16[1024,1024]{1,0:T(8,128)(2,1)}), bf16[256,1024]{1,0:T(8,128)(2,1)}) %reduce-scatter.18.cloned.1.call-update) | async-done | bytes 524304 | tf_op jit(solution)/shard_map/reduce_scatter | solution.py:94
  675.2 1.6 fusion.38
  676.8 41.4 %all-reduce = (f32[1024]{0:T(1024)}, f32[1024]{0:T(1024)}, f32[1024]{0:T(1024)}, f32[1024]{0:T(1024)}, f32[1024]{0:T(1024)}, /*index=5*/f32[1024]{0:T(1024)}) all-reduce(f32[1024]{0:T(1024)S(1)} %get-tuple-element.119, f32[1024]{0:T(1024)S(1)} %get-tuple-element.126, ...), channel_id=1, replica_groups=mesh['dp'=8,'tensor'=4] {'dp','tensor'}, use_global_device_ids=true, to_apply=%region_27.28 | all-reduce | flops 6144 | bytes 49152 | tf_op jit(solution)/shard_map/psum | solution.py:413
  718.2 2.3 fusion.25
  720.5 185.7 %all-reduce.4.cloned.1.call-done = (f32[1024,256]{1,0:T(8,128)}, f32[1024,256]{1,0:T(8,128)}, f32[1024,256]{1,0:T(8,128)}, f32[256,1024]{1,0:T(8,128)}, f32[1024...) async-done(((f32[1024,256]{1,0:T(8,128)}, f32[1024,256]{1,0:T(8,128)}, ...) | async-done | bytes 16777232 | tf_op jit(solution)/shard_map/psum | solution.py:391
  906.2 2.7 copy.67
  908.9 2.6 copy.68
  911.5 74.8 %reduce-scatter.20.cloned.1.call-done = bf16[512,1024]{1,0:T(8,128)(2,1)} async-done(((bf16[2048,1024]{1,0:T(8,128)(2,1)}), bf16[512,1024]{1,0:T(8,128)(2,1)}) %reduce-scatter.20.cloned.1.call-update) | async-done | bytes 1048592 | tf_op jit(solution)/shard_map/reduce_scatter | solution.py:352
  986.3 2.4 copy.79
  993.5 2.1 copy.85
  995.7 1.6 copy-done.34
  997.2 2.0 copy.86
  (211 shorter events, 22.8 us)
Async XLA Ops:
  7.2 282.2 %copy-start = (bf16[1024,1024]{1,0:T(8,128)(2,1)S(1)}, bf16[1024,1024]{1,0:T(8,128)(2,1)}, u32[]{:S(2)}) copy-start(bf16[1024,1024]{1,0:T(8,128)(2,1)} %param.41) | copy-start | bytes 6291460
  7.2 53.1 %all-gather.7.cloned.1.call-start = ((), (), s32[]{:S(2)}) async-start(), calls=%async_computation.7 | async-start | bytes 2621440 | tf_op jit(solution)/shard_map/all_gather | solution.py:66
  9.9 52.9 %copy-start.49 = (bf16[1024,256]{1,0:T(8,128)(2,1)S(1)}, bf16[1024,256]{1,0:T(8,128)(2,1)}, u32[]{:S(2)}) copy-start(bf16[1024,256]{1,0:T(8,128)(2,1)} %param.30) | copy-start | bytes 1572868
  12.1 109.8 %reduce-scatter.8.cloned.1.call-start = ((), (), s32[]{:S(2)}) async-start(), calls=%async_computation.8 | async-start | bytes 2621440 | tf_op jit(solution)/shard_map/reduce_scatter | solution.py:78
  14.3 50.6 %copy-start.2 = (s32[1024,1]{1,0:T(8,128)}, s32[1024,1]{1,0:T(8,128)S(1)}, u32[]{:S(2)}) copy-start(s32[1024,1]{1,0:T(8,128)S(1)} %copy.64.rs_ref) | copy-start | bytes 12292
  64.1 10.0 copy-start.12
  64.1 10.1 %copy-start.56 = (bf16[256,1024]{1,0:T(8,128)(2,1)S(1)}, bf16[256,1024]{1,0:T(8,128)(2,1)}, u32[]{:S(2)}) copy-start(bf16[256,1024]{1,0:T(8,128)(2,1)} %param.32) | copy-start | bytes 1572868
  64.9 9.3 copy-start.14
  74.2 47.8 %copy-start.28 = (bf16[256,1024]{1,0:T(8,128)(2,1)S(1)}, bf16[256,1024]{1,0:T(8,128)(2,1)}, u32[]{:S(2)}) copy-start(bf16[256,1024]{1,0:T(8,128)(2,1)} %param.22) | copy-start | bytes 1572868
  74.2 50.4 %copy-start.59 = (f32[1024]{0:T(1024)S(1)}, f32[1024]{0:T(1024)}, u32[]{:S(2)}) copy-start(f32[1024]{0:T(1024)} %param.33) | copy-start | bytes 12292
  74.2 50.4 %copy-start.60 = (f32[1024]{0:T(1024)S(1)}, f32[1024]{0:T(1024)}, u32[]{:S(2)}) copy-start(f32[1024]{0:T(1024)} %param.34) | copy-start | bytes 12292
  76.3 96.0 %all-gather.9.cloned.1.call-start = ((), (), s32[]{:S(2)}) async-start(), calls=%async_computation.9 | async-start | bytes 2621440 | tf_op jit(solution)/shard_map/all_gather | solution.py:66
  126.7 5.5 copy-start.46
  126.7 113.4 %reduce-scatter.10.cloned.1.call-start = ((), (), s32[]{:S(2)}) async-start(), calls=%async_computation.10 | async-start | bytes 2621440 | tf_op jit(solution)/shard_map/reduce_scatter | solution.py:78
  127.1 5.0 copy-start.62
  172.3 2.6 copy-start.4
  172.3 2.6 copy-start.6
  172.3 16.3 %copy-start.54 = (bf16[256,1024]{1,0:T(8,128)(2,1)S(1)}, bf16[256,1024]{1,0:T(8,128)(2,1)}, u32[]{:S(2)}) copy-start(bf16[256,1024]{1,0:T(8,128)(2,1)} %param.38) | copy-start | bytes 1572868
  174.8 13.8 %copy-start.8 = (bf16[1024,256]{1,0:T(8,128)(2,1)}, bf16[1024,256]{1,0:T(8,128)(2,1)S(1)}, u32[]{:S(2)}) copy-start(bf16[1024,256]{1,0:T(8,128)(2,1)S(1)} %convolution_convert_fusion.9.q_ref) | copy-start | bytes 1572868
  188.6 54.0 %copy-start.57 = (f32[1024]{0:T(1024)S(1)}, f32[1024]{0:T(1024)}, u32[]{:S(2)}) copy-start(f32[1024]{0:T(1024)} %param.39) | copy-start | bytes 12292
  188.6 54.0 %copy-start.61 = (f32[1024]{0:T(1024)S(1)}, f32[1024]{0:T(1024)}, u32[]{:S(2)}) copy-start(f32[1024]{0:T(1024)} %param.40) | copy-start | bytes 12292
  190.7 98.6 %all-gather.11.cloned.1.call-start = ((), (), s32[]{:S(2)}) async-start(), calls=%async_computation.11 | async-start | bytes 2621440 | tf_op jit(solution)/shard_map/all_gather | solution.py:66
  243.8 91.7 %all-gather.13.cloned.1.call-start = ((), (), s32[]{:S(2)}) async-start(), calls=%async_computation.13 | async-start | bytes 2621440 | tf_op jit(solution)/shard_map/all_gather | solution.py:70
  244.3 146.5 %reduce-scatter.14.cloned.1.call-start = ((), (), s32[]{:S(2)}) async-start(), calls=%async_computation.14 | async-start | bytes 2621440 | tf_op jit(solution)/shard_map/reduce_scatter | solution.py:94
  348.3 42.6 %copy-start.32 = (f32[256,1024]{1,0:T(8,128)S(1)}, f32[256,1024]{1,0:T(8,128)}, u32[]{:S(2)}) copy-start(f32[256,1024]{1,0:T(8,128)} %copy-done.31) | copy-start | bytes 3145732
  348.3 88.2 %copy-start.40 = (bf16[256,1024]{1,0:T(8,128)(2,1)S(1)}, bf16[256,1024]{1,0:T(8,128)(2,1)}, u32[]{:S(2)}) copy-start(bf16[256,1024]{1,0:T(8,128)(2,1)} %param.43) | copy-start | bytes 1572868
  348.3 88.2 %reduce-scatter.12.cloned.1.call-start = ((), (), s32[]{:S(2)}) async-start(), calls=%async_computation.12 | async-start | bytes 2621440 | tf_op jit(solution)/shard_map/reduce_scatter | solution.py:78
  355.3 129.8 %all-gather.15.cloned.1.call-start = ((), (), s32[]{:S(2)}) async-start(), calls=%async_computation.15 | async-start | bytes 2621440 | tf_op jit(solution)/shard_map/all_gather | solution.py:70
  439.5 48.4 %copy-start.5 = (bf16[2048,256]{1,0:T(8,128)(2,1)S(1)}, bf16[2048,256]{1,0:T(8,128)(2,1)}, u32[]{:S(2)}) copy-start(bf16[2048,256]{1,0:T(8,128)(2,1)} %convolution_convert_fusion.1.k_ref) | copy-start | bytes 3145732
  439.5 48.5 %copy-start.7 = (bf16[2048,256]{1,0:T(8,128)(2,1)S(1)}, bf16[2048,256]{1,0:T(8,128)(2,1)}, u32[]{:S(2)}) copy-start(bf16[2048,256]{1,0:T(8,128)(2,1)} %convolution_convert_fusion.v_ref) | copy-start | bytes 3145732
  439.6 122.3 %reduce-scatter.16.cloned.1.call-start = ((), (), s32[]{:S(2)}) async-start(), calls=%async_computation.16 | async-start | bytes 2621440 | tf_op jit(solution)/shard_map/reduce_scatter | solution.py:94
  485.2 2.8 copy-start.9
  487.6 20.3 %copy-start.55 = (bf16[1024,256]{1,0:T(8,128)(2,1)S(1)}, bf16[1024,256]{1,0:T(8,128)(2,1)}, u32[]{:S(2)}) copy-start(bf16[1024,256]{1,0:T(8,128)(2,1)} %param.35) | copy-start | bytes 1572868
  507.2 54.7 %copy-start.29 = (bf16[256,1024]{1,0:T(8,128)(2,1)S(1)}, bf16[256,1024]{1,0:T(8,128)(2,1)}, u32[]{:S(2)}) copy-start(bf16[256,1024]{1,0:T(8,128)(2,1)} %param.22) | copy-start | bytes 1572868
  507.2 54.7 %copy-start.33 = (bf16[256,1024]{1,0:T(8,128)(2,1)S(1)}, bf16[256,1024]{1,0:T(8,128)(2,1)}, u32[]{:S(2)}) copy-start(bf16[256,1024]{1,0:T(8,128)(2,1)} %reduce-scatter.8.cloned.1.call-done) | copy-start | bytes 1572868
  507.2 56.3 %copy-start.37 = (f32[256,1024]{1,0:T(8,128)S(1)}, f32[256,1024]{1,0:T(8,128)}, u32[]{:S(2)}) copy-start(f32[256,1024]{1,0:T(8,128)} %get-tuple-element.148) | copy-start | bytes 3145732
  510.1 101.7 %all-gather.17.cloned.1.call-start = ((), (), s32[]{:S(2)}) async-start(), calls=%async_computation.17 | async-start | bytes 2621440 | tf_op jit(solution)/shard_map/all_gather | solution.py:70
  566.2 48.1 %copy-start.11 = (bf16[1024,256]{1,0:T(8,128)(2,1)S(1)}, bf16[1024,256]{1,0:T(8,128)(2,1)}, u32[]{:S(2)}) copy-start(bf16[1024,256]{1,0:T(8,128)(2,1)} %copy-done.10) | copy-start | bytes 1572868
  566.2 48.1 %copy-start.13 = (bf16[1024,256]{1,0:T(8,128)(2,1)S(1)}, bf16[1024,256]{1,0:T(8,128)(2,1)}, u32[]{:S(2)}) copy-start(bf16[1024,256]{1,0:T(8,128)(2,1)} %copy-done.12) | copy-start | bytes 1572868
  566.2 48.1 %copy-start.15 = (bf16[1024,256]{1,0:T(8,128)(2,1)S(1)}, bf16[1024,256]{1,0:T(8,128)(2,1)}, u32[]{:S(2)}) copy-start(bf16[1024,256]{1,0:T(8,128)(2,1)} %copy-done.14) | copy-start | bytes 1572868
  566.2 109.0 %reduce-scatter.18.cloned.1.call-start = ((), (), s32[]{:S(2)}) async-start(), calls=%async_computation.18 | async-start | bytes 2621440 | tf_op jit(solution)/shard_map/reduce_scatter | solution.py:94
  611.8 13.3 %copy-start.48 = (bf16[1024,256]{1,0:T(8,128)(2,1)S(1)}, bf16[1024,256]{1,0:T(8,128)(2,1)}, u32[]{:S(2)}) copy-start(bf16[1024,256]{1,0:T(8,128)(2,1)} %param.29) | copy-start | bytes 1572868
  614.3 11.5 %copy-start.50 = (bf16[1024,256]{1,0:T(8,128)(2,1)S(1)}, bf16[1024,256]{1,0:T(8,128)(2,1)}, u32[]{:S(2)}) copy-start(bf16[1024,256]{1,0:T(8,128)(2,1)} %param.30) | copy-start | bytes 1572868
  628.8 277.4 %all-reduce.4.cloned.1.call-start = ((), (), s32[]{:S(2)}) async-start(), calls=%async_computation.20 | async-start | bytes 33554432 | tf_op jit(solution)/shard_map/psum | solution.py:391
  629.1 6.2 copy-start.68
  629.1 6.2 copy-start.69
  635.2 4.8 copy-start.27
  635.2 4.8 copy-start.66
  640.0 3.5 copy-start.17
  640.0 3.6 copy-start.63
  648.1 3.4 copy-start.21
  649.9 3.5 copy-start.39
  655.0 331.3 %reduce-scatter.20.cloned.1.call-start = ((), (), s32[]{:S(2)}) async-start(), calls=%async_computation.19 | async-start | bytes 5242880 | tf_op jit(solution)/shard_map/reduce_scatter | solution.py:352
  660.8 14.4 %copy-start.30 = (bf16[256,1024]{1,0:T(8,128)(2,1)S(1)}, bf16[256,1024]{1,0:T(8,128)(2,1)}, u32[]{:S(2)}) copy-start(bf16[256,1024]{1,0:T(8,128)(2,1)} %param.22) | copy-start | bytes 1572868
  660.8 14.4 %copy-start.58 = (f32[1024]{0:T(1024)S(1)}, f32[1024]{0:T(1024)}, u32[]{:S(2)}) copy-start(f32[1024]{0:T(1024)} %param.27) | copy-start | bytes 12292
  660.8 57.5 %copy-start.36 = (f32[256,1024]{1,0:T(8,128)S(1)}, f32[256,1024]{1,0:T(8,128)}, u32[]{:S(2)}) copy-start(f32[256,1024]{1,0:T(8,128)} %get-tuple-element.146) | copy-start | bytes 3145732
  906.2 82.5 %copy-start.45 = (f32[1024,256]{1,0:T(8,128)S(1)}, f32[1024,256]{1,0:T(8,128)}, u32[]{:S(2)}) copy-start(f32[1024,256]{1,0:T(8,128)} %get-tuple-element.160) | copy-start | bytes 3145732
  906.2 83.4 %copy-start.44 = (f32[1024,256]{1,0:T(8,128)S(1)}, f32[1024,256]{1,0:T(8,128)}, u32[]{:S(2)}) copy-start(f32[1024,256]{1,0:T(8,128)} %get-tuple-element.161) | copy-start | bytes 3145732
  908.9 81.7 %copy-start.43 = (f32[256,1024]{1,0:T(8,128)S(1)}, f32[256,1024]{1,0:T(8,128)}, u32[]{:S(2)}) copy-start(f32[256,1024]{1,0:T(8,128)} %get-tuple-element.162) | copy-start | bytes 3145732
  986.3 5.3 copy-start.42
  988.7 3.9 copy-start.41
  989.6 3.9 copy-start.35
  993.5 3.7 copy-start.34
  993.5 5.7 copy-start.1
  (21 other events, 35.8 us)
Sparse Core Ops, SparseCore 0:
  12.3 48.0 all-gather.6
  76.4 45.4 reduce-scatter.7
  126.8 45.4 all-gather.8
  190.8 49.1 reduce-scatter.9
  243.9 45.4 all-gather.10
  290.8 44.6 all-gather.12
  348.4 42.4 reduce-scatter.13
  393.3 43.1 reduce-scatter.11
  439.7 45.4 all-gather.14
  510.2 51.5 reduce-scatter.15
  566.3 45.4 all-gather.16
  628.9 46.2 reduce-scatter.17
  682.7 223.4 all-reduce.3
  909.6 76.6 reduce-scatter.19

commit v2 on v1

--- a/solution.py
+++ b/solution.py
@@ -25,78 +25,6 @@
     return 0.5 * (1.0 + inner) + 0.5 * values * (1.0 - inner * inner) * tanh_coeff * (
         1.0 + 3.0 * cubic_coeff * values * values
     )
-
-
-def segment_ids(lengths, count):
-    ends = jnp.cumsum(lengths, dtype=jnp.int32)
-    places = jnp.arange(count, dtype=jnp.int32)
-    return jnp.sum((places[:, None] >= ends[None, :]).astype(jnp.int32), axis=1)
-
-
-def normalize(rows, gain, shift):
-    centred = rows - jnp.mean(rows, axis=1, keepdims=True)
-    inverse = lax.rsqrt(jnp.mean(centred * centred, axis=1, keepdims=True) + eps)
-    unit = centred * inverse
-    return (unit * gain + shift, unit, inverse)
-
-
-def normalize_back(grad_out, unit, inverse, gain):
-    scaled = grad_out * gain
-    inner = (
-        scaled
-        - jnp.mean(scaled, axis=1, keepdims=True)
-        - unit * jnp.mean(scaled * unit, axis=1, keepdims=True)
-    )
-    return (inner * inverse, jnp.sum(grad_out * unit, axis=0), jnp.sum(grad_out, axis=0))
-
-
-def along_rows(left, right):
-    return lax.dot_general(
-        left, right, (((0,), (0,)), ((), ())), preferred_element_type=jnp.float32
-    )
-
-
-def against(left, weight):
-    return lax.dot_general(
-        left, weight, (((1,), (1,)), ((), ())), preferred_element_type=jnp.float32
-    )
-
-
-def spread_normed(rows):
-    return lax.all_gather(rows, "tensor", axis=0, tiled=True)
-
-
-def spread_grads(rows):
-    return lax.all_gather(rows, "tensor", axis=0, tiled=True)
-
-
-def sum_branch(left, weight, rows):
-
-    def term(start, count):
-        return jnp.dot(left, weight, preferred_element_type=jnp.float32)
-
-    return lax.psum_scatter(
-        term(jnp.int32(0), lax.axis_size("tensor") * rows).astype(jnp.bfloat16),
-        "tensor",
-        scatter_dimension=0,
-        tiled=True,
-    ).astype(jnp.float32)
-
-
-def sum_inputs(pairs, rows):
-
-    def term(start, count):
-        total = jnp.zeros((count, pairs[0][1].shape[0]), jnp.float32)
-        for left, weight in pairs:
-            total = total + against(left, weight)
-        return total
-
-    return lax.psum_scatter(
-        term(jnp.int32(0), lax.axis_size("tensor") * rows).astype(jnp.bfloat16),
-        "tensor",
-        scatter_dimension=0,
-        tiled=True,
-    ).astype(jnp.float32)
 
 
 BF=jnp.bfloat16
@@ -259,6 +187,118 @@
     return tseg,eseg,kpad,slo,shi,clo,chi
 
 
+def along_rows(left, right):
+    return lax.dot_general(
+        left, right, (((0,), (0,)), ((), ())), preferred_element_type=jnp.float32
+    )
+
+
+def against(left, weight):
+    return lax.dot_general(
+        left, weight, (((1,), (1,)), ((), ())), preferred_element_type=jnp.float32
+    )
+
+
+def times(left, weight):
+    return jnp.dot(left, weight, preferred_element_type=jnp.float32)
+
+
+def moments(rows):
+    centred = rows - jnp.mean(rows, axis=1, keepdims=True)
+    inverse = lax.rsqrt(jnp.mean(centred * centred, axis=1, keepdims=True) + eps)
+    return centred * inverse, inverse
+
+
+def normalize_back(grad_out, unit, inverse, gain):
+    scaled = grad_out * gain
+    inner = (
+        scaled
+        - jnp.mean(scaled, axis=1, keepdims=True)
+        - unit * jnp.mean(scaled * unit, axis=1, keepdims=True)
+    )
+    return (inner * inverse, jnp.sum(grad_out * unit, axis=0), jnp.sum(grad_out, axis=0))
+
+
+class Place:
+    def __init__(self):
+        self.dp = lax.axis_size("dp")
+        self.tensor = lax.axis_size("tensor")
+        self.d = lax.axis_index("dp")
+        self.t = lax.axis_index("tensor")
+        self.core = self.d % 2
+        self.half = self.t // 2
+        self.side = self.t % 2
+        self.keeper = self.core == self.half
+        self.shard = jnp.where(self.keeper, self.t, self.t ^ 2)
+
+    def swap(self, value, d_flip, t_flip, only=None):
+        pairs = []
+        for d in range(self.dp):
+            for t in range(self.tensor):
+                keeper = d % 2 == t // 2
+                if only is None or only == keeper:
+                    pairs.append((d * self.tensor + t, (d ^ d_flip) * self.tensor + (t ^ t_flip)))
+        return lax.ppermute(value, ("dp", "tensor"), pairs)
+
+    def home(self, value):
+        return jnp.where(self.keeper, value, self.swap(value, 1, 2, False))
+
+    def ordered(self, mine, other, which):
+        return jnp.where(
+            which == 0, jnp.concatenate([mine, other]), jnp.concatenate([other, mine])
+        )
+
+    def part(self, value, which, parts):
+        size = value.shape[0] // parts
+        return lax.dynamic_slice_in_dim(value, which * size, size, 0)
+
+    def both_cores(self, half_rows):
+        return self.ordered(half_rows, self.swap(half_rows, 1, 0), self.core)
+
+    def spread_columns(self, value):
+        near, far = self.part(value, self.core, 2), self.part(value, 1 - self.core, 2)
+        return jnp.concatenate(
+            [near, self.swap(far, 1, 0), self.swap(near, 0, 1), self.swap(far, 1, 1)], axis=1
+        )
+
+    def order(self):
+        return [self.shard, self.shard ^ 2, self.shard ^ 1, self.shard ^ 3]
+
+    def sum_half(self, value):
+        near, far = self.part(value, self.core, 2), self.part(value, 1 - self.core, 2)
+        return near.astype(jnp.float32) + self.swap(far.astype(jnp.bfloat16), 1, 0).astype(jnp.float32)
+
+    def sum_group_half(self, value):
+        mine = self.sum_half(value).astype(jnp.bfloat16)
+        return mine.astype(jnp.float32) + self.swap(mine, 0, 1).astype(jnp.float32)
+
+    def sum_group_quarter(self, value):
+        mine = self.sum_half(value)
+        near, far = self.part(mine, self.side, 2), self.part(mine, 1 - self.side, 2)
+        return near + self.swap(far.astype(jnp.bfloat16), 0, 1).astype(jnp.float32)
+
+    def moved_weight(self, weight):
+        piece = self.swap(self.part(weight, self.d, self.dp), 0, 2)
+        return jnp.where(self.keeper, weight, lax.all_gather(piece, "dp", axis=0, tiled=True))
+
+    def whole_weight(self, weight):
+        piece = self.part(weight, self.d, self.dp)
+        every = lax.all_gather(piece, ("dp", "tensor"), axis=0, tiled=False)
+        every = every.reshape((self.dp, self.tensor) + piece.shape)
+        return jnp.swapaxes(every, 0, 1).reshape((self.tensor,) + weight.shape)
+
+    def sum_weight(self, grad):
+        groups = [[d for d in range(self.dp) if d % 2 == c] for c in range(2)]
+        piece = lax.psum_scatter(
+            grad.astype(jnp.bfloat16), "dp", scatter_dimension=0, axis_index_groups=groups, tiled=True
+        )
+        total = piece.astype(jnp.float32) + self.swap(piece, 0, 2, False).astype(jnp.float32)
+        total = total.astype(jnp.bfloat16)
+        near, far = self.part(total, self.core, 2), self.part(total, 1 - self.core, 2)
+        piece = jnp.where(self.keeper, near, self.swap(far, 1, 0, True))
+        return lax.all_gather(piece, "dp", axis=0, tiled=True).astype(jnp.float32)
+
+
 def on_device(
     tokens,
     encoder_states,
@@ -283,126 +323,136 @@
     reduce_weight,
     cotangent,
 ):
-    share = tokens.shape[0]
+    place = Place()
+    width = causal_query.shape[1]
     length = pad_mask.shape[0]
     frames = encoder_states.shape[0]
-    heads = causal_query.shape[1] // HEAD_DIM
-    scale = HEAD_DIM ** (-0.5)
+
+    def of_group(value):
+        return jnp.where(place.keeper, value, place.swap(value, 1, 0))
+
+    def half_rows(quarter):
+        return place.ordered(quarter, place.swap(quarter, 0, 1), place.side)
+
+    def quarter_of(half):
+        return place.part(half, place.side, 2)
+
+    tok_lengths, enc_lengths, pad_mask = of_group(tok_lengths), of_group(enc_lengths), of_group(pad_mask)
+    block_q, block_k = 256, 512
     token_seg, frame_seg, key_seg, self_lo, self_hi, cross_lo, cross_hi = ranges(
-        tok_lengths[0], enc_lengths[0], pad_mask, length, frames, 256, 512
+        tok_lengths[0], enc_lengths[0], pad_mask, length, frames, block_q, block_k
     )
     self_keys = jnp.stack([token_seg, key_seg] + [token_seg] * 6)
     cross_keys = jnp.stack([frame_seg] * 8)
     seg_col, seg_row = token_seg[:, None], token_seg[None, :]
-    residual = tokens.astype(jnp.float32)
-    first_out, first_unit, first_inv = normalize(residual, first_gain, first_shift)
-    first_all = spread_normed(first_out.astype(jnp.bfloat16))
-    query = jnp.dot(first_all, causal_query, preferred_element_type=jnp.float32).astype(
-        jnp.bfloat16
-    )
-    keyed = jnp.dot(first_all, causal_key, preferred_element_type=jnp.float32).astype(jnp.bfloat16)
-    valued = jnp.dot(first_all, causal_value, preferred_element_type=jnp.float32).astype(
-        jnp.bfloat16
-    )
+
+    first_weight = place.moved_weight(
+        jnp.concatenate([causal_query, causal_key, causal_value], axis=1)
+    )
+    tokens_here = place.home(tokens)
+    tokens_half = half_rows(tokens_here)
+    residual = tokens_half.astype(jnp.float32)
+    unit, inverse = moments(residual)
+    first_all = place.both_cores((unit * first_gain + first_shift).astype(jnp.bfloat16))
+    mixed_in = times(first_all, first_weight).astype(jnp.bfloat16)
+    query, keyed, valued = (mixed_in[:, i * width : (i + 1) * width] for i in range(3))
+
+    encoder = of_group(encoder_states)
+    cross_weight = place.moved_weight(jnp.concatenate([cross_key, cross_value], axis=1))
+    cross_in = times(encoder, cross_weight).astype(jnp.bfloat16)
+    ckeyed, cvalued = cross_in[:, :width], cross_in[:, width:]
+    causal_out_all = place.whole_weight(causal_out)
+    cross_out_all = place.whole_weight(cross_out)
+    cross_query_all = place.whole_weight(cross_query)
+    order = place.order()
+    pick = lambda every, which: lax.dynamic_index_in_dim(every, which, 0, keepdims=False)
+    causal_out_perm = jnp.concatenate([pick(causal_out_all, s) for s in order])
+    cross_out_perm = jnp.concatenate([pick(cross_out_all, s) for s in order])
+    cross_query_perm = jnp.concatenate([pick(cross_query_all, s) for s in order], axis=1)
+    causal_out_here, cross_out_here = causal_out_perm[:width], cross_out_perm[:width]
+    cross_query_here = cross_query_perm[:, :width]
+
     mixed, self_logsum = attend_fwd(
-        query, keyed, valued, seg_col, self_keys, self_lo, self_hi, True, 256, 512
-    )
-    after_self = residual + sum_branch(mixed, causal_out, share)
-    second_out, second_unit, second_inv = normalize(after_self, second_gain, second_shift)
-    second_all = spread_normed(second_out.astype(jnp.bfloat16))
-    cquery = jnp.dot(second_all, cross_query, preferred_element_type=jnp.float32).astype(
-        jnp.bfloat16
-    )
-    ckeyed = jnp.dot(encoder_states, cross_key, preferred_element_type=jnp.float32).astype(
-        jnp.bfloat16
-    )
-    cvalued = jnp.dot(encoder_states, cross_value, preferred_element_type=jnp.float32).astype(
-        jnp.bfloat16
-    )
+        query, keyed, valued, seg_col, self_keys, self_lo, self_hi, True, block_q, block_k
+    )
+    after_self = residual + times(place.spread_columns(mixed), causal_out_perm)
+    second_unit, second_inv = moments(after_self)
+    second_all = place.both_cores((second_unit * second_gain + second_shift).astype(jnp.bfloat16))
+    cquery = times(second_all, cross_query_here).astype(jnp.bfloat16)
     cmixed, cross_logsum = attend_fwd(
-        cquery, ckeyed, cvalued, seg_col, cross_keys, cross_lo, cross_hi, False, 256, 512
-    )
-    after_cross = after_self + sum_branch(cmixed, cross_out, share)
-    third_out, third_unit, third_inv = normalize(after_cross, third_gain, third_shift)
-    third_all = spread_normed(third_out.astype(jnp.bfloat16))
-    pre_act = jnp.dot(third_all, expand_weight, preferred_element_type=jnp.float32)
+        cquery, ckeyed, cvalued, seg_col, cross_keys, cross_lo, cross_hi, False, block_q, block_k
+    )
+    after_cross = after_self + times(place.spread_columns(cmixed), cross_out_perm)
+    third_unit, third_inv = moments(after_cross)
+    third_all = place.both_cores((third_unit * third_gain + third_shift).astype(jnp.bfloat16))
+
+    ff_weight = place.moved_weight(jnp.concatenate([expand_weight, reduce_weight], axis=1))
+    hidden_width = expand_weight.shape[1]
+    expand_here, reduce_here = ff_weight[:, :hidden_width], ff_weight[:, hidden_width:]
+    cot_half = half_rows(place.home(cotangent))
+    grad_top = place.both_cores(cot_half)
+    grad_hidden = against(grad_top, reduce_here).astype(jnp.bfloat16)
+
+    pre_act = times(third_all, expand_here)
     hidden = smooth_gate(pre_act).astype(jnp.bfloat16)
-    output = (after_cross + sum_branch(hidden, reduce_weight, share)).astype(jnp.bfloat16)
-    grad_res = cotangent.astype(jnp.float32)
-    grad_top = spread_grads(grad_res.astype(jnp.bfloat16))
-    reduce_grad = along_rows(hidden, grad_top)
-    grad_hidden = against(grad_top, reduce_weight)
-    grad_expand_in = (grad_hidden * smooth_slope(pre_act)).astype(jnp.bfloat16)
-    expand_grad = along_rows(third_all, grad_expand_in)
-    third_in = sum_inputs(((grad_expand_in, expand_weight),), share)
+    grad_expand_in = (grad_hidden.astype(jnp.float32) * smooth_slope(pre_act)).astype(jnp.bfloat16)
+    third_in = place.sum_group_half(against(grad_expand_in, expand_here))
     back_rows, third_gain_grad, third_shift_grad = normalize_back(
         third_in, third_unit, third_inv, third_gain
     )
-    grad_res = grad_res + back_rows
-    grad_top = spread_grads(grad_res.astype(jnp.bfloat16))
+    grad_res = cot_half.astype(jnp.float32) + back_rows
+    out_here = quarter_of(after_cross) + place.sum_group_quarter(times(hidden, reduce_here))
+    output = place.home(out_here.astype(jnp.bfloat16))
+    reduce_grad = along_rows(hidden, grad_top)
+    expand_grad = along_rows(third_all, grad_expand_in)
+
+    grad_top = place.both_cores(grad_res.astype(jnp.bfloat16))
     cross_out_grad = along_rows(cmixed, grad_top)
-    grad_cmixed = against(grad_top, cross_out).astype(jnp.bfloat16)
+    grad_cmixed = against(grad_top, cross_out_here).astype(jnp.bfloat16)
     grad_cquery, grad_ckey, grad_cvalue = attend_bwd(
         cquery, ckeyed, cvalued, cmixed, grad_cmixed, cross_logsum, seg_row, cross_keys.T,
-        cross_lo, cross_hi, False, 256, 512,
-    )
+        cross_lo, cross_hi, False, block_q, block_k,
+    )
+    grad_cross_in = jnp.concatenate([grad_ckey, grad_cvalue], axis=1)
+    cross_grad = along_rows(encoder, grad_cross_in)
     cross_query_grad = along_rows(second_all, grad_cquery)
-    cross_key_grad = along_rows(encoder_states, grad_ckey)
-    cross_value_grad = along_rows(encoder_states, grad_cvalue)
-    encoder_grad = lax.psum_scatter(
-        (against(grad_ckey, cross_key) + against(grad_cvalue, cross_value)).astype(jnp.bfloat16),
-        "tensor",
-        scatter_dimension=0,
-        tiled=True,
-    )
-    second_in = sum_inputs(((grad_cquery, cross_query),), share)
+    encoder_grad = place.home(
+        place.sum_group_quarter(against(grad_cross_in, cross_weight)).astype(jnp.bfloat16)
+    )
+    second_in = against(place.spread_columns(grad_cquery), cross_query_perm)
     back_rows, second_gain_grad, second_shift_grad = normalize_back(
         second_in, second_unit, second_inv, second_gain
     )
     grad_res = grad_res + back_rows
-    grad_top = spread_grads(grad_res.astype(jnp.bfloat16))
+    grad_top = place.both_cores(grad_res.astype(jnp.bfloat16))
     causal_out_grad = along_rows(mixed, grad_top)
-    grad_mixed = against(grad_top, causal_out).astype(jnp.bfloat16)
+    grad_mixed = against(grad_top, causal_out_here).astype(jnp.bfloat16)
     grad_query, grad_key, grad_value = attend_bwd(
         query, keyed, valued, mixed, grad_mixed, self_logsum, seg_row, self_keys.T,
-        self_lo, self_hi, True, 256, 512,
-    )
-    causal_query_grad = along_rows(first_all, grad_query)
-    causal_key_grad = along_rows(first_all, grad_key)
-    causal_value_grad = along_rows(first_all, grad_value)
-    first_in = sum_inputs(
-        ((grad_query, causal_query), (grad_key, causal_key), (grad_value, causal_value)), share
-    )
+        self_lo, self_hi, True, block_q, block_k,
+    )
+    grad_in = jnp.concatenate([grad_query, grad_key, grad_value], axis=1)
+    causal_grad = along_rows(first_all, grad_in)
+    first_in = place.sum_group_quarter(against(grad_in, first_weight))
+    first_unit, first_inv = moments(tokens_here.astype(jnp.float32))
     back_rows, first_gain_grad, first_shift_grad = normalize_back(
         first_in, first_unit, first_inv, first_gain
     )
-    tokens_grad = (grad_res + back_rows).astype(jnp.bfloat16)
-    (
-        causal_query_grad,
-        causal_key_grad,
-        causal_value_grad,
-        causal_out_grad,
-        cross_query_grad,
-        cross_key_grad,
-        cross_value_grad,
-        cross_out_grad,
-        expand_grad,
-        reduce_grad,
-    ) = lax.psum(
-        (
-            causal_query_grad,
-            causal_key_grad,
-            causal_value_grad,
-            causal_out_grad,
-            cross_query_grad,
-            cross_key_grad,
-            cross_value_grad,
-            cross_out_grad,
-            expand_grad,
-            reduce_grad,
-        ),
-        "dp",
-    )
+    tokens_grad = place.home((quarter_of(grad_res) + back_rows).astype(jnp.bfloat16))
+
+    ff_grad = place.sum_weight(jnp.concatenate([expand_grad, reduce_grad.T], axis=1))
+    expand_grad, reduce_grad = ff_grad[:, :hidden_width], ff_grad[:, hidden_width:].T
+    cross_grads = place.sum_weight(jnp.concatenate([cross_grad, cross_query_grad], axis=1))
+    cross_key_grad, cross_value_grad, cross_query_grad = (
+        cross_grads[:, i * width : (i + 1) * width] for i in range(3)
+    )
+    causal_grads = place.sum_weight(causal_grad)
+    causal_query_grad, causal_key_grad, causal_value_grad = (
+        causal_grads[:, i * width : (i + 1) * width] for i in range(3)
+    )
+    cross_out_grad = place.sum_weight(cross_out_grad)
+    causal_out_grad = place.sum_weight(causal_out_grad)
+    once = (place.side == 0).astype(jnp.float32)
     (
         first_gain_grad,
         first_shift_grad,
@@ -414,10 +464,10 @@
         (
             first_gain_grad,
             first_shift_grad,
-            second_gain_grad,
-            second_shift_grad,
-            third_gain_grad,
-            third_shift_grad,
+            second_gain_grad * once,
+            second_shift_grad * once,
+            third_gain_grad * once,
+            third_shift_grad * once,
         ),
         ("dp", "tensor"),
     )

time: 1010 us -> 761 us (0.75)
  waiting for transfers between devices: 759 us -> 330 us
  starting transfers between devices: 2.03 us -> 81.2 us
  local copies, waits for them, and re-layouts: 25.6 us -> 66.6 us
  other arithmetic: 29 us -> 54 us
  blocking collectives: 41.4 us -> 61.7 us
    reduce_scatter x7 -> x5, waiting for transfers between devices: 315 us -> 38.8 us  [sum_weight(): lax.psum_scatter(grad.astype(jnp.bfloat16), 'dp', scatter_dimension=0, ax...]
    psum x1 -> x0, waiting for transfers between devices: 186 us -> none  [on_device(): lax.psum((causal_query_grad, causal_key_grad, causal_value_grad, causal_o...]
    ppermute x0 -> x47, waiting for transfers between devices: none -> 155 us  [swap(): return lax.ppermute(value, ('dp', 'tensor'), pairs)]
    all_gather x6 -> x9, waiting for transfers between devices: 258 us -> 136 us  [the longest x3 92.7 us: whole_weight(): every = lax.all_gather(piece, ('dp', 'tensor'), axis=0, tiled=False)]
    ppermute x0 -> x47, starting transfers between devices: none -> 80.1 us  [swap(): return lax.ppermute(value, ('dp', 'tensor'), pairs)]
    all_gather x0 -> x2, blocking collectives: none -> 22.2 us  [sum_weight(): return lax.all_gather(piece, 'dp', axis=0, tiled=True).astype(jnp.float32)]
    select_n x1 -> x11, other arithmetic: 0.01 us -> 12.9 us  [the longest x4 5.11 us: home(): return jnp.where(self.keeper, value, self.swap(value, 1, 2, False))]
    convert_element_type x6 -> x17, other arithmetic: 13.3 us -> 24.2 us  [the longest x2 6.09 us: on_device(): grad_top = place.both_cores(grad_res.astype(jnp.bfloat16))]
  transfers between devices with their start and end apart: 14 -> 61, of which waited for: 14 -> 27; matrix products, arithmetic and copies ran while one was open for 6% -> 20% of each run, Pallas kernels for 0% -> 5%
where the time goes in v2:
time: 761 us; the launch traced here: 755 us
  waiting for transfers between devices  330 us (43%)
  matrix products  88 us (12%)
  starting transfers between devices  81.2 us (11%)
  local copies, waits for them, and re-layouts  66.6 us (9%)
  blocking collectives  61.7 us (8%)
  Pallas kernels  58 us (8%)
  other arithmetic  54 us (7%)
  between operations  16.1 us (2%)
    ppermute x47, waiting for transfers between devices, swap(): return lax.ppermute(value, ('dp', 'tensor'), pairs)  155 us
    all_gather x3, waiting for transfers between devices, whole_weight(): every = lax.all_gather(piece, ('dp', 'tensor'), axis=0, tiled=False)  92.7 us
    ppermute x47, starting transfers between devices, swap(): return lax.ppermute(value, ('dp', 'tensor'), pairs)  80.1 us
    all_gather x3, waiting for transfers between devices, moved_weight(): lax.all_gather(piece, 'dp', axis=0, tiled=True)  43.1 us
    psum x1, blocking collectives, on_device(): lax.psum((first_gain_grad, first_shift_grad, second_gain_grad * once, sec...  39.5 us
    reduce_scatter x5, waiting for transfers between devices, sum_weight(): lax.psum_scatter(grad.astype(jnp.bfloat16), 'dp', scatter_dimension=0, ax...  38.8 us
    dot_general x7, matrix products, along_rows(): lax.dot_general(left, right, (((0,), (0,)), ((), ())), preferred_element_...  32.6 us
    pallas_call x2, Pallas kernels, attend_bwd(): pl.pallas_call(functools.partial(bwd_kernel, causal, heads, bq, bk), out_...  32.2 us
  transfers between devices with their start and end apart: 61, of which 27 were waited for; matrix products, arithmetic and copies ran while one was open for 20% of the time, Pallas kernels for 5%

profile of v2, /device:TPU:1, one launch (start us, length us, event | category | flops | bytes accessed | tf_op | source)
XLA Modules:
  0.0 755.4 jit_solution(7471129340464138385)
XLA Ops:
  13.3 3.2 collective-permute-start.4
  16.5 8.8 %collective-permute-done.4 = bf16[128,768]{1,0:T(8,128)(2,1)S(1)} collective-permute-done((bf16[128,768]{1,0:T(8,128)(2,1)S(1)}, bf16[128,768]{1,0:T(8,128)(2,1)S(1)}, u32[]{:S(2)}, u32[]{:S(2)}) %collective-permute-start.4) | collective-permute-done | bytes 196640 | tf_op jit(solution)/shard_map/ppermute | solution.py:241
  28.6 4.7 collective-permute-done.12
  35.6 6.3 collective-permute-start
  48.6 4.3 collective-permute-start.21
  53.0 22.6 %collective-permute-done = bf16[256,1024]{1,0:T(8,128)(2,1)S(1)} collective-permute-done((bf16[256,1024]{1,0:T(8,128)(2,1)S(1)}, bf16[256,1024]{1,0:T(8,128)(2,1)S(1)}, u32[]{:S(2)}, u32[]{:S(2)}) %collective-permute-start) | collective-permute-done | bytes 524320 | tf_op jit(solution)/shard_map/ppermute | solution.py:241
  76.4 2.6 collective-permute-start.1
  79.2 15.9 %collective-permute-done.1 = bf16[256,1024]{1,0:T(8,128)(2,1)S(1)} collective-permute-done((bf16[256,1024]{1,0:T(8,128)(2,1)S(1)}, bf16[256,1024]{1,0:T(8,128)(2,1)S(1)}, u32[]{:S(2)}, u32[]{:S(2)}) %collective-permute-start.1) | collective-permute-done | bytes 524320 | tf_op jit(solution)/shard_map/ppermute | solution.py:241
  100.5 4.5 convolution_convert_fusion.4
  105.1 10.8 %attend_fwd.2 = (bf16[1024,256]{1,0:T(8,128)(2,1)S(1)}, f32[8,1024]{1,0:T(8,128)S(1)}) custom-call(s32[4]{0:T(128)S(1)} %get-tuple-element.196.lo_ref, s32[4]{0:T(128)S(1)} %get-tuple-element.195.hi_ref, bf16[1024,256]{1,0:T(8,128)(2,1)S(1)} %get-tuple-element.183.q_ref, bf16[1024,256]{1,0:T(8,128)(2,1)S(1)} %get-tuple-element.182.k_ref, ...), custom_call_target="tpu_custom_call" | custom-call | tf_op jit(solution)/shard_map/attend_fwd/pallas_call | solution.py:102
  120.2 5.7 all-gather.25.cloned.1.call-done
  125.9 3.2 copy.88
  129.1 55.5 %all-gather.27.cloned.1.call-done = bf16[4096,256]{1,0:T(8,128)(2,1)} async-done(((bf16[128,256]{1,0:T(8,128)(2,1)}), bf16[4096,256]{1,0:T(8,128)(2,1)}) %all-gather.27.cloned.1.call-update) | async-done | bytes 2097168 | tf_op jit(solution)/shard_map/all_gather | solution.py:286
  187.1 2.6 fusion.115
  193.5 15.8 %all-gather.15.cloned.1.call-done = bf16[1024,512]{1,0:T(8,128)(2,1)} async-done(((bf16[128,512]{1,0:T(8,128)(2,1)}), bf16[1024,512]{1,0:T(8,128)(2,1)}) %all-gather.15.cloned.1.call-update) | async-done | bytes 1048592 | tf_op jit(solution)/shard_map/all_gather | solution.py:282
  209.3 4.8 convolution_convert_fusion
  215.2 2.9 convolution_convert_fusion.10.q_ref
  218.2 15.0 %attend_fwd.3 = (bf16[1024,256]{1,0:T(8,128)(2,1)S(1)}, f32[8,1024]{1,0:T(8,128)S(1)}) custom-call(s32[4]{0:T(128)S(1)} %and_select_fusion.1.lo_ref, s32[4]{0:T(128)S(1)} %and_select_fusion.hi_ref, bf16[1024,256]{1,0:T(8,128)(2,1)S(1)} %convolution_convert_fusion.10.q_ref, bf16[2048,256]{1,0:T(8,128)(2,1)S(1)} %get-tuple-element.166.k_ref, ...), custom_call_target="tpu_custom_call" | custom-call | tf_op jit(solution)/shard_map/attend_fwd/pallas_call | solution.py:102
  239.0 31.5 %all-gather.29.cloned.1.call-done = bf16[1024,1024]{1,0:T(8,128)(2,1)} async-done(((bf16[32,1024]{1,0:T(8,128)(2,1)}), bf16[1024,1024]{1,0:T(8,128)(2,1)}) %all-gather.29.cloned.1.call-update) | async-done | bytes 2097168 | tf_op jit(solution)/shard_map/all_gather | solution.py:286
  279.0 2.7 maximum_select_fusion.7
  282.0 27.2 %all-gather.17.cloned.1.call-done = bf16[1024,2048]{1,0:T(8,128)(2,1)} async-done(((bf16[128,2048]{1,0:T(8,128)(2,1)}), bf16[1024,2048]{1,0:T(8,128)(2,1)}) %all-gather.17.cloned.1.call-update) | async-done | bytes 4194320 | tf_op jit(solution)/shard_map/all_gather | solution.py:282
  309.2 2.6 broadcast_select_fusion
  311.8 6.0 fusion.44
  317.9 8.1 %fusion.6 = bf16[1024,1024]{1,0:T(8,128)(2,1)S(1)} fusion(f32[1024,1024]{1,0:T(8,128)S(1)} %fusion.44, bf16[1024,2048]{1,0:T(8,128)(2,1)S(1)} %broadcast_select_fusion, bf16[512,1024]{1,0:T(8,128)(2,1)} %collective-permute-done.23, bf16[512,1024]{1,0:T(8,128)(2,1)} %maximum_select_fusion.7, pred[]{:T(512)S(6)} %eq.30), kind=kOutput, calls=%fused_computation.8 | convolution fusion | flops 2178940928 | bytes 10485761 | tf_op jit(solution)/shard_map/dot_general | solution.py:197
  333.0 23.3 %collective-permute-done.25 = bf16[512,1024]{1,0:T(8,128)(2,1)S(1)} collective-permute-done((bf16[512,1024]{1,0:T(8,128)(2,1)S(1)}, bf16[512,1024]{1,0:T(8,128)(2,1)S(1)}, u32[]{:S(2)}, u32[]{:S(2)}) %collective-permute-start.25) | collective-permute-done | bytes 1048608 | tf_op jit(solution)/shard_map/ppermute | solution.py:241
  357.8 3.7 fusion.110
  366.2 19.3 %attend_bwd.2 = (bf16[1024,256]{1,0:T(8,128)(2,1)S(1)}, bf16[2048,256]{1,0:T(8,128)(2,1)S(1)}, bf16[2048,256]{1,0:T(8,128)(2,1)S(1)}) custom-call(s32[4]{0:T(128)S(1)} %and_select_fusion.1.lo_ref, s32[4]{0:T(128)S(1)} %and_select_fusion.hi_ref, bf16[1024,256]{1,0:T(8,128)(2,1)S(1)} %copy-done.11, bf16[2048,256]{1,0:T(8,128)(2,1)S(1)} %get-tuple-element.166.k_ref, ...), custom_call_target="tpu_custom_call" | custom-call | tf_op jit(solution)/shard_map/attend_bwd/pallas_call | solution.py:166
  390.3 5.3 fusion.53
  395.6 3.2 convolution_convert_fusion.6
  401.0 3.6 multiply_reduce_fusion.1
  410.0 2.8 convolution_convert_fusion.8.do_ref
  412.8 12.9 %attend_bwd.3 = (bf16[1024,256]{1,0:T(8,128)(2,1)S(1)}, bf16[1024,256]{1,0:T(8,128)(2,1)S(1)}, bf16[1024,256]{1,0:T(8,128)(2,1)S(1)}) custom-call(s32[4]{0:T(128)S(1)} %get-tuple-element.196.lo_ref, s32[4]{0:T(128)S(1)} %get-tuple-element.195.hi_ref, bf16[1024,256]{1,0:T(8,128)(2,1)S(1)} %copy-done.5, bf16[1024,256]{1,0:T(8,128)(2,1)S(1)} %copy-done.3, ...), custom_call_target="tpu_custom_call" | custom-call | tf_op jit(solution)/shard_map/attend_bwd/pallas_call | solution.py:166
  425.9 6.0 convolution_convert_fusion.3
  432.2 5.5 convolution_convert_fusion.2
  437.7 5.4 convolution_convert_fusion.1
  446.7 3.3 convolution_convert_fusion.5
  451.6 3.9 convolution_convert_fusion.7
  458.1 9.6 %collective-permute-done.42 = bf16[128,768]{1,0:T(8,128)(2,1)S(1)} collective-permute-done((bf16[128,768]{1,0:T(8,128)(2,1)S(1)}, bf16[128,768]{1,0:T(8,128)(2,1)S(1)}, u32[]{:S(2)}, u32[]{:S(2)}) %collective-permute-start.42) | collective-permute-done | bytes 196640 | tf_op jit(solution)/shard_map/ppermute | solution.py:241
  468.5 2.9 reduce-scatter.6.cloned.1.call-done
  471.5 4.0 collective-permute-start.37
  475.5 5.0 collective-permute-done.37
  483.1 7.3 collective-permute-done.38
  491.3 35.9 %reduce-scatter.14.cloned.1.call-done = bf16[256,2048]{0,1:T(8,128)(2,1)} async-done(((bf16[1024,2048]{0,1:T(8,128)(2,1)}), bf16[256,2048]{0,1:T(8,128)(2,1)}) %reduce-scatter.14.cloned.1.call-update) | async-done | bytes 1048592 | tf_op jit(solution)/shard_map/reduce_scatter | solution.py:292
  527.1 4.1 collective-permute-start.45
  531.2 5.5 fusion.40
  538.1 5.1 collective-permute-done.45
  546.9 12.4 %collective-permute-start.19 = (bf16[256,1024]{1,0:T(8,128)(2,1)S(1)}, bf16[256,1024]{1,0:T(8,128)(2,1)}, u32[]{:S(2)}, u32[]{:S(2)}) collective-permute-start(bf16[256,1024]{1,0:T(8,128)(2,1)S(1)} %dynamic-slice_convert_fusion.6), channel_id=1, source_target_pairs={{0,1},{1,0},{2,3},{3,2},{4,5},{5,4},{6,7},{7,6},{8,9},{9,8},{10,11... | collective-permute-start | bytes 1572872 | tf_op jit(solution)/shard_map/ppermute | solution.py:241
  560.9 8.5 %collective-permute-done.19 = bf16[256,1024]{1,0:T(8,128)(2,1)} collective-permute-done((bf16[256,1024]{1,0:T(8,128)(2,1)S(1)}, bf16[256,1024]{1,0:T(8,128)(2,1)}, u32[]{:S(2)}, u32[]{:S(2)}) %collective-permute-start.19) | collective-permute-done | bytes 524320 | tf_op jit(solution)/shard_map/ppermute | solution.py:241
  571.0 7.0 collective-permute-start.20
  578.0 7.0 fusion.88
  585.1 2.7 dynamic-slice_convert_fusion
  602.5 3.8 convert_add_fusion
  608.8 2.6 collective-permute-start.32
  612.6 4.9 collective-permute-start.39
  617.6 29.1 %collective-permute-done.39 = bf16[64,1024]{1,0:T(8,128)(2,1)S(1)} collective-permute-done((bf16[64,1024]{1,0:T(8,128)(2,1)}, bf16[64,1024]{1,0:T(8,128)(2,1)S(1)}, u32[]{:S(2)}, u32[]{:S(2)}) %collective-permute-start.39) | collective-permute-done | bytes 131104 | tf_op jit(solution)/shard_map/ppermute | solution.py:241
  654.5 4.3 collective-permute-start.33
  660.1 12.5 %all_gather.54 = bf16[256,1024]{1,0:T(8,128)(2,1)S(1)} all-gather(bf16[32,1024]{1,0:T(8,128)(2,1)S(1)} %dynamic-slice_select_fusion.3), channel_id=1, replica_groups=mesh['dp'=8,'tensor'=4] {'dp'}, dimensions={0}, use_global_device_ids=true | all-gather | bytes 589824 | tf_op jit(solution)/shard_map/all_gather | solution.py:299
  673.7 9.7 %all_gather.52 = bf16[256,1024]{1,0:T(8,128)(2,1)S(1)} all-gather(bf16[32,1024]{1,0:T(8,128)(2,1)S(1)} %dynamic-slice_select_fusion.4), channel_id=1, replica_groups=mesh['dp'=8,'tensor'=4] {'dp'}, dimensions={0}, use_global_device_ids=true | all-gather | bytes 589824 | tf_op jit(solution)/shard_map/all_gather | solution.py:299
  684.5 39.5 %all-reduce = (f32[1024]{0:T(1024)}, f32[1024]{0:T(1024)}, f32[1024]{0:T(1024)}, f32[1024]{0:T(1024)}, f32[1024]{0:T(1024)}, /*index=5*/f32[1024]{0:T(1024)}) all-reduce(f32[1024]{0:T(1024)S(1)} %get-tuple-element.142, f32[1024]{0:T(1024)S(1)} %get-tuple-element.145, ...), channel_id=1, replica_groups=mesh['dp'=8,'tensor'=4] {'dp','tensor'}, use_global_device_ids=true, to_apply=%region_22.23 | all-reduce | flops 6144 | bytes 49152 | tf_op jit(solution)/shard_map/psum | solution.py:463
  727.1 3.1 fusion.112
  730.3 3.1 fusion.113
  733.4 4.1 slice.81
  737.4 5.3 copy.95
  742.8 3.2 convert_element_type.256
  (366 shorter events, 131.1 us)
Async XLA Ops:
  7.2 93.3 %all-gather.13.cloned.1.call-start = ((), (), s32[]{:S(2)}) async-start(), calls=%async_computation.5 | async-start | bytes 1769472 | tf_op jit(solution)/shard_map/all_gather | solution.py:282
  13.3 12.0 %collective-permute-start.4 = (bf16[128,768]{1,0:T(8,128)(2,1)S(1)}, bf16[128,768]{1,0:T(8,128)(2,1)S(1)}, u32[]{:S(2)}, u32[]{:S(2)}) collective-permute-start(bf16[128,768]{1,0:T(8,128)(2,1)S(1)} %constant_dynamic-slice_fusion.16), channel_id=1, source_target_pairs={{0,2},{1,3},{2,0},{3,1},{4,6},{5,7},{6,4},{7,5},{8,10},{9,11},{10,... | collective-permute-start | bytes 589832 | tf_op jit(solution)/shard_map/ppermute | solution.py:241
  26.0 99.9 %all-gather.25.cloned.1.call-start = ((), (), s32[]{:S(2)}) async-start(), calls=%async_computation.16 | async-start | bytes 2162688 | tf_op jit(solution)/shard_map/all_gather | solution.py:286
  26.8 157.8 %all-gather.27.cloned.1.call-start = ((), (), s32[]{:S(2)}) async-start(), calls=%async_computation.17 | async-start | bytes 2162688 | tf_op jit(solution)/shard_map/all_gather | solution.py:286
  28.3 181.0 %all-gather.15.cloned.1.call-start = ((), (), s32[]{:S(2)}) async-start(), calls=%async_computation.6 | async-start | bytes 1179648 | tf_op jit(solution)/shard_map/all_gather | solution.py:282
  28.5 180.8 %copy-start.29 = (bf16[1024,512]{1,0:T(8,128)(2,1)}, bf16[1024,512]{1,0:T(8,128)(2,1)S(1)}, u32[]{:S(2)}) copy-start(bf16[1024,512]{1,0:T(8,128)(2,1)S(1)} %constant_dynamic-update-slice_fusion.3) | copy-start | bytes 3145732
  28.5 4.8 collective-permute-start.12
  34.0 236.6 %all-gather.29.cloned.1.call-start = ((), (), s32[]{:S(2)}) async-start(), calls=%async_computation.18 | async-start | bytes 2162688 | tf_op jit(solution)/shard_map/all_gather | solution.py:286
  35.5 273.6 %all-gather.17.cloned.1.call-start = ((), (), s32[]{:S(2)}) async-start(), calls=%async_computation.7 | async-start | bytes 4718592 | tf_op jit(solution)/shard_map/all_gather | solution.py:282
  35.6 40.0 %collective-permute-start = (bf16[256,1024]{1,0:T(8,128)(2,1)S(1)}, bf16[256,1024]{1,0:T(8,128)(2,1)S(1)}, u32[]{:S(2)}, u32[]{:S(2)}) collective-permute-start(bf16[256,1024]{1,0:T(8,128)(2,1)S(1)} %copy-done.37), channel_id=1, source_target_pairs={{2,4},{3,5},{4,2},{5,3},{10,12},{11,13},{12,10},{13,11},{18,20},{1... | collective-permute-start | bytes 1572872 | tf_op jit(solution)/shard_map/ppermute | solution.py:241
  46.8 49.1 %copy-start.56 = (f32[1024]{0:T(1024)S(1)}, f32[1024]{0:T(1024)}, u32[]{:S(2)}) copy-start(f32[1024]{0:T(1024)} %param.28) | copy-start | bytes 12292
  46.8 51.1 %collective-permute-start.17 = (bf16[128,2048]{1,0:T(8,128)(2,1)}, bf16[128,2048]{1,0:T(8,128)(2,1)S(1)}, u32[]{:S(2)}, u32[]{:S(2)}) collective-permute-start(bf16[128,2048]{1,0:T(8,128)(2,1)} %constant_dynamic-slice_fusion.6), channel_id=1, source_target_pairs={{0,2},{1,3},{2,0},{3,1},{4,6},{5,7},{6,4},{7,5},{8,10},{9,11},{10,... | collective-permute-start | bytes 1572872 | tf_op jit(solution)/shard_map/ppermute | solution.py:241
  46.9 1.2 collective-permute-start.9
  47.3 1.3 collective-permute-start.2
  47.4 51.9 %collective-permute-start.5 = (s32[1024]{0:T(1024)S(1)}, s32[1024]{0:T(1024)S(1)}, u32[]{:S(2)}, u32[]{:S(2)}) collective-permute-start(s32[1024]{0:T(1024)S(1)} %copy-done.60), channel_id=1, source_target_pairs={{0,4},{1,5},{2,6},{3,7},{4,0},{5,1},{6,2},{7,3},{8,12},{9,13},{10,... | collective-permute-start | bytes 12296 | tf_op jit(solution)/shard_map/ppermute | solution.py:241
  48.1 161.2 %collective-permute-start.11 = (bf16[2048,1024]{1,0:T(8,128)(2,1)}, bf16[2048,1024]{1,0:T(8,128)(2,1)}, u32[]{:S(2)}, u32[]{:S(2)}) collective-permute-start(bf16[2048,1024]{1,0:T(8,128)(2,1)} %param.23), channel_id=1, source_target_pairs={{0,4},{1,5},{2,6},{3,7},{4,0},{5,1},{6,2},{7,3},{8,12},{9,13},{10,... | collective-permute-start | bytes 12582920 | tf_op jit(solution)/shard_map/ppermute | solution.py:241
  48.6 188.1 %collective-permute-start.21 = (bf16[256,1024]{1,0:T(8,128)(2,1)}, bf16[256,1024]{1,0:T(8,128)(2,1)}, u32[]{:S(2)}, u32[]{:S(2)}) collective-permute-start(bf16[256,1024]{1,0:T(8,128)(2,1)} %param.43), channel_id=1, source_target_pairs={{2,4},{3,5},{4,2},{5,3},{10,12},{11,13},{12,10},{13,11},{18,20},{1... | collective-permute-start | bytes 1572872 | tf_op jit(solution)/shard_map/ppermute | solution.py:241
  76.4 110.6 %copy-start.15 = (bf16[256,1024]{1,0:T(8,128)(2,1)}, bf16[256,1024]{1,0:T(8,128)(2,1)S(1)}, u32[]{:S(2)}) copy-start(bf16[256,1024]{1,0:T(8,128)(2,1)S(1)} %get-tuple-element.156) | copy-start | bytes 1572868
  76.4 18.7 %collective-permute-start.1 = (bf16[256,1024]{1,0:T(8,128)(2,1)S(1)}, bf16[256,1024]{1,0:T(8,128)(2,1)S(1)}, u32[]{:S(2)}, u32[]{:S(2)}) collective-permute-start(bf16[256,1024]{1,0:T(8,128)(2,1)S(1)} %get-tuple-element.156), channel_id=1, source_target_pairs={{0,1},{1,0},{2,3},{3,2},{4,5},{5,4},{6,7},{7,6},{8,9},{9,8},{10,11... | collective-permute-start | bytes 1572872 | tf_op jit(solution)/shard_map/ppermute | solution.py:241
  97.5 3.0 collective-permute-start.3
  98.8 351.3 %reduce-scatter.10.cloned.1.call-start = ((), (), s32[]{:S(2)}) async-start(), calls=%async_computation.11 | async-start | bytes 1966080 | tf_op jit(solution)/shard_map/reduce_scatter | solution.py:292
  118.3 68.8 %collective-permute-start.8 = (bf16[512,256]{1,0:T(8,128)(2,1)}, bf16[512,256]{1,0:T(8,128)(2,1)}, u32[]{:S(2)}, u32[]{:S(2)}) collective-permute-start(bf16[512,256]{1,0:T(8,128)(2,1)} %get-tuple-element.189), channel_id=1, source_target_pairs={{0,5},{1,4},{2,7},{3,6},{4,1},{5,0},{6,3},{7,2},{8,13},{9,12},{10,... | collective-permute-start | bytes 786440 | tf_op jit(solution)/shard_map/ppermute | solution.py:241
  118.3 68.8 %collective-permute-start.6 = (bf16[512,256]{1,0:T(8,128)(2,1)}, bf16[512,256]{1,0:T(8,128)(2,1)}, u32[]{:S(2)}, u32[]{:S(2)}) collective-permute-start(bf16[512,256]{1,0:T(8,128)(2,1)} %get-tuple-element.189), channel_id=1, source_target_pairs={{0,4},{1,5},{2,6},{3,7},{4,0},{5,1},{6,2},{7,3},{8,12},{9,13},{10,... | collective-permute-start | bytes 786440 | tf_op jit(solution)/shard_map/ppermute | solution.py:241
  118.4 68.6 %collective-permute-start.7 = (bf16[512,256]{1,0:T(8,128)(2,1)S(1)}, bf16[512,256]{1,0:T(8,128)(2,1)}, u32[]{:S(2)}, u32[]{:S(2)}) collective-permute-start(bf16[512,256]{1,0:T(8,128)(2,1)S(1)} %get-tuple-element.188), channel_id=1, source_target_pairs={{0,1},{1,0},{2,3},{3,2},{4,5},{5,4},{6,7},{7,6},{8,9},{9,8},{10,11... | collective-permute-start | bytes 786440 | tf_op jit(solution)/shard_map/ppermute | solution.py:241
  191.9 22.5 %collective-permute-start.10 = (bf16[512,1024]{1,0:T(8,128)(2,1)}, bf16[512,1024]{1,0:T(8,128)(2,1)}, u32[]{:S(2)}, u32[]{:S(2)}) collective-permute-start(bf16[512,1024]{1,0:T(8,128)(2,1)} %add_convert_fusion.4), channel_id=1, source_target_pairs={{0,4},{1,5},{2,6},{3,7},{4,0},{5,1},{6,2},{7,3},{8,12},{9,13},{10,... | collective-permute-start | bytes 3145736 | tf_op jit(solution)/shard_map/ppermute | solution.py:241
  234.8 37.8 %collective-permute-start.15 = (bf16[512,256]{1,0:T(8,128)(2,1)}, bf16[512,256]{1,0:T(8,128)(2,1)}, u32[]{:S(2)}, u32[]{:S(2)}) collective-permute-start(bf16[512,256]{1,0:T(8,128)(2,1)} %get-tuple-element.187), channel_id=1, source_target_pairs={{0,5},{1,4},{2,7},{3,6},{4,1},{5,0},{6,3},{7,2},{8,13},{9,12},{10,... | collective-permute-start | bytes 786440 | tf_op jit(solution)/shard_map/ppermute | solution.py:241
  235.8 36.7 %collective-permute-start.13 = (bf16[512,256]{1,0:T(8,128)(2,1)}, bf16[512,256]{1,0:T(8,128)(2,1)}, u32[]{:S(2)}, u32[]{:S(2)}) collective-permute-start(bf16[512,256]{1,0:T(8,128)(2,1)} %get-tuple-element.187), channel_id=1, source_target_pairs={{0,4},{1,5},{2,6},{3,7},{4,0},{5,1},{6,2},{7,3},{8,12},{9,13},{10,... | collective-permute-start | bytes 786440 | tf_op jit(solution)/shard_map/ppermute | solution.py:241
  236.4 36.2 %collective-permute-start.14 = (bf16[512,256]{1,0:T(8,128)(2,1)S(1)}, bf16[512,256]{1,0:T(8,128)(2,1)}, u32[]{:S(2)}, u32[]{:S(2)}) collective-permute-start(bf16[512,256]{1,0:T(8,128)(2,1)S(1)} %get-tuple-element.186), channel_id=1, source_target_pairs={{0,1},{1,0},{2,3},{3,2},{4,5},{5,4},{6,7},{7,6},{8,9},{9,8},{10,11... | collective-permute-start | bytes 786440 | tf_op jit(solution)/shard_map/ppermute | solution.py:241
  237.7 41.3 %collective-permute-start.22 = (bf16[256,1024]{1,0:T(8,128)(2,1)S(1)}, bf16[256,1024]{1,0:T(8,128)(2,1)}, u32[]{:S(2)}, u32[]{:S(2)}) collective-permute-start(bf16[256,1024]{1,0:T(8,128)(2,1)S(1)} %broadcast_select_fusion.12), channel_id=1, source_target_pairs={{0,1},{1,0},{2,3},{3,2},{4,5},{5,4},{6,7},{7,6},{8,9},{9,8},{10,11... | collective-permute-start | bytes 1572872 | tf_op jit(solution)/shard_map/ppermute | solution.py:241
  278.7 33.1 %collective-permute-start.16 = (bf16[512,1024]{1,0:T(8,128)(2,1)}, bf16[512,1024]{1,0:T(8,128)(2,1)}, u32[]{:S(2)}, u32[]{:S(2)}) collective-permute-start(bf16[512,1024]{1,0:T(8,128)(2,1)} %add_convert_fusion.3), channel_id=1, source_target_pairs={{0,4},{1,5},{2,6},{3,7},{4,0},{5,1},{6,2},{7,3},{8,12},{9,13},{10,... | collective-permute-start | bytes 3145736 | tf_op jit(solution)/shard_map/ppermute | solution.py:241
  281.7 36.2 %collective-permute-start.23 = (bf16[512,1024]{1,0:T(8,128)(2,1)}, bf16[512,1024]{1,0:T(8,128)(2,1)}, u32[]{:S(2)}, u32[]{:S(2)}) collective-permute-start(bf16[512,1024]{1,0:T(8,128)(2,1)} %maximum_select_fusion.7), channel_id=1, source_target_pairs={{0,4},{1,5},{2,6},{3,7},{4,0},{5,1},{6,2},{7,3},{8,12},{9,13},{10,... | collective-permute-start | bytes 3145736 | tf_op jit(solution)/shard_map/ppermute | solution.py:241
  328.6 2.7 collective-permute-start.24
  331.8 24.6 %collective-permute-start.25 = (bf16[512,1024]{1,0:T(8,128)(2,1)S(1)}, bf16[512,1024]{1,0:T(8,128)(2,1)S(1)}, u32[]{:S(2)}, u32[]{:S(2)}) collective-permute-start(bf16[512,1024]{1,0:T(8,128)(2,1)S(1)} %add_convert_fusion.2), channel_id=1, source_target_pairs={{0,1},{1,0},{2,3},{3,2},{4,5},{5,4},{6,7},{7,6},{8,9},{9,8},{10,11... | collective-permute-start | bytes 3145736 | tf_op jit(solution)/shard_map/ppermute | solution.py:241
  361.5 3.4 collective-permute-start.26
  386.2 14.2 %collective-permute-start.29 = (bf16[512,256]{1,0:T(8,128)(2,1)}, bf16[512,256]{1,0:T(8,128)(2,1)}, u32[]{:S(2)}, u32[]{:S(2)}) collective-permute-start(bf16[512,256]{1,0:T(8,128)(2,1)} %get-tuple-element.185), channel_id=1, source_target_pairs={{0,5},{1,4},{2,7},{3,6},{4,1},{5,0},{6,3},{7,2},{8,13},{9,12},{10,... | collective-permute-start | bytes 786440 | tf_op jit(solution)/shard_map/ppermute | solution.py:241
  387.7 12.7 %collective-permute-start.27 = (bf16[512,256]{1,0:T(8,128)(2,1)}, bf16[512,256]{1,0:T(8,128)(2,1)}, u32[]{:S(2)}, u32[]{:S(2)}) collective-permute-start(bf16[512,256]{1,0:T(8,128)(2,1)} %get-tuple-element.185), channel_id=1, source_target_pairs={{0,4},{1,5},{2,6},{3,7},{4,0},{5,1},{6,2},{7,3},{8,12},{9,13},{10,... | collective-permute-start | bytes 786440 | tf_op jit(solution)/shard_map/ppermute | solution.py:241
  387.8 12.6 %collective-permute-start.28 = (bf16[512,256]{1,0:T(8,128)(2,1)S(1)}, bf16[512,256]{1,0:T(8,128)(2,1)}, u32[]{:S(2)}, u32[]{:S(2)}) collective-permute-start(bf16[512,256]{1,0:T(8,128)(2,1)S(1)} %get-tuple-element.184), channel_id=1, source_target_pairs={{0,1},{1,0},{2,3},{3,2},{4,5},{5,4},{6,7},{7,6},{8,9},{9,8},{10,11... | collective-permute-start | bytes 786440 | tf_op jit(solution)/shard_map/ppermute | solution.py:241
  400.1 71.3 %reduce-scatter.6.cloned.1.call-start = ((), (), s32[]{:S(2)}) async-start(), calls=%async_computation.8 | async-start | bytes 1966080 | tf_op jit(solution)/shard_map/reduce_scatter | solution.py:292
  407.1 2.9 collective-permute-start.30
  431.9 95.2 %reduce-scatter.14.cloned.1.call-start = ((), (), s32[]{:S(2)}) async-start(), calls=%async_computation.14 | async-start | bytes 5242880 | tf_op jit(solution)/shard_map/reduce_scatter | solution.py:292
  445.5 150.4 %reduce-scatter.12.cloned.1.call-start = ((), (), s32[]{:S(2)}) async-start(), calls=%async_computation.13 | async-start | bytes 655360 | tf_op jit(solution)/shard_map/reduce_scatter | solution.py:292
  450.1 162.5 %reduce-scatter.8.cloned.1.call-start = ((), (), s32[]{:S(2)}) async-start(), calls=%async_computation.10 | async-start | bytes 655360 | tf_op jit(solution)/shard_map/reduce_scatter | solution.py:292
  450.1 6.5 collective-permute-start.41
  455.5 271.6 %all-gather.21.cloned.1.call-start = ((), (), s32[]{:S(2)}) async-start(), calls=%async_computation.12 | async-start | bytes 1769472 | tf_op jit(solution)/shard_map/all_gather | solution.py:299
  456.8 11.0 %collective-permute-start.42 = (bf16[128,768]{1,0:T(8,128)(2,1)S(1)}, bf16[128,768]{1,0:T(8,128)(2,1)S(1)}, u32[]{:S(2)}, u32[]{:S(2)}) collective-permute-start(bf16[128,768]{1,0:T(8,128)(2,1)S(1)} %constant_dynamic-slice_fusion.1), channel_id=1, source_target_pairs={{0,4},{1,5},{6,2},{7,3},{8,12},{9,13},{14,10},{15,11},{16,20},{17,... | collective-permute-start | bytes 589832 | tf_op jit(solution)/shard_map/ppermute | solution.py:241
  468.5 261.8 %all-gather.19.cloned.1.call-start = ((), (), s32[]{:S(2)}) async-start(), calls=%async_computation.9 | async-start | bytes 1769472 | tf_op jit(solution)/shard_map/all_gather | solution.py:299
  471.5 9.1 %collective-permute-start.37 = (bf16[256,768]{1,0:T(8,128)(2,1)}, bf16[256,768]{1,0:T(8,128)(2,1)S(1)}, u32[]{:S(2)}, u32[]{:S(2)}) collective-permute-start(bf16[256,768]{1,0:T(8,128)(2,1)} %reduce-scatter.6.cloned.1.call-done), channel_id=1, source_target_pairs={{2,0},{3,1},{4,6},{5,7},{10,8},{11,9},{12,14},{13,15},{18,16},{19,... | collective-permute-start | bytes 1179656 | tf_op jit(solution)/shard_map/ppermute | solution.py:241
  481.8 8.7 %collective-permute-start.38 = (bf16[128,768]{1,0:T(8,128)(2,1)S(1)}, bf16[128,768]{1,0:T(8,128)(2,1)S(1)}, u32[]{:S(2)}, u32[]{:S(2)}) collective-permute-start(bf16[128,768]{1,0:T(8,128)(2,1)S(1)} %constant_dynamic-slice_fusion.3), channel_id=1, source_target_pairs={{0,4},{1,5},{6,2},{7,3},{8,12},{9,13},{14,10},{15,11},{16,20},{17,... | collective-permute-start | bytes 589832 | tf_op jit(solution)/shard_map/ppermute | solution.py:241
  491.2 242.2 %all-gather.23.cloned.1.call-start = ((), (), s32[]{:S(2)}) async-start(), calls=%async_computation.15 | async-start | bytes 4718592 | tf_op jit(solution)/shard_map/all_gather | solution.py:299
  527.1 16.1 %collective-permute-start.45 = (bf16[256,2048]{0,1:T(8,128)(2,1)}, bf16[256,2048]{0,1:T(8,128)(2,1)S(1)}, u32[]{:S(2)}, u32[]{:S(2)}) collective-permute-start(bf16[256,2048]{0,1:T(8,128)(2,1)} %reduce-scatter.14.cloned.1.call-done), channel_id=1, source_target_pairs={{2,0},{3,1},{4,6},{5,7},{10,8},{11,9},{12,14},{13,15},{18,16},{19,... | collective-permute-start | bytes 3145736 | tf_op jit(solution)/shard_map/ppermute | solution.py:241
  536.9 8.2 %collective-permute-start.18 = (bf16[512,1024]{1,0:T(8,128)(2,1)S(1)}, bf16[512,1024]{1,0:T(8,128)(2,1)S(1)}, u32[]{:S(2)}, u32[]{:S(2)}) collective-permute-start(bf16[512,1024]{1,0:T(8,128)(2,1)S(1)} %dynamic-slice_convert_fusion.4), channel_id=1, source_target_pairs={{0,4},{1,5},{2,6},{3,7},{4,0},{5,1},{6,2},{7,3},{8,12},{9,13},{10,... | collective-permute-start | bytes 3145736 | tf_op jit(solution)/shard_map/ppermute | solution.py:241
  543.6 16.3 %collective-permute-start.46 = (bf16[128,2048]{0,1:T(8,128)(2,1)S(1)}, bf16[128,2048]{0,1:T(8,128)(2,1)S(1)}, u32[]{:S(2)}, u32[]{:S(2)}) collective-permute-start(bf16[128,2048]{0,1:T(8,128)(2,1)S(1)} %constant_dynamic-slice_fusion.7), channel_id=1, source_target_pairs={{0,4},{1,5},{6,2},{7,3},{8,12},{9,13},{14,10},{15,11},{16,20},{17,... | collective-permute-start | bytes 1572872 | tf_op jit(solution)/shard_map/ppermute | solution.py:241
  546.9 22.5 %collective-permute-start.19 = (bf16[256,1024]{1,0:T(8,128)(2,1)S(1)}, bf16[256,1024]{1,0:T(8,128)(2,1)}, u32[]{:S(2)}, u32[]{:S(2)}) collective-permute-start(bf16[256,1024]{1,0:T(8,128)(2,1)S(1)} %dynamic-slice_convert_fusion.6), channel_id=1, source_target_pairs={{0,1},{1,0},{2,3},{3,2},{4,5},{5,4},{6,7},{7,6},{8,9},{9,8},{10,11... | collective-permute-start | bytes 1572872 | tf_op jit(solution)/shard_map/ppermute | solution.py:241
  571.0 19.0 %collective-permute-start.20 = (bf16[256,1024]{1,0:T(8,128)(2,1)S(1)}, bf16[256,1024]{1,0:T(8,128)(2,1)S(1)}, u32[]{:S(2)}, u32[]{:S(2)}) collective-permute-start(bf16[256,1024]{1,0:T(8,128)(2,1)S(1)} %add_convert_fusion.5), channel_id=1, source_target_pairs={{2,4},{3,5},{4,2},{5,3},{10,12},{11,13},{12,10},{13,11},{18,20},{1... | collective-permute-start | bytes 1572872 | tf_op jit(solution)/shard_map/ppermute | solution.py:241
  587.7 14.8 %collective-permute-start.34 = (bf16[1024,1024]{1,0:T(8,128)(2,1)S(1)}, bf16[1024,1024]{1,0:T(8,128)(2,1)}, u32[]{:S(2)}, u32[]{:S(2)}) collective-permute-start(bf16[1024,1024]{1,0:T(8,128)(2,1)S(1)} %dynamic-slice_convert_fusion), channel_id=1, source_target_pairs={{0,4},{1,5},{2,6},{3,7},{4,0},{5,1},{6,2},{7,3},{8,12},{9,13},{10,... | collective-permute-start | bytes 6291464 | tf_op jit(solution)/shard_map/ppermute | solution.py:241
  595.9 10.5 %collective-permute-start.31 = (bf16[512,1024]{1,0:T(8,128)(2,1)}, bf16[512,1024]{1,0:T(8,128)(2,1)}, u32[]{:S(2)}, u32[]{:S(2)}) collective-permute-start(bf16[512,1024]{1,0:T(8,128)(2,1)} %dynamic-slice_convert_fusion.2), channel_id=1, source_target_pairs={{0,4},{1,5},{2,6},{3,7},{4,0},{5,1},{6,2},{7,3},{8,12},{9,13},{10,... | collective-permute-start | bytes 3145736 | tf_op jit(solution)/shard_map/ppermute | solution.py:241
  595.9 4.1 collective-permute-start.43
  601.0 16.6 %collective-permute-start.44 = (bf16[32,1024]{1,0:T(8,128)(2,1)S(1)}, bf16[32,1024]{1,0:T(8,128)(2,1)S(1)}, u32[]{:S(2)}, u32[]{:S(2)}) collective-permute-start(bf16[32,1024]{1,0:T(8,128)(2,1)S(1)} %constant_dynamic-slice_fusion), channel_id=1, source_target_pairs={{0,4},{1,5},{6,2},{7,3},{8,12},{9,13},{14,10},{15,11},{16,20},{17,... | collective-permute-start | bytes 196616 | tf_op jit(solution)/shard_map/ppermute | solution.py:241
  608.8 38.8 %collective-permute-start.32 = (bf16[256,1024]{1,0:T(8,128)(2,1)S(1)}, bf16[256,1024]{1,0:T(8,128)(2,1)}, u32[]{:S(2)}, u32[]{:S(2)}) collective-permute-start(bf16[256,1024]{1,0:T(8,128)(2,1)S(1)} %dynamic-slice_convert_fusion.5), channel_id=1, source_target_pairs={{0,1},{1,0},{2,3},{3,2},{4,5},{5,4},{6,7},{7,6},{8,9},{9,8},{10,11... | collective-permute-start | bytes 1572872 | tf_op jit(solution)/shard_map/ppermute | solution.py:241
  612.5 36.8 %collective-permute-start.35 = (bf16[512,1024]{1,0:T(8,128)(2,1)}, bf16[512,1024]{1,0:T(8,128)(2,1)}, u32[]{:S(2)}, u32[]{:S(2)}) collective-permute-start(bf16[512,1024]{1,0:T(8,128)(2,1)} %dynamic-slice_convert_fusion.1), channel_id=1, source_target_pairs={{0,1},{1,0},{2,3},{3,2},{4,5},{5,4},{6,7},{7,6},{8,9},{9,8},{10,11... | collective-permute-start | bytes 3145736 | tf_op jit(solution)/shard_map/ppermute | solution.py:241
  612.6 34.1 %collective-permute-start.39 = (bf16[64,1024]{1,0:T(8,128)(2,1)}, bf16[64,1024]{1,0:T(8,128)(2,1)S(1)}, u32[]{:S(2)}, u32[]{:S(2)}) collective-permute-start(bf16[64,1024]{1,0:T(8,128)(2,1)} %reduce-scatter.8.cloned.1.call-done), channel_id=1, source_target_pairs={{2,0},{3,1},{4,6},{5,7},{10,8},{11,9},{12,14},{13,15},{18,16},{19,... | collective-permute-start | bytes 393224 | tf_op jit(solution)/shard_map/ppermute | solution.py:241
  651.9 73.0 %collective-permute-start.36 = (bf16[512,1024]{1,0:T(8,128)(2,1)S(1)}, bf16[512,1024]{1,0:T(8,128)(2,1)}, u32[]{:S(2)}, u32[]{:S(2)}) collective-permute-start(bf16[512,1024]{1,0:T(8,128)(2,1)S(1)} %add_convert_fusion.1), channel_id=1, source_target_pairs={{2,4},{3,5},{4,2},{5,3},{10,12},{11,13},{12,10},{13,11},{18,20},{1... | collective-permute-start | bytes 3145736 | tf_op jit(solution)/shard_map/ppermute | solution.py:241
  654.5 69.5 %collective-permute-start.33 = (bf16[256,1024]{1,0:T(8,128)(2,1)S(1)}, bf16[256,1024]{1,0:T(8,128)(2,1)S(1)}, u32[]{:S(2)}, u32[]{:S(2)}) collective-permute-start(bf16[256,1024]{1,0:T(8,128)(2,1)S(1)} %fusion.63), channel_id=1, source_target_pairs={{2,4},{3,5},{4,2},{5,3},{10,12},{11,13},{12,10},{13,11},{18,20},{1... | collective-permute-start | bytes 1572872 | tf_op jit(solution)/shard_map/ppermute | solution.py:241
  658.8 14.9 %collective-permute-start.40 = (bf16[32,1024]{1,0:T(8,128)(2,1)S(1)}, bf16[32,1024]{1,0:T(8,128)(2,1)S(1)}, u32[]{:S(2)}, u32[]{:S(2)}) collective-permute-start(bf16[32,1024]{1,0:T(8,128)(2,1)S(1)} %constant_dynamic-slice_fusion.2), channel_id=1, source_target_pairs={{0,4},{1,5},{6,2},{7,3},{8,12},{9,13},{14,10},{15,11},{16,20},{17,... | collective-permute-start | bytes 196616 | tf_op jit(solution)/shard_map/ppermute | solution.py:241
  (67 other events, 474.3 us)
Sparse Core Ops, SparseCore 0:
  26.1 29.8 all-gather.12
  59.5 66.3 all-gather.24
  129.4 55.1 all-gather.26
  186.9 22.3 all-gather.14
  212.7 57.8 all-gather.28
  272.9 36.2 all-gather.16
  400.3 37.1 reduce-scatter.9
  440.5 30.9 reduce-scatter.5
  474.4 52.6 reduce-scatter.13
  530.6 24.6 reduce-scatter.11
  558.7 24.7 reduce-scatter.7
  586.0 26.2 all-gather.20
  614.9 25.6 all-gather.18
  642.5 39.7 all-gather.22

commit v3 on v2

--- a/solution.py
+++ b/solution.py
@@ -104,6 +104,7 @@
         in_specs=[sm,sm,vm,vm,vm,vm,vm],out_specs=(vm,vm),
         scratch_shapes=[pltpu.VMEM((bq,width),F32)],
         compiler_params=pltpu.CompilerParams(vmem_limit_bytes=40<<20),
+        cost_estimate=pl.CostEstimate(flops=22_000_000_000, bytes_accessed=8_000_000, transcendentals=0),
         name="attend_fwd",
     )(lo,hi,q,k,v,rseg,kseg)
 
@@ -168,6 +169,7 @@
         in_specs=[sm,sm]+[vm]*8,out_specs=(vm,vm,vm),
         scratch_shapes=[pltpu.VMEM((keys,width),F32),pltpu.VMEM((keys,width),F32),pltpu.VMEM((heads*bq,width),BF),pltpu.VMEM((heads*bq,width),BF),pltpu.VMEM((bq,width),F32)],
         compiler_params=pltpu.CompilerParams(vmem_limit_bytes=40<<20),
+        cost_estimate=pl.CostEstimate(flops=30_000_000_000, bytes_accessed=8_000_000, transcendentals=0),
         name="attend_bwd",
     )(lo,hi,q,k,v,o,do,lse,rseg,kseg)
 
@@ -287,16 +289,184 @@
         every = every.reshape((self.dp, self.tensor) + piece.shape)
         return jnp.swapaxes(every, 0, 1).reshape((self.tensor,) + weight.shape)
 
-    def sum_weight(self, grad):
-        groups = [[d for d in range(self.dp) if d % 2 == c] for c in range(2)]
-        piece = lax.psum_scatter(
-            grad.astype(jnp.bfloat16), "dp", scatter_dimension=0, axis_index_groups=groups, tiled=True
+
+def sum_kernel(dp, shapes, units, *refs):
+    count = len(shapes)
+    ins, outs = refs[:count], refs[count : 2 * count]
+    rest = refs[2 * count :]
+    bits = [b for b in (2, 4, 8, 16, 32, 64) if b < dp]
+    steps = len(bits)
+    per = steps + 1
+    land = [rest[u * 2 * per : u * 2 * per + per] for u in range(len(units))]
+    hold = [rest[u * 2 * per + per : (u + 1) * 2 * per] for u in range(len(units))]
+    send_sem, recv_sem = rest[len(units) * 2 * per :]
+    d, t = lax.axis_index("dp"), lax.axis_index("tensor")
+    keeper = (d % 2) == (t // 2)
+    MESH = pl.DeviceIdType.MESH
+
+    barrier = pltpu.get_barrier_semaphore()
+    around = [(d ^ b, t) for b in bits] + [(d, t ^ 2), (d ^ 1, t)]
+    for device in around:
+        pl.semaphore_signal(barrier, inc=1, device_id=device, device_id_type=MESH)
+    pl.semaphore_wait(barrier, len(around))
+
+    def my(bit):
+        return (d // bit) % 2
+
+    def order(u):
+        return bits if units[u][3] == 0 else bits[::-1]
+
+    def source(u, step):
+        array, first, rows, _ = units[u]
+        return (ins[array], first) if step == 0 else (hold[u][step - 1], 0)
+
+    def copy(u, stage, src, dst, device):
+        return pltpu.make_async_remote_copy(
+            src_ref=src, dst_ref=dst, send_sem=send_sem.at[u, stage], recv_sem=recv_sem.at[u, stage],
+            device_id=device, device_id_type=MESH,
         )
-        total = piece.astype(jnp.float32) + self.swap(piece, 0, 2, False).astype(jnp.float32)
-        total = total.astype(jnp.bfloat16)
-        near, far = self.part(total, self.core, 2), self.part(total, 1 - self.core, 2)
-        piece = jnp.where(self.keeper, near, self.swap(far, 1, 0, True))
-        return lax.all_gather(piece, "dp", axis=0, tiled=True).astype(jnp.float32)
+
+    def quarter(u):
+        array, first, rows, _ = units[u]
+        place = first
+        for step, bit in enumerate(order(u)):
+            place = place + my(bit) * (rows >> (step + 1))
+        return place
+
+    def scatter_copy(u, step):
+        ref, first = source(u, step)
+        size = units[u][2] >> (step + 1)
+        bit = order(u)[step]
+        start = pl.multiple_of(first + (1 - my(bit)) * size, 16)
+        return copy(u, step, ref.at[pl.ds(start, size)], land[u][step], (d ^ bit, t))
+
+    def plane_copy(u):
+        ref, first = source(u, steps)
+        return copy(u, steps, ref, land[u][steps], (d, t ^ 2))
+
+    def gather_copy(u, step):
+        array, first, rows, _ = units[u]
+        bit = order(u)[steps - 1 - step]
+        size = rows >> (steps - step)
+        start = quarter(u)
+        for back in range(step):
+            done = order(u)[steps - 1 - back]
+            start = start - my(done) * (rows >> (steps - back))
+        block = outs[array].at[pl.ds(pl.multiple_of(start, 16), size)]
+        return copy(u, steps + 1 + step, block, block, (d ^ bit, t))
+
+    def core_copy(u):
+        array, first, rows, _ = units[u]
+        block = outs[array].at[pl.ds(first, rows)]
+        return copy(u, 2 * steps + 1, block, block, (d ^ 1, t))
+
+    def add(dst, dst_first, left, left_first, right, rows):
+        chunk = min(rows, 32)
+
+        def body(i, _):
+            at = i * chunk
+            a = left[pl.ds(pl.multiple_of(left_first + at, 16), chunk), :].astype(jnp.float32)
+            b = right[pl.ds(pl.multiple_of(at, 16), chunk), :].astype(jnp.float32)
+            dst[pl.ds(pl.multiple_of(dst_first + at, 16), chunk), :] = (a + b).astype(jnp.bfloat16)
+            return 0
+
+        lax.fori_loop(0, rows // chunk, body, 0)
+
+    def begin(u, stage):
+        if stage < steps:
+            scatter_copy(u, stage).start()
+        elif stage == steps:
+
+            @pl.when(jnp.logical_not(keeper))
+            def _():
+                plane_copy(u).start()
+        else:
+
+            @pl.when(keeper)
+            def _():
+                (gather_copy(u, stage - steps - 1) if stage <= 2 * steps else core_copy(u)).start()
+
+    def end(u, stage):
+        array, first, rows, _ = units[u]
+        if stage < steps:
+            one = scatter_copy(u, stage)
+            one.wait_recv()
+            ref, row = source(u, stage)
+            size = rows >> (stage + 1)
+            add(hold[u][stage], 0, ref, row + my(order(u)[stage]) * size, land[u][stage], size)
+            one.wait_send()
+        elif stage == steps:
+
+            @pl.when(jnp.logical_not(keeper))
+            def _():
+                plane_copy(u).wait_send()
+
+            @pl.when(keeper)
+            def _():
+                plane_copy(u).wait_recv()
+                ref, row = source(u, steps)
+                add(outs[array], quarter(u), ref, row, land[u][steps], rows >> steps)
+        elif stage <= 2 * steps:
+
+            @pl.when(keeper)
+            def _():
+                gather_copy(u, stage - steps - 1).wait()
+        else:
+
+            @pl.when(keeper)
+            def _():
+                core_copy(u).wait_send()
+
+            @pl.when(jnp.logical_not(keeper))
+            def _():
+                core_copy(u).wait_recv()
+
+    last = 2 * steps + 2
+    wave = sorted({u // 2 for u in range(len(units))})
+    for tick in range(len(wave) + last):
+        for stage in reversed(range(last + 1)):
+            pair = tick - stage
+            if 0 <= pair < len(wave):
+                for u in (2 * pair, 2 * pair + 1):
+                    if stage > 0:
+                        end(u, stage - 1)
+                    if stage < last:
+                        begin(u, stage)
+
+
+def sum_weights(grads, split, collective_id):
+    dp = lax.axis_size("dp")
+    shapes = [grad.shape for grad in grads]
+    units = []
+    for pair in range(len(grads) // 2):
+        rows = shapes[2 * pair][0] // split[pair]
+        for part in range(split[pair]):
+            for side in range(2):
+                units.append((2 * pair + side, part * rows, rows, side))
+    steps = 0
+    while 2 << steps < dp:
+        steps += 1
+    scratch = []
+    for array, first, rows, side in units:
+        width = shapes[array][1]
+        sizes = [rows >> (k + 1) for k in range(steps)] + [rows >> steps]
+        scratch += [pltpu.VMEM((size, width), jnp.bfloat16) for size in sizes]
+        scratch += [pltpu.VMEM((size, width), jnp.bfloat16) for size in sizes]
+    stages = 2 * steps + 2
+    vmem = pl.BlockSpec(memory_space=pltpu.VMEM)
+    return pl.pallas_call(
+        functools.partial(sum_kernel, dp, shapes, units),
+        out_shape=[jax.ShapeDtypeStruct(shape, jnp.bfloat16) for shape in shapes],
+        in_specs=[vmem] * len(grads),
+        out_specs=[vmem] * len(grads),
+        scratch_shapes=scratch
+        + [pltpu.SemaphoreType.DMA((len(units), stages)), pltpu.SemaphoreType.DMA((len(units), stages))],
+        compiler_params=pltpu.CompilerParams(
+            collective_id=collective_id, has_side_effects=True, vmem_limit_bytes=56 << 20
+        ),
+        cost_estimate=pl.CostEstimate(flops=100_000_000_000, bytes_accessed=16_000_000, transcendentals=0),
+        name="sum_weights",
+    )(*grads)
 
 
 def on_device(
@@ -440,18 +610,28 @@
     )
     tokens_grad = place.home((quarter_of(grad_res) + back_rows).astype(jnp.bfloat16))
 
-    ff_grad = place.sum_weight(jnp.concatenate([expand_grad, reduce_grad.T], axis=1))
-    expand_grad, reduce_grad = ff_grad[:, :hidden_width], ff_grad[:, hidden_width:].T
-    cross_grads = place.sum_weight(jnp.concatenate([cross_grad, cross_query_grad], axis=1))
+    bf16 = jnp.bfloat16
+    sums = sum_weights(
+        [
+            expand_grad.astype(bf16),
+            reduce_grad.astype(bf16),
+            jnp.concatenate([cross_grad, cross_query_grad], axis=1).astype(bf16),
+            causal_grad.astype(bf16),
+            cross_out_grad.astype(bf16),
+            causal_out_grad.astype(bf16),
+        ],
+        (2, 1, 1),
+        0,
+    )
+    expand_grad, reduce_grad, cross_grads, causal_grads, cross_out_grad, causal_out_grad = (
+        value.astype(jnp.float32) for value in sums
+    )
     cross_key_grad, cross_value_grad, cross_query_grad = (
         cross_grads[:, i * width : (i + 1) * width] for i in range(3)
     )
-    causal_grads = place.sum_weight(causal_grad)
     causal_query_grad, causal_key_grad, causal_value_grad = (
         causal_grads[:, i * width : (i + 1) * width] for i in range(3)
     )
-    cross_out_grad = place.sum_weight(cross_out_grad)
-    causal_out_grad = place.sum_weight(causal_out_grad)
     once = (place.side == 0).astype(jnp.float32)
     (
         first_gain_grad,

time: 761 us -> 694 us (0.912)
  Pallas kernels: 58 us -> 194 us
  waiting for transfers between devices: 330 us -> 216 us
  starting transfers between devices: 81.2 us -> 48.2 us
  blocking collectives: 61.7 us -> 43.9 us
  local copies, waits for them, and re-layouts: 66.6 us -> 50.2 us
  matrix products: 88 us -> 74.2 us
  other arithmetic: 54 us -> 45.5 us
    pallas_call x0 -> x1, Pallas kernels: none -> 139 us  [sum_weights(): pl.pallas_call(functools.partial(sum_kernel, dp, shapes, units), out_shap...]
    ppermute x47 -> x37, waiting for transfers between devices: 155 us -> 76.8 us  [swap(): return lax.ppermute(value, ('dp', 'tensor'), pairs)]
    reduce_scatter x5 -> x0, waiting for transfers between devices: 38.8 us -> none  [sum_weight(): lax.psum_scatter(grad.astype(jnp.bfloat16), 'dp', scatter_dimension=0, ax...]
    ppermute x47 -> x37, starting transfers between devices: 80.1 us -> 48 us  [swap(): return lax.ppermute(value, ('dp', 'tensor'), pairs)]
    all_gather x2 -> x0, blocking collectives: 22.2 us -> none  [sum_weight(): return lax.all_gather(piece, 'dp', axis=0, tiled=True).astype(jnp.float32)]
    dot_general x7, matrix products: 26.5 us -> 16.8 us  [against(): lax.dot_general(left, weight, (((1,), (1,)), ((), ())), preferred_element...]
    unnamed x148 -> x163, local copies, waits for them, and re-layouts: 29.8 us -> 22.8 us
  transfers between devices with their start and end apart: 61 -> 43, of which waited for: 27 -> 14; matrix products, arithmetic and copies ran while one was open for 20% -> 21% of each run, Pallas kernels for 5% -> 25%
where the time goes in v3:
time: 694 us; the launch traced here: 688 us
  waiting for transfers between devices  216 us (31%)
  Pallas kernels  194 us (28%)
  matrix products  74.2 us (11%)
  local copies, waits for them, and re-layouts  50.2 us (7%)
  starting transfers between devices  48.2 us (7%)
  other arithmetic  45.5 us (7%)
  blocking collectives  43.9 us (6%)
  between operations  15.8 us (2%)
    pallas_call x1, Pallas kernels, sum_weights(): pl.pallas_call(functools.partial(sum_kernel, dp, shapes, units), out_shap...  139 us
    all_gather x3, waiting for transfers between devices, whole_weight(): every = lax.all_gather(piece, ('dp', 'tensor'), axis=0, tiled=False)  94.2 us
    ppermute x37, waiting for transfers between devices, swap(): return lax.ppermute(value, ('dp', 'tensor'), pairs)  76.8 us
    ppermute x37, starting transfers between devices, swap(): return lax.ppermute(value, ('dp', 'tensor'), pairs)  48 us
    all_gather x3, waiting for transfers between devices, moved_weight(): lax.all_gather(piece, 'dp', axis=0, tiled=True)  45.1 us
    psum x1, blocking collectives, on_device(): lax.psum((first_gain_grad, first_shift_grad, second_gain_grad * once, sec...  43.9 us
    pallas_call x2, Pallas kernels, attend_bwd(): pl.pallas_call(functools.partial(bwd_kernel, causal, heads, bq, bk), out_...  30.8 us
    dot_general x7, matrix products, along_rows(): lax.dot_general(left, right, (((0,), (0,)), ((), ())), preferred_element_...  29.6 us
  transfers between devices with their start and end apart: 43, of which 14 were waited for; matrix products, arithmetic and copies ran while one was open for 21% of the time, Pallas kernels for 25%

profile of v3, /device:TPU:1, one launch (start us, length us, event | category | flops | bytes accessed | tf_op | source)
XLA Modules:
  0.0 687.7 jit_solution(18436281086125835609)
XLA Ops:
  7.3 2.1 constant_dynamic-update-slice_fusion.2
  9.3 2.0 constant_dynamic-update-slice_fusion.1
  13.2 3.2 collective-permute-start.4
  16.4 8.8 %collective-permute-done.4 = bf16[128,768]{1,0:T(8,128)(2,1)S(1)} collective-permute-done((bf16[128,768]{1,0:T(8,128)(2,1)S(1)}, bf16[128,768]{1,0:T(8,128)(2,1)S(1)}, u32[]{:S(2)}, u32[]{:S(2)}) %collective-permute-start.4) | collective-permute-done | bytes 196640 | tf_op jit(solution)/shard_map/ppermute | solution.py:243
  28.5 4.7 collective-permute-done.12
  33.9 3.3 constant_dynamic-update-slice_fusion.6
  38.8 1.9 constant_dynamic-slice_fusion.2
  40.6 5.1 collective-permute-start.9
  45.9 4.8 collective-permute-start
  53.3 25.5 %collective-permute-done = bf16[256,1024]{1,0:T(8,128)(2,1)S(1)} collective-permute-done((bf16[256,1024]{1,0:T(8,128)(2,1)S(1)}, bf16[256,1024]{1,0:T(8,128)(2,1)S(1)}, u32[]{:S(2)}, u32[]{:S(2)}) %collective-permute-start) | collective-permute-done | bytes 524320 | tf_op jit(solution)/shard_map/ppermute | solution.py:243
  79.3 8.0 %collective-permute-done.1 = bf16[256,1024]{1,0:T(8,128)(2,1)S(1)} collective-permute-done((bf16[256,1024]{1,0:T(8,128)(2,1)S(1)}, bf16[256,1024]{1,0:T(8,128)(2,1)S(1)}, u32[]{:S(2)}, u32[]{:S(2)}) %collective-permute-start.1) | collective-permute-done | bytes 524320 | tf_op jit(solution)/shard_map/ppermute | solution.py:243
  90.5 2.2 collective-permute-done.3
  92.7 4.5 convolution_convert_fusion.4
  97.4 9.3 %attend_fwd.2 = (bf16[1024,256]{1,0:T(8,128)(2,1)S(1)}, f32[8,1024]{1,0:T(8,128)S(1)}) custom-call(s32[4]{0:T(128)S(1)} %get-tuple-element.113.lo_ref, s32[4]{0:T(128)S(1)} %get-tuple-element.112.hi_ref, bf16[1024,256]{1,0:T(8,128)(2,1)S(1)} %get-tuple-element.100.q_ref, bf16[1024,256]{1,0:T(8,128)(2,1)S(1)} %get-tuple-element.99.k_ref, ...), custom_call_target="tpu_custom_call" | custom-call | flops 22000001024 | bytes 8000000 | tf_op jit(solution)/shard_map/attend_fwd/pallas_call | solution.py:102
  109.5 7.2 %collective-permute-start.21 = (bf16[256,1024]{1,0:T(8,128)(2,1)}, bf16[256,1024]{1,0:T(8,128)(2,1)}, u32[]{:S(2)}, u32[]{:S(2)}) collective-permute-start(bf16[256,1024]{1,0:T(8,128)(2,1)} %param.43), channel_id=1, source_target_pairs={{2,4},{3,5},{4,2},{5,3},{10,12},{11,13},{12,10},{13,11},{18,20},{1... | collective-permute-start | bytes 1572872 | tf_op jit(solution)/shard_map/ppermute | solution.py:243
  116.7 10.5 %all-gather.16.cloned.1.call-done = bf16[1024,1024]{1,0:T(8,128)(2,1)} async-done(((bf16[32,1024]{1,0:T(8,128)(2,1)}), bf16[1024,1024]{1,0:T(8,128)(2,1)}) %all-gather.16.cloned.1.call-update) | async-done | bytes 2097168 | tf_op jit(solution)/shard_map/all_gather | solution.py:288
  127.2 1.8 copy.84
  129.2 2.4 collective-permute-done.7
  131.6 3.7 fusion.115
  135.3 51.3 %all-gather.18.cloned.1.call-done = bf16[4096,256]{1,0:T(8,128)(2,1)} async-done(((bf16[128,256]{1,0:T(8,128)(2,1)}), bf16[4096,256]{1,0:T(8,128)(2,1)}) %all-gather.18.cloned.1.call-update) | async-done | bytes 2097168 | tf_op jit(solution)/shard_map/all_gather | solution.py:288
  186.6 1.9 copy.85
  192.3 19.0 %all-gather.12.cloned.1.call-done = bf16[1024,512]{1,0:T(8,128)(2,1)} async-done(((bf16[128,512]{1,0:T(8,128)(2,1)}), bf16[1024,512]{1,0:T(8,128)(2,1)}) %all-gather.12.cloned.1.call-update) | async-done | bytes 1048592 | tf_op jit(solution)/shard_map/all_gather | solution.py:284
  211.3 4.9 convolution_convert_fusion
  217.2 2.9 convolution_convert_fusion.10.q_ref
  220.1 15.0 %attend_fwd.3 = (bf16[1024,256]{1,0:T(8,128)(2,1)S(1)}, f32[8,1024]{1,0:T(8,128)S(1)}) custom-call(s32[4]{0:T(128)S(1)} %and_select_fusion.1.lo_ref, s32[4]{0:T(128)S(1)} %and_select_fusion.hi_ref, bf16[1024,256]{1,0:T(8,128)(2,1)S(1)} %convolution_convert_fusion.10.q_ref, bf16[2048,256]{1,0:T(8,128)(2,1)S(1)} %get-tuple-element.83.k_ref, ...), custom_call_target="tpu_custom_call" | custom-call | flops 22000001024 | bytes 8000000 | tf_op jit(solution)/shard_map/attend_fwd/pallas_call | solution.py:102
  240.2 32.4 %all-gather.20.cloned.1.call-done = bf16[1024,1024]{1,0:T(8,128)(2,1)} async-done(((bf16[32,1024]{1,0:T(8,128)(2,1)}), bf16[1024,1024]{1,0:T(8,128)(2,1)}) %all-gather.20.cloned.1.call-update) | async-done | bytes 2097168 | tf_op jit(solution)/shard_map/all_gather | solution.py:288
  272.6 1.8 copy.87
  276.1 2.5 fusion.116
  281.0 2.7 maximum_select_fusion.7
  284.0 26.1 %all-gather.14.cloned.1.call-done = bf16[1024,2048]{1,0:T(8,128)(2,1)} async-done(((bf16[128,2048]{1,0:T(8,128)(2,1)}), bf16[1024,2048]{1,0:T(8,128)(2,1)}) %all-gather.14.cloned.1.call-update) | async-done | bytes 4194320 | tf_op jit(solution)/shard_map/all_gather | solution.py:284
  310.1 2.6 broadcast_select_fusion
  312.8 4.6 fusion.44
  317.4 4.7 fusion.40
  322.0 2.7 dynamic-slice_convert_fusion.4
  325.0 6.7 fusion.6
  331.7 2.6 fusion.42
  334.3 2.0 copy-done.28
  339.9 2.4 convert_add_fusion.4
  346.2 6.8 convolution_convert_fusion.1.refs_1_
  353.0 2.7 collective-permute-done.19
  355.9 5.7 collective-permute-start.20
  361.6 22.1 %collective-permute-done.25 = bf16[512,1024]{1,0:T(8,128)(2,1)S(1)} collective-permute-done((bf16[512,1024]{1,0:T(8,128)(2,1)S(1)}, bf16[512,1024]{1,0:T(8,128)(2,1)S(1)}, u32[]{:S(2)}, u32[]{:S(2)}) %collective-permute-start.25) | collective-permute-done | bytes 1048608 | tf_op jit(solution)/shard_map/ppermute | solution.py:243
  384.9 2.3 fusion.110
  388.4 6.1 convolution_convert_fusion.2.refs_0_
  397.9 19.7 %attend_bwd.2 = (bf16[1024,256]{1,0:T(8,128)(2,1)S(1)}, bf16[2048,256]{1,0:T(8,128)(2,1)S(1)}, bf16[2048,256]{1,0:T(8,128)(2,1)S(1)}) custom-call(s32[4]{0:T(128)S(1)} %and_select_fusion.1.lo_ref, s32[4]{0:T(128)S(1)} %and_select_fusion.hi_ref, bf16[1024,256]{1,0:T(8,128)(2,1)S(1)} %copy-done.15, bf16[2048,256]{1,0:T(8,128)(2,1)S(1)} %get-tuple-element.83.k_ref, ...), custom_call_target="tpu_custom_call" | custom-call | flops 30000001024 | bytes 8000000 | tf_op jit(solution)/shard_map/attend_bwd/pallas_call | solution.py:167
  417.9 1.8 collective-permute-start.28
  421.2 2.4 fusion.88
  425.8 4.9 fusion.53
  431.0 1.7 multiply_reduce_fusion.1
  432.8 2.1 fusion.109
  435.9 3.2 convolution_convert_fusion.7
  445.5 11.1 %attend_bwd.3 = (bf16[1024,256]{1,0:T(8,128)(2,1)S(1)}, bf16[1024,256]{1,0:T(8,128)(2,1)S(1)}, bf16[1024,256]{1,0:T(8,128)(2,1)S(1)}) custom-call(s32[4]{0:T(128)S(1)} %copy-done.13, s32[4]{0:T(128)S(1)} %copy-done.11, bf16[1024,256]{1,0:T(8,128)(2,1)S(1)} %copy-done.9, bf16[1024,256]{1,0:T(8,128)(2,1)S(1)} %copy-done.7, bf16[1024,256]{1,0:T(8,128)(2,1)S(1)} %copy-done.5, ...), custom_call_target="tpu_custom_call" | custom-call | flops 30000001024 | bytes 8000000 | tf_op jit(solution)/shard_map/attend_bwd/pallas_call | solution.py:167
  458.4 1.8 fusion.87
  463.1 5.5 convolution_convert_fusion.3.refs_3_
  472.4 138.7 %sum_weights.1 = (bf16[1024,1024]{1,0:T(8,128)(2,1)}, bf16[1024,1024]{1,0:T(8,128)(2,1)}, bf16[1024,768]{1,0:T(8,128)(2,1)}, bf16[1024,768]{1,0:T(8,128)(2,1)}, ...) custom-call(bf16[1024,1024]{1,0:T(8,128)(2,1)} %convolution_convert_fusion.2.refs_0_, ...), custom_call_target="tpu_custom_call" | custom-call | flops 99999997952 | bytes 16000000 | tf_op jit(solution)/shard_map/sum_weights/pallas_call | solution.py:457
  611.1 2.3 convert_element_type.202
  613.4 2.1 convert_element_type.205
  615.5 2.5 convert_element_type.206
  618.0 2.5 convert_element_type.207
  622.6 2.1 collective-permute-start.36
  625.1 4.5 collective-permute-start.33
  629.7 1.7 fusion.113
  633.8 43.9 %all-reduce = (f32[1024]{0:T(1024)}, f32[1024]{0:T(1024)}, f32[1024]{0:T(1024)}, f32[1024]{0:T(1024)}, f32[1024]{0:T(1024)}, /*index=5*/f32[1024]{0:T(1024)}) all-reduce(f32[1024]{0:T(1024)S(1)} %get-tuple-element.59, f32[1024]{0:T(1024)S(1)} %get-tuple-element.62, ...), channel_id=1, replica_groups=mesh['dp'=8,'tensor'=4] {'dp','tensor'}, use_global_device_ids=true, to_apply=%region_22.23 | all-reduce | flops 6144 | bytes 49152 | tf_op jit(solution)/shard_map/psum | solution.py:643
  677.7 1.9 broadcast_select_fusion.11
  (319 shorter events, 70.4 us)
Async XLA Ops:
  7.2 18.8 %copy-start = (bf16[256,1024]{1,0:T(8,128)(2,1)S(1)}, bf16[256,1024]{1,0:T(8,128)(2,1)}, u32[]{:S(2)}) copy-start(bf16[256,1024]{1,0:T(8,128)(2,1)} %param.32) | copy-start | bytes 1572868
  7.2 21.1 %copy-start.36 = (bf16[1024,256]{1,0:T(8,128)(2,1)S(1)}, bf16[1024,256]{1,0:T(8,128)(2,1)}, u32[]{:S(2)}) copy-start(bf16[1024,256]{1,0:T(8,128)(2,1)} %param.36) | copy-start | bytes 1572868
  7.2 85.5 %all-gather.10.cloned.1.call-start = ((), (), s32[]{:S(2)}) async-start(), calls=%async_computation | async-start | bytes 1769472 | tf_op jit(solution)/shard_map/all_gather | solution.py:284
  9.3 19.0 %copy-start.37 = (bf16[1024,256]{1,0:T(8,128)(2,1)S(1)}, bf16[1024,256]{1,0:T(8,128)(2,1)}, u32[]{:S(2)}) copy-start(bf16[1024,256]{1,0:T(8,128)(2,1)} %param.37) | copy-start | bytes 1572868
  13.2 12.0 %collective-permute-start.4 = (bf16[128,768]{1,0:T(8,128)(2,1)S(1)}, bf16[128,768]{1,0:T(8,128)(2,1)S(1)}, u32[]{:S(2)}, u32[]{:S(2)}) collective-permute-start(bf16[128,768]{1,0:T(8,128)(2,1)S(1)} %constant_dynamic-slice_fusion.11), channel_id=1, source_target_pairs={{0,2},{1,3},{2,0},{3,1},{4,6},{5,7},{6,4},{7,5},{8,10},{9,11},{10,... | collective-permute-start | bytes 589832 | tf_op jit(solution)/shard_map/ppermute | solution.py:243
  25.9 101.3 %all-gather.16.cloned.1.call-start = ((), (), s32[]{:S(2)}) async-start(), calls=%async_computation.3 | async-start | bytes 2162688 | tf_op jit(solution)/shard_map/all_gather | solution.py:288
  26.7 159.9 %all-gather.18.cloned.1.call-start = ((), (), s32[]{:S(2)}) async-start(), calls=%async_computation.4 | async-start | bytes 2162688 | tf_op jit(solution)/shard_map/all_gather | solution.py:288
  28.2 183.1 %all-gather.12.cloned.1.call-start = ((), (), s32[]{:S(2)}) async-start(), calls=%async_computation.1 | async-start | bytes 1179648 | tf_op jit(solution)/shard_map/all_gather | solution.py:284
  28.4 182.9 %copy-start.26 = (bf16[1024,512]{1,0:T(8,128)(2,1)}, bf16[1024,512]{1,0:T(8,128)(2,1)S(1)}, u32[]{:S(2)}) copy-start(bf16[1024,512]{1,0:T(8,128)(2,1)S(1)} %constant_dynamic-update-slice_fusion.3) | copy-start | bytes 3145732
  28.4 4.8 collective-permute-start.12
  33.9 238.7 %all-gather.20.cloned.1.call-start = ((), (), s32[]{:S(2)}) async-start(), calls=%async_computation.5 | async-start | bytes 2162688 | tf_op jit(solution)/shard_map/all_gather | solution.py:288
  37.2 8.5 %copy-start.66 = (s32[1,4]{1,0:T(1,128)S(1)}, s32[1,4]{1,0:T(1,128)}, u32[]{:S(2)}) copy-start(s32[1,4]{1,0:T(1,128)} %param.24) | copy-start | bytes 52
  37.2 8.6 %copy-start.34 = (bf16[256,1024]{1,0:T(8,128)(2,1)S(1)}, bf16[256,1024]{1,0:T(8,128)(2,1)}, u32[]{:S(2)}) copy-start(bf16[256,1024]{1,0:T(8,128)(2,1)} %param.22) | copy-start | bytes 1572868
  37.2 13.4 %copy-start.65 = (s32[1024]{0:T(1024)S(1)}, s32[1024]{0:T(1024)}, u32[]{:S(2)}) copy-start(s32[1024]{0:T(1024)} %param.26) | copy-start | bytes 12292
  40.6 47.5 %copy-start.52 = (f32[1024]{0:T(1024)S(1)}, f32[1024]{0:T(1024)}, u32[]{:S(2)}) copy-start(f32[1024]{0:T(1024)} %param.27) | copy-start | bytes 12292
  40.6 47.5 %copy-start.62 = (f32[1024]{0:T(1024)S(1)}, f32[1024]{0:T(1024)}, u32[]{:S(2)}) copy-start(f32[1024]{0:T(1024)} %param.28) | copy-start | bytes 12292
  40.6 68.9 %collective-permute-start.17 = (bf16[128,2048]{1,0:T(8,128)(2,1)}, bf16[128,2048]{1,0:T(8,128)(2,1)}, u32[]{:S(2)}, u32[]{:S(2)}) collective-permute-start(bf16[128,2048]{1,0:T(8,128)(2,1)} %constant_dynamic-slice_fusion.2), channel_id=1, source_target_pairs={{0,2},{1,3},{2,0},{3,1},{4,6},{5,7},{6,4},{7,5},{8,10},{9,11},{10,... | collective-permute-start | bytes 1572872 | tf_op jit(solution)/shard_map/ppermute | solution.py:243
  40.6 11.7 %collective-permute-start.9 = (s32[1,4]{1,0:T(1,128)S(1)}, s32[1,4]{1,0:T(1,128)S(1)}, u32[]{:S(2)}, u32[]{:S(2)}) collective-permute-start(s32[1,4]{1,0:T(1,128)S(1)} %copy-done.67), channel_id=1, source_target_pairs={{0,4},{1,5},{2,6},{3,7},{4,0},{5,1},{6,2},{7,3},{8,12},{9,13},{10,... | collective-permute-start | bytes 56 | tf_op jit(solution)/shard_map/ppermute | solution.py:243
  45.8 7.3 %collective-permute-start.2 = (s32[1,4]{1,0:T(1,128)S(1)}, s32[1,4]{1,0:T(1,128)S(1)}, u32[]{:S(2)}, u32[]{:S(2)}) collective-permute-start(s32[1,4]{1,0:T(1,128)S(1)} %copy-done.66), channel_id=1, source_target_pairs={{0,4},{1,5},{2,6},{3,7},{4,0},{5,1},{6,2},{7,3},{8,12},{9,13},{10,... | collective-permute-start | bytes 56 | tf_op jit(solution)/shard_map/ppermute | solution.py:243
  45.9 32.9 %collective-permute-start = (bf16[256,1024]{1,0:T(8,128)(2,1)S(1)}, bf16[256,1024]{1,0:T(8,128)(2,1)S(1)}, u32[]{:S(2)}, u32[]{:S(2)}) collective-permute-start(bf16[256,1024]{1,0:T(8,128)(2,1)S(1)} %copy-done.34), channel_id=1, source_target_pairs={{2,4},{3,5},{4,2},{5,3},{10,12},{11,13},{12,10},{13,11},{18,20},{1... | collective-permute-start | bytes 1572872 | tf_op jit(solution)/shard_map/ppermute | solution.py:243
  50.7 39.8 %collective-permute-start.5 = (s32[1024]{0:T(1024)S(1)}, s32[1024]{0:T(1024)S(1)}, u32[]{:S(2)}, u32[]{:S(2)}) collective-permute-start(s32[1024]{0:T(1024)S(1)} %copy-done.65), channel_id=1, source_target_pairs={{0,4},{1,5},{2,6},{3,7},{4,0},{5,1},{6,2},{7,3},{8,12},{9,13},{10,... | collective-permute-start | bytes 12296 | tf_op jit(solution)/shard_map/ppermute | solution.py:243
  52.3 257.9 %all-gather.14.cloned.1.call-start = ((), (), s32[]{:S(2)}) async-start(), calls=%async_computation.2 | async-start | bytes 4718592 | tf_op jit(solution)/shard_map/all_gather | solution.py:284
  52.4 158.9 %collective-permute-start.11 = (bf16[2048,1024]{1,0:T(8,128)(2,1)}, bf16[2048,1024]{1,0:T(8,128)(2,1)}, u32[]{:S(2)}, u32[]{:S(2)}) collective-permute-start(bf16[2048,1024]{1,0:T(8,128)(2,1)} %param.23), channel_id=1, source_target_pairs={{0,4},{1,5},{2,6},{3,7},{4,0},{5,1},{6,2},{7,3},{8,12},{9,13},{10,... | collective-permute-start | bytes 12582920 | tf_op jit(solution)/shard_map/ppermute | solution.py:243
  79.0 52.5 %copy-start.18 = (bf16[256,1024]{1,0:T(8,128)(2,1)}, bf16[256,1024]{1,0:T(8,128)(2,1)S(1)}, u32[]{:S(2)}) copy-start(bf16[256,1024]{1,0:T(8,128)(2,1)S(1)} %get-tuple-element.73) | copy-start | bytes 1572868
  79.0 8.3 %collective-permute-start.1 = (bf16[256,1024]{1,0:T(8,128)(2,1)S(1)}, bf16[256,1024]{1,0:T(8,128)(2,1)S(1)}, u32[]{:S(2)}, u32[]{:S(2)}) collective-permute-start(bf16[256,1024]{1,0:T(8,128)(2,1)S(1)} %get-tuple-element.73), channel_id=1, source_target_pairs={{0,1},{1,0},{2,3},{3,2},{4,5},{5,4},{6,7},{7,6},{8,9},{9,8},{10,11... | collective-permute-start | bytes 1572872 | tf_op jit(solution)/shard_map/ppermute | solution.py:243
  89.7 3.0 collective-permute-start.3
  90.2 7.2 %copy-start.10 = (s32[4]{0:T(128)}, s32[4]{0:T(128)S(1)}, u32[]{:S(2)}) copy-start(s32[4]{0:T(128)S(1)} %get-tuple-element.112.hi_ref) | copy-start | bytes 52
  90.2 7.2 %copy-start.12 = (s32[4]{0:T(128)}, s32[4]{0:T(128)S(1)}, u32[]{:S(2)}) copy-start(s32[4]{0:T(128)S(1)} %get-tuple-element.113.lo_ref) | copy-start | bytes 52
  97.3 9.3 %copy-start.4 = (bf16[1024,256]{1,0:T(8,128)(2,1)}, bf16[1024,256]{1,0:T(8,128)(2,1)S(1)}, u32[]{:S(2)}) copy-start(bf16[1024,256]{1,0:T(8,128)(2,1)S(1)} %get-tuple-element.98.v_ref) | copy-start | bytes 1572868
  97.3 9.3 %copy-start.6 = (bf16[1024,256]{1,0:T(8,128)(2,1)}, bf16[1024,256]{1,0:T(8,128)(2,1)S(1)}, u32[]{:S(2)}) copy-start(bf16[1024,256]{1,0:T(8,128)(2,1)S(1)} %get-tuple-element.99.k_ref) | copy-start | bytes 1572868
  97.3 9.3 %copy-start.8 = (bf16[1024,256]{1,0:T(8,128)(2,1)}, bf16[1024,256]{1,0:T(8,128)(2,1)S(1)}, u32[]{:S(2)}) copy-start(bf16[1024,256]{1,0:T(8,128)(2,1)S(1)} %get-tuple-element.100.q_ref) | copy-start | bytes 1572868
  107.5 21.6 %collective-permute-start.8 = (bf16[512,256]{1,0:T(8,128)(2,1)S(1)}, bf16[512,256]{1,0:T(8,128)(2,1)}, u32[]{:S(2)}, u32[]{:S(2)}) collective-permute-start(bf16[512,256]{1,0:T(8,128)(2,1)S(1)} %get-tuple-element.106), channel_id=1, source_target_pairs={{0,5},{1,4},{2,7},{3,6},{4,1},{5,0},{6,3},{7,2},{8,13},{9,12},{10,... | collective-permute-start | bytes 786440 | tf_op jit(solution)/shard_map/ppermute | solution.py:243
  107.6 24.0 %collective-permute-start.6 = (bf16[512,256]{1,0:T(8,128)(2,1)S(1)}, bf16[512,256]{1,0:T(8,128)(2,1)}, u32[]{:S(2)}, u32[]{:S(2)}) collective-permute-start(bf16[512,256]{1,0:T(8,128)(2,1)S(1)} %get-tuple-element.106), channel_id=1, source_target_pairs={{0,4},{1,5},{2,6},{3,7},{4,0},{5,1},{6,2},{7,3},{8,12},{9,13},{10,... | collective-permute-start | bytes 786440 | tf_op jit(solution)/shard_map/ppermute | solution.py:243
  107.9 23.7 %collective-permute-start.7 = (bf16[512,256]{1,0:T(8,128)(2,1)S(1)}, bf16[512,256]{1,0:T(8,128)(2,1)}, u32[]{:S(2)}, u32[]{:S(2)}) collective-permute-start(bf16[512,256]{1,0:T(8,128)(2,1)S(1)} %get-tuple-element.105), channel_id=1, source_target_pairs={{0,1},{1,0},{2,3},{3,2},{4,5},{5,4},{6,7},{7,6},{8,9},{9,8},{10,11... | collective-permute-start | bytes 786440 | tf_op jit(solution)/shard_map/ppermute | solution.py:243
  109.5 128.3 %collective-permute-start.21 = (bf16[256,1024]{1,0:T(8,128)(2,1)}, bf16[256,1024]{1,0:T(8,128)(2,1)}, u32[]{:S(2)}, u32[]{:S(2)}) collective-permute-start(bf16[256,1024]{1,0:T(8,128)(2,1)} %param.43), channel_id=1, source_target_pairs={{2,4},{3,5},{4,2},{5,3},{10,12},{11,13},{12,10},{13,11},{18,20},{1... | collective-permute-start | bytes 1572872 | tf_op jit(solution)/shard_map/ppermute | solution.py:243
  190.6 25.7 %collective-permute-start.10 = (bf16[512,1024]{1,0:T(8,128)(2,1)}, bf16[512,1024]{1,0:T(8,128)(2,1)}, u32[]{:S(2)}, u32[]{:S(2)}) collective-permute-start(bf16[512,1024]{1,0:T(8,128)(2,1)} %add_convert_fusion.3), channel_id=1, source_target_pairs={{0,4},{1,5},{2,6},{3,7},{4,0},{5,1},{6,2},{7,3},{8,12},{9,13},{10,... | collective-permute-start | bytes 3145736 | tf_op jit(solution)/shard_map/ppermute | solution.py:243
  220.1 15.0 %copy-start.14 = (bf16[1024,256]{1,0:T(8,128)(2,1)}, bf16[1024,256]{1,0:T(8,128)(2,1)S(1)}, u32[]{:S(2)}) copy-start(bf16[1024,256]{1,0:T(8,128)(2,1)S(1)} %convolution_convert_fusion.10.q_ref) | copy-start | bytes 1572868
  220.1 17.6 %copy-start.38 = (bf16[256,1024]{1,0:T(8,128)(2,1)S(1)}, bf16[256,1024]{1,0:T(8,128)(2,1)}, u32[]{:S(2)}) copy-start(bf16[256,1024]{1,0:T(8,128)(2,1)} %param.43) | copy-start | bytes 1572868
  235.9 38.6 %collective-permute-start.15 = (bf16[512,256]{1,0:T(8,128)(2,1)}, bf16[512,256]{1,0:T(8,128)(2,1)}, u32[]{:S(2)}, u32[]{:S(2)}) collective-permute-start(bf16[512,256]{1,0:T(8,128)(2,1)} %get-tuple-element.104), channel_id=1, source_target_pairs={{0,5},{1,4},{2,7},{3,6},{4,1},{5,0},{6,3},{7,2},{8,13},{9,12},{10,... | collective-permute-start | bytes 786440 | tf_op jit(solution)/shard_map/ppermute | solution.py:243
  236.9 37.6 %collective-permute-start.13 = (bf16[512,256]{1,0:T(8,128)(2,1)}, bf16[512,256]{1,0:T(8,128)(2,1)}, u32[]{:S(2)}, u32[]{:S(2)}) collective-permute-start(bf16[512,256]{1,0:T(8,128)(2,1)} %get-tuple-element.104), channel_id=1, source_target_pairs={{0,4},{1,5},{2,6},{3,7},{4,0},{5,1},{6,2},{7,3},{8,12},{9,13},{10,... | collective-permute-start | bytes 786440 | tf_op jit(solution)/shard_map/ppermute | solution.py:243
  237.5 37.1 %collective-permute-start.14 = (bf16[512,256]{1,0:T(8,128)(2,1)S(1)}, bf16[512,256]{1,0:T(8,128)(2,1)}, u32[]{:S(2)}, u32[]{:S(2)}) collective-permute-start(bf16[512,256]{1,0:T(8,128)(2,1)S(1)} %get-tuple-element.103), channel_id=1, source_target_pairs={{0,1},{1,0},{2,3},{3,2},{4,5},{5,4},{6,7},{7,6},{8,9},{9,8},{10,11... | collective-permute-start | bytes 786440 | tf_op jit(solution)/shard_map/ppermute | solution.py:243
  238.9 42.2 %collective-permute-start.22 = (bf16[256,1024]{1,0:T(8,128)(2,1)S(1)}, bf16[256,1024]{1,0:T(8,128)(2,1)}, u32[]{:S(2)}, u32[]{:S(2)}) collective-permute-start(bf16[256,1024]{1,0:T(8,128)(2,1)S(1)} %broadcast_select_fusion.12), channel_id=1, source_target_pairs={{0,1},{1,0},{2,3},{3,2},{4,5},{5,4},{6,7},{7,6},{8,9},{9,8},{10,11... | collective-permute-start | bytes 1572872 | tf_op jit(solution)/shard_map/ppermute | solution.py:243
  280.8 32.0 %collective-permute-start.16 = (bf16[512,1024]{1,0:T(8,128)(2,1)}, bf16[512,1024]{1,0:T(8,128)(2,1)}, u32[]{:S(2)}, u32[]{:S(2)}) collective-permute-start(bf16[512,1024]{1,0:T(8,128)(2,1)} %add_convert_fusion.2), channel_id=1, source_target_pairs={{0,4},{1,5},{2,6},{3,7},{4,0},{5,1},{6,2},{7,3},{8,12},{9,13},{10,... | collective-permute-start | bytes 3145736 | tf_op jit(solution)/shard_map/ppermute | solution.py:243
  283.7 41.3 %collective-permute-start.23 = (bf16[512,1024]{1,0:T(8,128)(2,1)}, bf16[512,1024]{1,0:T(8,128)(2,1)}, u32[]{:S(2)}, u32[]{:S(2)}) collective-permute-start(bf16[512,1024]{1,0:T(8,128)(2,1)} %maximum_select_fusion.7), channel_id=1, source_target_pairs={{0,4},{1,5},{2,6},{3,7},{4,0},{5,1},{6,2},{7,3},{8,12},{9,13},{10,... | collective-permute-start | bytes 3145736 | tf_op jit(solution)/shard_map/ppermute | solution.py:243
  317.4 7.6 %copy-start.76 = (f32[1024,1024]{1,0:T(8,128)}, f32[1024,1024]{1,0:T(8,128)S(1)}, u32[]{:S(2)}) copy-start(f32[1024,1024]{1,0:T(8,128)S(1)} %fusion.44) | copy-start | bytes 12582916
  324.8 15.1 %collective-permute-start.18 = (bf16[512,1024]{1,0:T(8,128)(2,1)}, bf16[512,1024]{1,0:T(8,128)(2,1)}, u32[]{:S(2)}, u32[]{:S(2)}) collective-permute-start(bf16[512,1024]{1,0:T(8,128)(2,1)} %dynamic-slice_convert_fusion.4), channel_id=1, source_target_pairs={{0,4},{1,5},{2,6},{3,7},{4,0},{5,1},{6,2},{7,3},{8,12},{9,13},{10,... | collective-permute-start | bytes 3145736 | tf_op jit(solution)/shard_map/ppermute | solution.py:243
  337.5 6.2 collective-permute-start.24
  342.3 13.3 %collective-permute-start.19 = (bf16[256,1024]{1,0:T(8,128)(2,1)S(1)}, bf16[256,1024]{1,0:T(8,128)(2,1)S(1)}, u32[]{:S(2)}, u32[]{:S(2)}) collective-permute-start(bf16[256,1024]{1,0:T(8,128)(2,1)S(1)} %dynamic-slice_convert_fusion.6), channel_id=1, source_target_pairs={{0,1},{1,0},{2,3},{3,2},{4,5},{5,4},{6,7},{7,6},{8,9},{9,8},{10,11... | collective-permute-start | bytes 1572872 | tf_op jit(solution)/shard_map/ppermute | solution.py:243
  345.3 10.4 %copy-start.17 = (f32[512,1024]{1,0:T(8,128)S(1)}, f32[512,1024]{1,0:T(8,128)}, u32[]{:S(2)}) copy-start(f32[512,1024]{1,0:T(8,128)} %copy-done.16) | copy-start | bytes 6291460
  345.3 38.5 %collective-permute-start.25 = (bf16[512,1024]{1,0:T(8,128)(2,1)S(1)}, bf16[512,1024]{1,0:T(8,128)(2,1)S(1)}, u32[]{:S(2)}, u32[]{:S(2)}) collective-permute-start(bf16[512,1024]{1,0:T(8,128)(2,1)S(1)} %add_convert_fusion.1), channel_id=1, source_target_pairs={{0,1},{1,0},{2,3},{3,2},{4,5},{5,4},{6,7},{7,6},{8,9},{9,8},{10,11... | collective-permute-start | bytes 3145736 | tf_op jit(solution)/shard_map/ppermute | solution.py:243
  355.9 39.7 %collective-permute-start.20 = (bf16[256,1024]{1,0:T(8,128)(2,1)S(1)}, bf16[256,1024]{1,0:T(8,128)(2,1)S(1)}, u32[]{:S(2)}, u32[]{:S(2)}) collective-permute-start(bf16[256,1024]{1,0:T(8,128)(2,1)S(1)} %add_convert_fusion.4), channel_id=1, source_target_pairs={{2,4},{3,5},{4,2},{5,3},{10,12},{11,13},{12,10},{13,11},{18,20},{1... | collective-permute-start | bytes 1572872 | tf_op jit(solution)/shard_map/ppermute | solution.py:243
  387.2 9.3 %copy-start.47 = (bf16[256,1024]{1,0:T(8,128)(2,1)S(1)}, bf16[256,1024]{1,0:T(8,128)(2,1)}, u32[]{:S(2)}) copy-start(bf16[256,1024]{1,0:T(8,128)(2,1)} %copy-done.46) | copy-start | bytes 1572868
  387.2 9.3 %collective-permute-start.26 = (bf16[512,1024]{1,0:T(8,128)(2,1)S(1)}, bf16[512,1024]{1,0:T(8,128)(2,1)S(1)}, u32[]{:S(2)}, u32[]{:S(2)}) collective-permute-start(bf16[512,1024]{1,0:T(8,128)(2,1)S(1)} %get-tuple-element.76), channel_id=1, source_target_pairs={{0,4},{1,5},{2,6},{3,7},{4,0},{5,1},{6,2},{7,3},{8,12},{9,13},{10,... | collective-permute-start | bytes 3145736 | tf_op jit(solution)/shard_map/ppermute | solution.py:243
  417.7 12.9 %collective-permute-start.29 = (bf16[512,256]{1,0:T(8,128)(2,1)S(1)}, bf16[512,256]{1,0:T(8,128)(2,1)S(1)}, u32[]{:S(2)}, u32[]{:S(2)}) collective-permute-start(bf16[512,256]{1,0:T(8,128)(2,1)S(1)} %get-tuple-element.102), channel_id=1, source_target_pairs={{0,5},{1,4},{2,7},{3,6},{4,1},{5,0},{6,3},{7,2},{8,13},{9,12},{10,... | collective-permute-start | bytes 786440 | tf_op jit(solution)/shard_map/ppermute | solution.py:243
  417.8 13.2 %collective-permute-start.27 = (bf16[512,256]{1,0:T(8,128)(2,1)S(1)}, bf16[512,256]{1,0:T(8,128)(2,1)S(1)}, u32[]{:S(2)}, u32[]{:S(2)}) collective-permute-start(bf16[512,256]{1,0:T(8,128)(2,1)S(1)} %get-tuple-element.102), channel_id=1, source_target_pairs={{0,4},{1,5},{2,6},{3,7},{4,0},{5,1},{6,2},{7,3},{8,12},{9,13},{10,... | collective-permute-start | bytes 786440 | tf_op jit(solution)/shard_map/ppermute | solution.py:243
  417.9 13.1 %collective-permute-start.28 = (bf16[512,256]{1,0:T(8,128)(2,1)S(1)}, bf16[512,256]{1,0:T(8,128)(2,1)S(1)}, u32[]{:S(2)}, u32[]{:S(2)}) collective-permute-start(bf16[512,256]{1,0:T(8,128)(2,1)S(1)} %get-tuple-element.101), channel_id=1, source_target_pairs={{0,1},{1,0},{2,3},{3,2},{4,5},{5,4},{6,7},{7,6},{8,9},{9,8},{10,11... | collective-permute-start | bytes 786440 | tf_op jit(solution)/shard_map/ppermute | solution.py:243
  424.0 44.6 %collective-permute-start.34 = (bf16[1024,1024]{1,0:T(8,128)(2,1)S(1)}, bf16[1024,1024]{1,0:T(8,128)(2,1)S(1)}, u32[]{:S(2)}, u32[]{:S(2)}) collective-permute-start(bf16[1024,1024]{1,0:T(8,128)(2,1)S(1)} %dynamic-slice_convert_fusion), channel_id=1, source_target_pairs={{0,4},{1,5},{2,6},{3,7},{4,0},{5,1},{6,2},{7,3},{8,12},{9,13},{10,... | collective-permute-start | bytes 6291464 | tf_op jit(solution)/shard_map/ppermute | solution.py:243
  434.9 8.7 %collective-permute-start.30 = (bf16[512,1024]{1,0:T(8,128)(2,1)S(1)}, bf16[512,1024]{1,0:T(8,128)(2,1)S(1)}, u32[]{:S(2)}, u32[]{:S(2)}) collective-permute-start(bf16[512,1024]{1,0:T(8,128)(2,1)S(1)} %get-tuple-element.74), channel_id=1, source_target_pairs={{0,4},{1,5},{2,6},{3,7},{4,0},{5,1},{6,2},{7,3},{8,12},{9,13},{10,... | collective-permute-start | bytes 3145736 | tf_op jit(solution)/shard_map/ppermute | solution.py:243
  460.5 10.1 %collective-permute-start.31 = (bf16[512,1024]{1,0:T(8,128)(2,1)S(1)}, bf16[512,1024]{1,0:T(8,128)(2,1)S(1)}, u32[]{:S(2)}, u32[]{:S(2)}) collective-permute-start(bf16[512,1024]{1,0:T(8,128)(2,1)S(1)} %dynamic-slice_convert_fusion.2), channel_id=1, source_target_pairs={{0,4},{1,5},{2,6},{3,7},{4,0},{5,1},{6,2},{7,3},{8,12},{9,13},{10,... | collective-permute-start | bytes 3145736 | tf_op jit(solution)/shard_map/ppermute | solution.py:243
  470.5 151.8 %collective-permute-start.35 = (bf16[512,1024]{1,0:T(8,128)(2,1)}, bf16[512,1024]{1,0:T(8,128)(2,1)S(1)}, u32[]{:S(2)}, u32[]{:S(2)}) collective-permute-start(bf16[512,1024]{1,0:T(8,128)(2,1)} %dynamic-slice_convert_fusion.1), channel_id=1, source_target_pairs={{0,1},{1,0},{2,3},{3,2},{4,5},{5,4},{6,7},{7,6},{8,9},{9,8},{10,11... | collective-permute-start | bytes 3145736 | tf_op jit(solution)/shard_map/ppermute | solution.py:243
  471.0 149.5 %collective-permute-start.32 = (bf16[256,1024]{1,0:T(8,128)(2,1)S(1)}, bf16[256,1024]{1,0:T(8,128)(2,1)}, u32[]{:S(2)}, u32[]{:S(2)}) collective-permute-start(bf16[256,1024]{1,0:T(8,128)(2,1)S(1)} %dynamic-slice_convert_fusion.5), channel_id=1, source_target_pairs={{0,1},{1,0},{2,3},{3,2},{4,5},{5,4},{6,7},{7,6},{8,9},{9,8},{10,11... | collective-permute-start | bytes 1572872 | tf_op jit(solution)/shard_map/ppermute | solution.py:243
  622.6 57.0 %collective-permute-start.36 = (bf16[512,1024]{1,0:T(8,128)(2,1)S(1)}, bf16[512,1024]{1,0:T(8,128)(2,1)S(1)}, u32[]{:S(2)}, u32[]{:S(2)}) collective-permute-start(bf16[512,1024]{1,0:T(8,128)(2,1)S(1)} %add_convert_fusion), channel_id=1, source_target_pairs={{2,4},{3,5},{4,2},{5,3},{10,12},{11,13},{12,10},{13,11},{18,20},{1... | collective-permute-start | bytes 3145736 | tf_op jit(solution)/shard_map/ppermute | solution.py:243
  625.1 52.6 %collective-permute-start.33 = (bf16[256,1024]{1,0:T(8,128)(2,1)S(1)}, bf16[256,1024]{1,0:T(8,128)(2,1)}, u32[]{:S(2)}, u32[]{:S(2)}) collective-permute-start(bf16[256,1024]{1,0:T(8,128)(2,1)S(1)} %fusion.63), channel_id=1, source_target_pairs={{2,4},{3,5},{4,2},{5,3},{10,12},{11,13},{12,10},{13,11},{18,20},{1... | collective-permute-start | bytes 1572872 | tf_op jit(solution)/shard_map/ppermute | solution.py:243
  633.8 46.9 %copy-start.1 = (bf16[256,1024]{1,0:T(8,128)(2,1)S(1)}, bf16[256,1024]{1,0:T(8,128)(2,1)}, u32[]{:S(2)}) copy-start(bf16[256,1024]{1,0:T(8,128)(2,1)} %param.32) | copy-start | bytes 1572868
  (57 other events, 148.2 us)
Sparse Core Ops, SparseCore 0:
  26.0 28.8 all-gather.9
  58.4 68.7 all-gather.15
  130.7 55.8 all-gather.17
  188.9 22.3 all-gather.11
  214.6 57.8 all-gather.19
  274.3 35.7 all-gather.13

commit v4 on v3

--- a/solution.py
+++ b/solution.py
@@ -290,25 +290,76 @@
         return jnp.swapaxes(every, 0, 1).reshape((self.tensor,) + weight.shape)
 
 
-def sum_kernel(dp, shapes, units, *refs):
-    count = len(shapes)
-    ins, outs = refs[:count], refs[count : 2 * count]
-    rest = refs[2 * count :]
+class Copies:
+    def __init__(self, send_sem, recv_sem):
+        self.send_sem, self.recv_sem, self.known = send_sem, recv_sem, {}
+
+    def __call__(self, name, src, dst, device):
+        at = self.known.setdefault(name, len(self.known))
+        return pltpu.make_async_remote_copy(
+            src_ref=src,
+            dst_ref=dst,
+            send_sem=self.send_sem.at[at],
+            recv_sem=self.recv_sem.at[at],
+            device_id=device,
+            device_id_type=pl.DeviceIdType.MESH,
+        )
+
+
+def greet(devices):
+    barrier = pltpu.get_barrier_semaphore()
+    for device in devices:
+        pl.semaphore_signal(
+            barrier, inc=1, device_id=device, device_id_type=pl.DeviceIdType.MESH
+        )
+    pl.semaphore_wait(barrier, len(devices))
+
+
+def rows_of(ref, start, size, step=16):
+    return ref.at[pl.ds(pl.multiple_of(start, step), size)]
+
+
+def norm_rows(src, src_first, dst, dst_first, rows, gain, shift):
+    chunk = 64
+
+    def body(i, _):
+        at = i * chunk
+        x = src[pl.ds(pl.multiple_of(src_first + at, 16), chunk), :].astype(jnp.float32)
+        unit, inverse = moments(x)
+        dst[pl.ds(pl.multiple_of(dst_first + at, 16), chunk), :] = (
+            unit * gain[...] + shift[...]
+        ).astype(jnp.bfloat16)
+        return 0
+
+    lax.fori_loop(0, rows // chunk, body, 0)
+
+
+def sum_kernel(dp, counts, units, spans, *refs):
+    arrays, row_arrays = counts
+    it = iter(refs)
+    take = lambda count: [next(it) for _ in range(count)]
+    ins, parts = take(arrays), take(row_arrays)
+    small_in, after, tokens, grad_in, gain = take(5)
+    outs, row_outs = take(arrays), take(row_arrays)
+    (small_out,) = take(1)
     bits = [b for b in (2, 4, 8, 16, 32, 64) if b < dp]
     steps = len(bits)
-    per = steps + 1
-    land = [rest[u * 2 * per : u * 2 * per + per] for u in range(len(units))]
-    hold = [rest[u * 2 * per + per : (u + 1) * 2 * per] for u in range(len(units))]
-    send_sem, recv_sem = rest[len(units) * 2 * per :]
+    land, hold = [], []
+    for unit in units:
+        own = 0 if unit[4] else steps
+        hold.append(take(own))
+        land.append(([None] * (steps - own)) + take(own + 1))
+    row_land = [take(2) for _ in range(row_arrays)]
+    row_hold = [take(2) for _ in range(row_arrays)]
+    small_hold, small_land, small_send, small_recv, row_send, row_recv, send_sem, recv_sem = take(8)
     d, t = lax.axis_index("dp"), lax.axis_index("tensor")
-    keeper = (d % 2) == (t // 2)
+    core, side = d % 2, t % 2
+    keeper = core == t // 2
+    other = jnp.logical_not(keeper)
     MESH = pl.DeviceIdType.MESH
 
-    barrier = pltpu.get_barrier_semaphore()
-    around = [(d ^ b, t) for b in bits] + [(d, t ^ 2), (d ^ 1, t)]
-    for device in around:
-        pl.semaphore_signal(barrier, inc=1, device_id=device, device_id_type=MESH)
-    pl.semaphore_wait(barrier, len(around))
+    around = [(d ^ b, t) for b in bits] + [(d ^ 1, t), (d, t ^ 2), (d, t ^ 1)]
+    greet(around + [(d ^ 1, t ^ 2)])
 
     def my(bit):
         return (d // bit) % 2
@@ -317,7 +368,9 @@
         return bits if units[u][3] == 0 else bits[::-1]
 
     def source(u, step):
-        array, first, rows, _ = units[u]
+        array, first, rows, _, summed = units[u]
+        if summed:
+            return ins[array], first >> steps
         return (ins[array], first) if step == 0 else (hold[u][step - 1], 0)
 
     def copy(u, stage, src, dst, device):
@@ -327,36 +380,33 @@
         )
 
     def quarter(u):
-        array, first, rows, _ = units[u]
-        place = first
+        place = units[u][1]
         for step, bit in enumerate(order(u)):
-            place = place + my(bit) * (rows >> (step + 1))
+            place = place + my(bit) * (units[u][2] >> (step + 1))
         return place
 
     def scatter_copy(u, step):
         ref, first = source(u, step)
         size = units[u][2] >> (step + 1)
         bit = order(u)[step]
-        start = pl.multiple_of(first + (1 - my(bit)) * size, 16)
-        return copy(u, step, ref.at[pl.ds(start, size)], land[u][step], (d ^ bit, t))
+        return copy(u, step, rows_of(ref, first + (1 - my(bit)) * size, size), land[u][step], (d ^ bit, t))
 
     def plane_copy(u):
         ref, first = source(u, steps)
-        return copy(u, steps, ref, land[u][steps], (d, t ^ 2))
+        return copy(u, steps, rows_of(ref, first, units[u][2] >> steps), land[u][steps], (d, t ^ 2))
 
     def gather_copy(u, step):
-        array, first, rows, _ = units[u]
+        array, first, rows = units[u][:3]
         bit = order(u)[steps - 1 - step]
         size = rows >> (steps - step)
         start = quarter(u)
         for back in range(step):
-            done = order(u)[steps - 1 - back]
-            start = start - my(done) * (rows >> (steps - back))
-        block = outs[array].at[pl.ds(pl.multiple_of(start, 16), size)]
+            start = start - my(order(u)[steps - 1 - back]) * (rows >> (steps - back))
+        block = rows_of(outs[array], start, size)
         return copy(u, steps + 1 + step, block, block, (d ^ bit, t))
 
     def core_copy(u):
-        array, first, rows, _ = units[u]
+        array, first, rows = units[u][:3]
         block = outs[array].at[pl.ds(first, rows)]
         return copy(u, 2 * steps + 1, block, block, (d ^ 1, t))
 
@@ -374,10 +424,11 @@
 
     def begin(u, stage):
         if stage < steps:
-            scatter_copy(u, stage).start()
+            if not units[u][4]:
+                scatter_copy(u, stage).start()
         elif stage == steps:
 
-            @pl.when(jnp.logical_not(keeper))
+            @pl.when(other)
             def _():
                 plane_copy(u).start()
         else:
@@ -387,17 +438,18 @@
                 (gather_copy(u, stage - steps - 1) if stage <= 2 * steps else core_copy(u)).start()
 
     def end(u, stage):
-        array, first, rows, _ = units[u]
+        array, first, rows = units[u][:3]
         if stage < steps:
-            one = scatter_copy(u, stage)
-            one.wait_recv()
-            ref, row = source(u, stage)
-            size = rows >> (stage + 1)
-            add(hold[u][stage], 0, ref, row + my(order(u)[stage]) * size, land[u][stage], size)
-            one.wait_send()
+            if not units[u][4]:
+                one = scatter_copy(u, stage)
+                one.wait_recv()
+                ref, row = source(u, stage)
+                size = rows >> (stage + 1)
+                add(hold[u][stage], 0, ref, row + my(order(u)[stage]) * size, land[u][stage], size)
+                one.wait_send()
         elif stage == steps:
 
-            @pl.when(jnp.logical_not(keeper))
+            @pl.when(other)
             def _():
                 plane_copy(u).wait_send()
 
@@ -417,56 +469,738 @@
             def _():
                 core_copy(u).wait_send()
 
-            @pl.when(jnp.logical_not(keeper))
+            @pl.when(other)
             def _():
                 core_copy(u).wait_recv()
 
+    def row_copy(a, stage):
+        size = spans[a]
+        if stage == 0:
+            src, dst, device = rows_of(parts[a], (1 - core) * 2 * size, 2 * size), row_land[a][0], (d ^ 1, t)
+        elif stage == 1:
+            src, dst, device = rows_of(row_hold[a][0], (1 - side) * size, size), row_land[a][1], (d, t ^ 1)
+        else:
+            src, dst, device = row_hold[a][1], row_outs[a], (d ^ 1, t ^ 2)
+        return pltpu.make_async_remote_copy(
+            src_ref=src, dst_ref=dst, send_sem=row_send.at[a, stage], recv_sem=row_recv.at[a, stage],
+            device_id=device, device_id_type=MESH,
+        )
+
+    def row_quarter(a):
+        size = spans[a]
+
+        def body(i, _):
+            at = pl.ds(pl.multiple_of(i * 32, 32), 32)
+            total = row_hold[a][0][pl.ds(pl.multiple_of(side * size + i * 32, 32), 32), :].astype(jnp.float32)
+            total = total + row_land[a][1][at, :].astype(jnp.float32)
+            if a == 1:
+                total = total + after[at, :]
+            elif a == 2:
+                unit, inverse = moments(tokens[at, :].astype(jnp.float32))
+                total = grad_in[at, :] + normalize_back(total, unit, inverse, gain[...])[0]
+            row_hold[a][1][at, :] = total.astype(jnp.bfloat16)
+            return 0
+
+        lax.fori_loop(0, size // 32, body, 0)
+
+    def row_end(a, stage):
+        if stage == 0:
+            row_copy(a, 0).wait()
+            add(row_hold[a][0], 0, parts[a], core * 2 * spans[a], row_land[a][0], 2 * spans[a])
+            row_copy(a, 1).start()
+        elif stage == 1:
+            row_copy(a, 1).wait()
+            row_quarter(a)
+
+            @pl.when(keeper)
+            def _():
+                row_outs[a][...] = row_hold[a][1][...]
+
+            @pl.when(other)
+            def _():
+                row_copy(a, 2).start()
+        else:
+
+            @pl.when(other)
+            def _():
+                row_copy(a, 2).wait()
+
+    def small_copy(step):
+        return pltpu.make_async_remote_copy(
+            src_ref=small_hold.at[step], dst_ref=small_land.at[step], send_sem=small_send.at[step],
+            recv_sem=small_recv.at[step], device_id=around[step], device_id_type=MESH,
+        )
+
+    def small_step(step):
+        small_copy(step).wait()
+        total = small_hold[step] + small_land[step]
+        if step + 1 < len(around):
+            small_hold[step + 1] = total
+            small_copy(step + 1).start()
+        else:
+            small_out[...] = total
+
+    for a in range(row_arrays):
+        row_copy(a, 0).start()
+    small_hold[0] = small_in[...]
+    small_copy(0).start()
     last = 2 * steps + 2
-    wave = sorted({u // 2 for u in range(len(units))})
-    for tick in range(len(wave) + last):
+    waves = len(units) // 2
+    for tick in range(waves + last):
         for stage in reversed(range(last + 1)):
             pair = tick - stage
-            if 0 <= pair < len(wave):
+            if 0 <= pair < waves:
                 for u in (2 * pair, 2 * pair + 1):
                     if stage > 0:
                         end(u, stage - 1)
                     if stage < last:
                         begin(u, stage)
-
-
-def sum_weights(grads, split, collective_id):
+        if tick < len(around):
+            small_step(tick)
+        for a in range(row_arrays):
+            if tick == a:
+                row_end(a, 0)
+            if tick == a + 2:
+                row_end(a, 1)
+    for a in range(row_arrays):
+        row_end(a, 2)
+
+
+def sum_all(grads, split, summed, parts, norm_grads, after, tokens, grad_in, gain, collective_id):
     dp = lax.axis_size("dp")
-    shapes = [grad.shape for grad in grads]
-    units = []
+    steps = 0
+    while 2 << steps < dp:
+        steps += 1
+    shapes, units, scratch = [], [], []
+    bf16, f32 = jnp.bfloat16, jnp.float32
+    for index, grad in enumerate(grads):
+        scale = 1 << steps if summed[index // 2] else 1
+        shapes.append((grad.shape[0] * scale, grad.shape[1]))
     for pair in range(len(grads) // 2):
         rows = shapes[2 * pair][0] // split[pair]
         for part in range(split[pair]):
             for side in range(2):
-                units.append((2 * pair + side, part * rows, rows, side))
-    steps = 0
-    while 2 << steps < dp:
-        steps += 1
-    scratch = []
-    for array, first, rows, side in units:
+                units.append((2 * pair + side, part * rows, rows, side, summed[pair]))
+    for array, first, rows, side, done in units:
         width = shapes[array][1]
-        sizes = [rows >> (k + 1) for k in range(steps)] + [rows >> steps]
-        scratch += [pltpu.VMEM((size, width), jnp.bfloat16) for size in sizes]
-        scratch += [pltpu.VMEM((size, width), jnp.bfloat16) for size in sizes]
+        if not done:
+            scratch += [pltpu.VMEM((rows >> (k + 1), width), bf16) for k in range(steps)] * 2
+        scratch.append(pltpu.VMEM((rows >> steps, width), bf16))
     stages = 2 * steps + 2
     vmem = pl.BlockSpec(memory_space=pltpu.VMEM)
+    spans = [part.shape[0] // 4 for part in parts]
+    wide = norm_grads.shape[1]
+    row_land = [pltpu.VMEM((many * span, wide), bf16) for span in spans for many in (2, 1)]
+    semaphores = pltpu.SemaphoreType.DMA
     return pl.pallas_call(
-        functools.partial(sum_kernel, dp, shapes, units),
-        out_shape=[jax.ShapeDtypeStruct(shape, jnp.bfloat16) for shape in shapes],
-        in_specs=[vmem] * len(grads),
-        out_specs=[vmem] * len(grads),
+        functools.partial(sum_kernel, dp, (len(grads), len(parts)), units, spans),
+        out_shape=[jax.ShapeDtypeStruct(shape, bf16) for shape in shapes]
+        + [jax.ShapeDtypeStruct((span, wide), bf16) for span in spans]
+        + [jax.ShapeDtypeStruct(norm_grads.shape, f32)],
+        in_specs=[vmem] * (len(grads) + len(parts) + 5),
+        out_specs=[vmem] * (len(grads) + len(parts) + 1),
         scratch_shapes=scratch
-        + [pltpu.SemaphoreType.DMA((len(units), stages)), pltpu.SemaphoreType.DMA((len(units), stages))],
+        + row_land * 2
+        + [pltpu.VMEM((steps + 3,) + norm_grads.shape, f32)] * 2
+        + [semaphores((steps + 3,))] * 2
+        + [semaphores((len(parts), 3))] * 2
+        + [semaphores((len(units), stages))] * 2,
+        compiler_params=pltpu.CompilerParams(
+            collective_id=collective_id, has_side_effects=True, vmem_limit_bytes=60 << 20
+        ),
+        cost_estimate=pl.CostEstimate(flops=100_000_000_000, bytes_accessed=16_000_000, transcendentals=0),
+        name="sum_all",
+    )(*grads, *parts, norm_grads, after, tokens, grad_in, gain[None])
+
+
+def start_kernel(*refs):
+    (tokens, gain, shift, *weights, out_weight, encoder) = refs[:8]
+    (rows_half, normed, query, keyed, valued, moved, whole, encoder_out) = refs[8:16]
+    send_sem, recv_sem = refs[16:]
+    d, t = lax.axis_index("dp"), lax.axis_index("tensor")
+    core, side, column = d % 2, t % 2, (d // 2) % 4
+    keeper = core == t // 2
+    other = jnp.logical_not(keeper)
+    away = jnp.where(keeper, 0, 1)
+    count = tokens.shape[0]
+    copy = Copies(send_sem, recv_sem)
+    pieces = 4
+    piece = count // pieces
+
+    greet(
+        [(d ^ 2, t), (d ^ 4, t), (d ^ 6, t), (d ^ 1, t), (d, t ^ 1), (d, t ^ 2), (d, t ^ 3), (d ^ 1, t ^ 2)]
+    )
+
+    def place(s, p):
+        return rows_of(rows_half, s * count + p * piece, piece)
+
+    def swap_tokens(p):
+        return copy(("swap", p), tokens.at[pl.ds(p * piece, piece)], place(side, p), (d ^ 1, t ^ 2))
+
+    def pass_tokens(p, src):
+        return copy(("pass", p), src, place(side, p), (d, t ^ 1))
+
+    part = weights[0].shape[0] // 4
+
+    def move(a):
+        return copy(
+            ("move", a), rows_of(weights[a], column * part, part), rows_of(moved.at[a], column * part, part), (d, t ^ 2)
+        )
+
+    def share(a, m):
+        block = rows_of(moved.at[a], column * part, part)
+        return copy(("share", a, m), block, block, (d ^ (2 * m), t))
+
+    shard_rows = out_weight.shape[0]
+    slim = shard_rows // 8
+    slice_at = core * (4 * slim) + column * slim
+
+    def spread(x):
+        block = (2 if x % 2 else 0) + away
+        return copy(
+            ("spread", x), rows_of(out_weight, slice_at, slim),
+            rows_of(whole, block * shard_rows + slice_at, slim), (d, t ^ x),
+        )
+
+    def level(j, m):
+        block = rows_of(whole, j * shard_rows + slice_at, slim)
+        return copy(("level", j, m), block, block, (d ^ (2 * m), t))
+
+    def hand(j):
+        at = core * (4 * slim)
+        return copy(
+            ("hand", j), rows_of(whole, j * shard_rows + at, 4 * slim),
+            rows_of(whole, (j ^ 1) * shard_rows + at, 4 * slim), (d ^ 1, t),
+        )
+
+    def give(s):
+        block = rows_of(normed, core * (2 * count) + s * count, count)
+        return copy(("give", 0), block, block, (d ^ 1, t))
+
+    def give_late(s):
+        block = rows_of(normed, core * (2 * count) + s * count, count)
+        return copy(("give", 1), block, block, (d ^ 1, t))
+
+    encoder_copy = copy("encoder", encoder, encoder_out, (d ^ 1, t))
+
+    @pl.when(other)
+    def _():
+        for p in range(pieces):
+            swap_tokens(p).start()
+
+    @pl.when(keeper)
+    def _():
+        for p in range(pieces):
+            pass_tokens(p, tokens.at[pl.ds(p * piece, piece)]).start()
+        for a in range(3):
+            move(a).start()
+
+    for x in (1, 2, 3):
+        spread(x).start()
+
+    @pl.when(keeper)
+    def _():
+        encoder_copy.start()
+        rows_half[pl.ds(pl.multiple_of(side * count, 16), count), :] = tokens[...]
+
+    whole[pl.ds(pl.multiple_of(away * shard_rows + slice_at, 16), slim), :] = out_weight[
+        pl.ds(pl.multiple_of(slice_at, 16), slim), :
+    ]
+
+    @pl.when(other)
+    def _():
+        for p in range(pieces):
+            swap_tokens(p).wait_recv()
+            pass_tokens(p, place(side, p)).start()
+        for a in range(3):
+            move(a).wait_recv()
+            for m in (1, 2, 3):
+                share(a, m).start()
+
+    mine = core * (2 * count)
+    norm_rows(rows_half, side * count, normed, mine + side * count, count, gain, shift)
+    give(side).start()
+
+    for p in range(pieces):
+        copy(("pass", p), place(1 - side, p), place(1 - side, p), (d, t ^ 1)).wait_recv()
+    norm_rows(rows_half, (1 - side) * count, normed, mine + (1 - side) * count, count, gain, shift)
+    give_late(1 - side).start()
+
+    for x in (1, 2, 3):
+        spread(x).wait_recv()
+    for j in range(4):
+        for m in (1, 2, 3):
+            level(j, m).start()
+
+    @pl.when(keeper)
+    def _():
+        for a in range(3):
+            moved[a] = weights[a][...]
+        encoder_out[...] = encoder[...]
+
+    @pl.when(other)
+    def _():
+        for a in range(3):
+            for m in (1, 2, 3):
+                share(a, m).wait_recv()
+
+    def project(first):
+        def body(i, _):
+            at = pl.ds(pl.multiple_of(first + i * 256, 256), 256)
+            for a, out in enumerate((query, keyed, valued)):
+                out[at, :] = jnp.dot(
+                    normed[at, :], moved[a], preferred_element_type=jnp.float32
+                ).astype(jnp.bfloat16)
+            return 0
+
+        lax.fori_loop(0, (2 * count) // 256, body, 0)
+
+    project(mine)
+
+    give(side).wait()
+    give_late(1 - side).wait()
+    project((1 - core) * (2 * count))
+
+    for j in range(4):
+        for m in (1, 2, 3):
+            level(j, m).wait_recv()
+    for j in range(4):
+        hand(j).start()
+    for j in range(4):
+        for m in (1, 2, 3):
+            level(j, m).wait_send()
+    for x in (1, 2, 3):
+        spread(x).wait_send()
+    for j in range(4):
+        hand(j).wait()
+
+    @pl.when(keeper)
+    def _():
+        for p in range(pieces):
+            pass_tokens(p, tokens.at[pl.ds(p * piece, piece)]).wait_send()
+        for a in range(3):
+            move(a).wait_send()
+        encoder_copy.wait_send()
+
+    @pl.when(other)
+    def _():
+        for p in range(pieces):
+            swap_tokens(p).wait_send()
+            pass_tokens(p, place(side, p)).wait_send()
+        for a in range(3):
+            for m in (1, 2, 3):
+                share(a, m).wait_send()
+        encoder_copy.wait_recv()
+
+
+def start_layer(tokens, gain, shift, weights, out_weight, encoder, collective_id):
+    rows, wide = tokens.shape
+    width = weights[0].shape[1]
+    bf16 = jnp.bfloat16
+    shape = jax.ShapeDtypeStruct
+    vmem = pl.BlockSpec(memory_space=pltpu.VMEM)
+    return pl.pallas_call(
+        start_kernel,
+        out_shape=(
+            shape((2 * rows, wide), bf16),
+            shape((4 * rows, wide), bf16),
+            shape((4 * rows, width), bf16),
+            shape((4 * rows, width), bf16),
+            shape((4 * rows, width), bf16),
+            shape((3,) + weights[0].shape, bf16),
+            shape((4 * out_weight.shape[0], out_weight.shape[1]), bf16),
+            shape(encoder.shape, bf16),
+        ),
+        in_specs=[vmem] * 8,
+        out_specs=(vmem,) * 8,
+        scratch_shapes=[
+            pltpu.SemaphoreType.DMA((64,)),
+            pltpu.SemaphoreType.DMA((64,)),
+        ],
         compiler_params=pltpu.CompilerParams(
             collective_id=collective_id, has_side_effects=True, vmem_limit_bytes=56 << 20
         ),
-        cost_estimate=pl.CostEstimate(flops=100_000_000_000, bytes_accessed=16_000_000, transcendentals=0),
-        name="sum_weights",
-    )(*grads)
+        cost_estimate=pl.CostEstimate(flops=35_000_000_000, bytes_accessed=16_000_000, transcendentals=0),
+        name="start_layer",
+    )(tokens, gain[None], shift[None], *weights, out_weight, encoder)
+
+
+def add_dot(left, right, over_rows=False):
+    return lax.dot_general(
+        left, right, (((1,), (1 if over_rows else 0,)), ((), ())), preferred_element_type=jnp.float32
+    )
+
+
+class Exchange:
+    def __init__(self, copy, mine, land, core, d, t, chunk):
+        self.copy, self.mine, self.land, self.core, self.chunk = copy, mine, land, core, chunk
+        self.half = mine.shape[0] // 2
+        self.to = [(d ^ 1, t), (d, t ^ 1), (d ^ 1, t ^ 1)]
+
+    def one(self, j, ch):
+        core = self.core if j == 1 else 1 - self.core
+        return self.copy(
+            ("exchange", j, ch),
+            rows_of(self.mine, core * self.half + ch * self.chunk, self.chunk),
+            self.land.at[j, pl.ds(ch * self.chunk, self.chunk)],
+            self.to[j],
+        )
+
+    def start(self, ch):
+        for j in (1, 2, 0):
+            self.one(j, ch).start()
+
+    def arrive(self, ch):
+        for j in range(3):
+            self.one(j, ch).wait_recv()
+
+    def pieces(self, ch):
+        first = self.core * self.half + ch * self.chunk
+        own = self.mine[pl.ds(pl.multiple_of(first, 16), self.chunk), :]
+        return [own] + [self.land[j, pl.ds(ch * self.chunk, self.chunk), :] for j in range(3)]
+
+    def sent(self, ch):
+        for j in range(3):
+            self.one(j, ch).wait_send()
+
+
+def by_rows(rows, step, body):
+    def turn(i, _):
+        body(pl.multiple_of(i * step, step))
+        return 0
+
+    lax.fori_loop(0, rows // step, turn, 0)
+
+
+def forward_kernel(*refs):
+    (mixed, out_all, start, gain, shift, weight) = refs[:6]
+    (after, normed, result) = refs[6:9]
+    (land, product, send_sem, recv_sem) = refs[9:]
+    d, t = lax.axis_index("dp"), lax.axis_index("tensor")
+    core = d % 2
+    chunk = product.shape[0]
+    half = after.shape[0]
+    width = mixed.shape[1]
+    copy = Copies(send_sem, recv_sem)
+    greet([(d ^ 1, t), (d, t ^ 1), (d ^ 1, t ^ 1)])
+    exchange = Exchange(copy, mixed, land, core, d, t, chunk)
+
+    def give(ch):
+        block = rows_of(normed, core * half + ch * chunk, chunk)
+        return copy(("give", ch), block, block, (d ^ 1, t))
+
+    chunks = half // chunk
+    for ch in range(chunks):
+        exchange.start(ch)
+    for ch in range(chunks):
+        exchange.arrive(ch)
+        product[...] = sum(
+            add_dot(piece, out_all[j * width : (j + 1) * width, :])
+            for j, piece in enumerate(exchange.pieces(ch))
+        )
+
+        def rows(at, ch=ch):
+            x = start[pl.ds(pl.multiple_of(ch * chunk + at, 16), 32), :].astype(jnp.float32)
+            x = x + product[pl.ds(at, 32), :]
+            after[pl.ds(pl.multiple_of(ch * chunk + at, 16), 32), :] = x
+            unit, inverse = moments(x)
+            normed[pl.ds(pl.multiple_of(core * half + ch * chunk + at, 16), 32), :] = (
+                unit * gain[...] + shift[...]
+            ).astype(jnp.bfloat16)
+
+        by_rows(chunk, 32, rows)
+        give(ch).start()
+
+    def project(first, rows):
+        at = pl.ds(pl.multiple_of(first, 16), rows)
+        result[at, :] = add_dot(normed[at, :], weight[...]).astype(jnp.bfloat16)
+
+    project(core * half, half)
+    for ch in range(chunks):
+        give(ch).wait()
+    project((1 - core) * half, half)
+    for ch in range(chunks):
+        exchange.sent(ch)
+
+
+def forward_step(mixed, out_all, start, gain, shift, weight, collective_id):
+    rows, width = mixed.shape
+    half, wide = start.shape
+    chunk = half // 4
+    shape = jax.ShapeDtypeStruct
+    vmem = pl.BlockSpec(memory_space=pltpu.VMEM)
+    return pl.pallas_call(
+        forward_kernel,
+        out_shape=(
+            shape((half, wide), jnp.float32),
+            shape((rows, wide), jnp.bfloat16),
+            shape((rows, weight.shape[1]), jnp.bfloat16),
+        ),
+        in_specs=[vmem] * 6,
+        out_specs=(vmem,) * 3,
+        scratch_shapes=[
+            pltpu.VMEM((3, half, width), jnp.bfloat16),
+            pltpu.VMEM((chunk, wide), jnp.float32),
+            pltpu.SemaphoreType.DMA((20,)),
+            pltpu.SemaphoreType.DMA((20,)),
+        ],
+        compiler_params=pltpu.CompilerParams(
+            collective_id=collective_id, has_side_effects=True, vmem_limit_bytes=56 << 20
+        ),
+        cost_estimate=pl.CostEstimate(flops=20_000_000_000, bytes_accessed=8_000_000, transcendentals=0),
+        name="forward_step",
+    )(mixed, out_all, start, gain[None], shift[None], weight)
+
+
+def backward_kernel(*refs):
+    (grad_query, query_all, after, gain, grad_in, weight) = refs[:6]
+    (grad_res, grad_top, result, norm_grads) = refs[6:10]
+    (land, product, send_sem, recv_sem) = refs[10:]
+    d, t = lax.axis_index("dp"), lax.axis_index("tensor")
+    core = d % 2
+    chunk = product.shape[0]
+    half = after.shape[0]
+    copy = Copies(send_sem, recv_sem)
+    greet([(d ^ 1, t), (d, t ^ 1), (d ^ 1, t ^ 1)])
+    exchange = Exchange(copy, grad_query, land, core, d, t, chunk)
+
+    def give(ch):
+        block = rows_of(grad_top, core * half + ch * chunk, chunk)
+        return copy(("give", ch), block, block, (d ^ 1, t))
+
+    chunks = half // chunk
+    for ch in range(chunks):
+        exchange.start(ch)
+    norm_grads[...] = jnp.zeros_like(norm_grads)
+    for ch in range(chunks):
+        exchange.arrive(ch)
+        product[...] = sum(add_dot(piece, query_all[j], True) for j, piece in enumerate(exchange.pieces(ch)))
+
+        def rows(at, ch=ch):
+            here = pl.ds(pl.multiple_of(ch * chunk + at, 16), 32)
+            unit, inverse = moments(after[here, :])
+            back, gain_grad, shift_grad = normalize_back(product[pl.ds(at, 32), :], unit, inverse, gain[...])
+            total = grad_in[here, :] + back
+            grad_res[here, :] = total
+            grad_top[pl.ds(pl.multiple_of(core * half + ch * chunk + at, 16), 32), :] = total.astype(jnp.bfloat16)
+            norm_grads[0:1, :] += gain_grad[None]
+            norm_grads[1:2, :] += shift_grad[None]
+
+        by_rows(chunk, 32, rows)
+        give(ch).start()
+
+    def project(first, rows):
+        at = pl.ds(pl.multiple_of(first, 16), rows)
+        result[at, :] = add_dot(grad_top[at, :], weight[...], True).astype(jnp.bfloat16)
+
+    project(core * half, half)
+    for ch in range(chunks):
+        give(ch).wait()
+    project((1 - core) * half, half)
+    for ch in range(chunks):
+        exchange.sent(ch)
+
+
+def backward_step(grad_query, query_all, after, gain, grad_in, weight, collective_id):
+    rows, width = grad_query.shape
+    half, wide = after.shape
+    chunk = half // 4
+    shape = jax.ShapeDtypeStruct
+    vmem = pl.BlockSpec(memory_space=pltpu.VMEM)
+    return pl.pallas_call(
+        backward_kernel,
+        out_shape=(
+            shape((half, wide), jnp.float32),
+            shape((rows, wide), jnp.bfloat16),
+            shape((rows, weight.shape[0]), jnp.bfloat16),
+            shape((8, wide), jnp.float32),
+        ),
+        in_specs=[vmem] * 6,
+        out_specs=(vmem,) * 4,
+        scratch_shapes=[
+            pltpu.VMEM((3, half, width), jnp.bfloat16),
+            pltpu.VMEM((chunk, wide), jnp.float32),
+            pltpu.SemaphoreType.DMA((20,)),
+            pltpu.SemaphoreType.DMA((20,)),
+        ],
+        compiler_params=pltpu.CompilerParams(
+            collective_id=collective_id, has_side_effects=True, vmem_limit_bytes=56 << 20
+        ),
+        cost_estimate=pl.CostEstimate(flops=20_000_000_000, bytes_accessed=8_000_000, transcendentals=0),
+        name="backward_step",
+    )(grad_query, query_all, after, gain[None], grad_in, weight)
+
+
+def hidden_kernel(*refs):
+    (mixed, out_all, start, gain, shift, expand, reduce, grad_out, cot) = refs[:9]
+    (after, normed, hidden, grad_pre, grad_res, grad_top, result, norm_grads) = refs[9:17]
+    (land, product, own, far_send, far_land, sum_send, sum_land, send_sem, recv_sem) = refs[17:]
+    d, t = lax.axis_index("dp"), lax.axis_index("tensor")
+    core = d % 2
+    chunk = product.shape[0]
+    half = after.shape[0]
+    width = mixed.shape[1]
+    chunks = half // chunk
+    copy = Copies(send_sem, recv_sem)
+    greet([(d ^ 1, t), (d, t ^ 1), (d ^ 1, t ^ 1)])
+    exchange = Exchange(copy, mixed, land, core, d, t, chunk)
+
+    def give(name, ref, ch):
+        block = rows_of(ref, core * half + ch * chunk, chunk)
+        return copy((name, ch), block, block, (d ^ 1, t))
+
+    def slab(ref, ch):
+        return ref.at[pl.ds(ch * chunk, chunk)]
+
+    def far(ch):
+        return copy(("far", ch), slab(far_send, ch), slab(far_land, ch), (d ^ 1, t))
+
+    def whole(ch):
+        return copy(("whole", ch), slab(sum_send, ch), slab(sum_land, ch), (d, t ^ 1))
+
+    def residual(ch):
+        exchange.arrive(ch)
+        product[...] = sum(
+            add_dot(piece, out_all[j * width : (j + 1) * width, :])
+            for j, piece in enumerate(exchange.pieces(ch))
+        )
+
+        def rows(at):
+            here = pl.ds(pl.multiple_of(ch * chunk + at, 16), 32)
+            x = start[here, :] + product[pl.ds(at, 32), :]
+            after[here, :] = x
+            unit, inverse = moments(x)
+            normed[pl.ds(pl.multiple_of(core * half + ch * chunk + at, 16), 32), :] = (
+                unit * gain[...] + shift[...]
+            ).astype(jnp.bfloat16)
+
+        by_rows(chunk, 32, rows)
+        give("normed", normed, ch).start()
+
+    def feed(first):
+        every = pl.ds(pl.multiple_of(first, 16), chunk)
+        product[...] = add_dot(normed[every, :], expand[...])
+        own[...] = add_dot(grad_out[every, :], reduce[...], True)
+
+        def rows(at):
+            here = pl.ds(pl.multiple_of(first + at, 16), 32)
+            z = product[pl.ds(at, 32), :]
+            inner = jnp.tanh(tanh_coeff * (z + cubic_coeff * z * z * z))
+            hidden[here, :] = (0.5 * z * (1.0 + inner)).astype(jnp.bfloat16)
+            slope = 0.5 * (1.0 + inner) + 0.5 * z * (1.0 - inner * inner) * tanh_coeff * (
+                1.0 + 3.0 * cubic_coeff * z * z
+            )
+            upper = own[pl.ds(at, 32), :].astype(jnp.bfloat16).astype(jnp.float32)
+            grad_pre[here, :] = (upper * slope).astype(jnp.bfloat16)
+
+        by_rows(chunk, 32, rows)
+        return add_dot(grad_pre[pl.ds(pl.multiple_of(first, 16), chunk), :], expand[...], True)
+
+    def both(ch):
+        copy(
+            ("normed", ch), *([rows_of(normed, (1 - core) * half + ch * chunk, chunk)] * 2), (d ^ 1, t)
+        ).wait_recv()
+        far_send[pl.ds(ch * chunk, chunk), :] = feed((1 - core) * half + ch * chunk).astype(jnp.bfloat16)
+        far(ch).start()
+        own[...] = feed(core * half + ch * chunk)
+        far(ch).wait_recv()
+
+        def rows(at):
+            here = pl.ds(pl.multiple_of(ch * chunk + at, 16), 32)
+            sum_send[here, :] = (own[pl.ds(at, 32), :] + far_land[here, :].astype(jnp.float32)).astype(jnp.bfloat16)
+
+        by_rows(chunk, 32, rows)
+        whole(ch).start()
+
+    def back(ch):
+        whole(ch).wait_recv()
+
+        def rows(at):
+            here = pl.ds(pl.multiple_of(ch * chunk + at, 16), 32)
+            grad = sum_send[here, :].astype(jnp.float32) + sum_land[here, :].astype(jnp.float32)
+            unit, inverse = moments(after[here, :])
+            down, gain_grad, shift_grad = normalize_back(grad, unit, inverse, gain[...])
+            total = cot[here, :].astype(jnp.float32) + down
+            grad_res[here, :] = total
+            grad_top[pl.ds(pl.multiple_of(core * half + ch * chunk + at, 16), 32), :] = total.astype(jnp.bfloat16)
+            norm_grads[0:1, :] += gain_grad[None]
+            norm_grads[1:2, :] += shift_grad[None]
+
+        by_rows(chunk, 32, rows)
+        give("top", grad_top, ch).start()
+
+    def project(first, rows):
+        at = pl.ds(pl.multiple_of(first, 16), rows)
+        result[at, :] = add_dot(grad_top[at, :], out_all[:width, :], True).astype(jnp.bfloat16)
+
+    for ch in range(chunks):
+        exchange.start(ch)
+    norm_grads[...] = jnp.zeros_like(norm_grads)
+    residual(0)
+    residual(1)
+    both(0)
+    residual(2)
+    both(1)
+    residual(3)
+    both(2)
+    back(0)
+    both(3)
+    back(1)
+    back(2)
+    back(3)
+    project(core * half, half)
+    for ch in range(chunks):
+        copy(
+            ("top", ch), *([rows_of(grad_top, (1 - core) * half + ch * chunk, chunk)] * 2), (d ^ 1, t)
+        ).wait_recv()
+    project((1 - core) * half, half)
+    for ch in range(chunks):
+        exchange.sent(ch)
+        give("normed", normed, ch).wait_send()
+        give("top", grad_top, ch).wait_send()
+        far(ch).wait_send()
+        whole(ch).wait_send()
+
+
+def hidden_step(mixed, out_all, start, gain, shift, expand, reduce, grad_out, cot, collective_id):
+    rows, width = mixed.shape
+    half, wide = start.shape
+    inner = expand.shape[1]
+    chunk = half // 4
+    bf16, f32 = jnp.bfloat16, jnp.float32
+    shape = jax.ShapeDtypeStruct
+    vmem = pl.BlockSpec(memory_space=pltpu.VMEM)
+    return pl.pallas_call(
+        hidden_kernel,
+        out_shape=(
+            shape((half, wide), f32),
+            shape((rows, wide), bf16),
+            shape((rows, inner), bf16),
+            shape((rows, inner), bf16),
+            shape((half, wide), f32),
+            shape((rows, wide), bf16),
+            shape((rows, width), bf16),
+            shape((8, wide), f32),
+        ),
+        in_specs=[vmem] * 9,
+        out_specs=(vmem,) * 8,
+        scratch_shapes=[
+            pltpu.VMEM((3, half, width), bf16),
+            pltpu.VMEM((chunk, max(wide, inner)), f32),
+            pltpu.VMEM((chunk, max(wide, inner)), f32),
+            pltpu.VMEM((half, wide), bf16),
+            pltpu.VMEM((half, wide), bf16),
+            pltpu.VMEM((half, wide), bf16),
+            pltpu.VMEM((half, wide), bf16),
+            pltpu.SemaphoreType.DMA((32,)),
+            pltpu.SemaphoreType.DMA((32,)),
+        ],
+        compiler_params=pltpu.CompilerParams(
+            collective_id=collective_id, has_side_effects=True, vmem_limit_bytes=60 << 20
+        ),
+        cost_estimate=pl.CostEstimate(flops=50_000_000_000, bytes_accessed=16_000_000, transcendentals=0),
+        name="hidden_step",
+    )(mixed, out_all, start, gain[None], shift[None], expand, reduce, grad_out, cot)
 
 
 def on_device(
@@ -516,69 +1250,53 @@
     cross_keys = jnp.stack([frame_seg] * 8)
     seg_col, seg_row = token_seg[:, None], token_seg[None, :]
 
-    first_weight = place.moved_weight(
-        jnp.concatenate([causal_query, causal_key, causal_value], axis=1)
-    )
-    tokens_here = place.home(tokens)
-    tokens_half = half_rows(tokens_here)
-    residual = tokens_half.astype(jnp.float32)
-    unit, inverse = moments(residual)
-    first_all = place.both_cores((unit * first_gain + first_shift).astype(jnp.bfloat16))
-    mixed_in = times(first_all, first_weight).astype(jnp.bfloat16)
-    query, keyed, valued = (mixed_in[:, i * width : (i + 1) * width] for i in range(3))
-
-    encoder = of_group(encoder_states)
-    cross_weight = place.moved_weight(jnp.concatenate([cross_key, cross_value], axis=1))
+    cross_weight = place.moved_weight(jnp.concatenate([cross_key, cross_value, cross_query], axis=1))
+    cross_query_here = cross_weight[:, 2 * width :]
+    cross_weight = cross_weight[:, : 2 * width]
+    tokens_half, first_all, query, keyed, valued, moved, causal_out_perm, encoder = start_layer(
+        tokens,
+        first_gain,
+        first_shift,
+        (causal_query, causal_key, causal_value),
+        causal_out,
+        encoder_states,
+        1,
+    )
+    tokens_here = quarter_of(tokens_half)
     cross_in = times(encoder, cross_weight).astype(jnp.bfloat16)
     ckeyed, cvalued = cross_in[:, :width], cross_in[:, width:]
-    causal_out_all = place.whole_weight(causal_out)
     cross_out_all = place.whole_weight(cross_out)
     cross_query_all = place.whole_weight(cross_query)
     order = place.order()
     pick = lambda every, which: lax.dynamic_index_in_dim(every, which, 0, keepdims=False)
-    causal_out_perm = jnp.concatenate([pick(causal_out_all, s) for s in order])
     cross_out_perm = jnp.concatenate([pick(cross_out_all, s) for s in order])
-    cross_query_perm = jnp.concatenate([pick(cross_query_all, s) for s in order], axis=1)
+    cross_query_every = jnp.stack([pick(cross_query_all, s) for s in order])
     causal_out_here, cross_out_here = causal_out_perm[:width], cross_out_perm[:width]
-    cross_query_here = cross_query_perm[:, :width]
 
     mixed, self_logsum = attend_fwd(
         query, keyed, valued, seg_col, self_keys, self_lo, self_hi, True, block_q, block_k
     )
-    after_self = residual + times(place.spread_columns(mixed), causal_out_perm)
-    second_unit, second_inv = moments(after_self)
-    second_all = place.both_cores((second_unit * second_gain + second_shift).astype(jnp.bfloat16))
-    cquery = times(second_all, cross_query_here).astype(jnp.bfloat16)
+    after_self, second_all, cquery = forward_step(
+        mixed, causal_out_perm, tokens_half, second_gain, second_shift, cross_query_here, 2
+    )
     cmixed, cross_logsum = attend_fwd(
         cquery, ckeyed, cvalued, seg_col, cross_keys, cross_lo, cross_hi, False, block_q, block_k
     )
-    after_cross = after_self + times(place.spread_columns(cmixed), cross_out_perm)
-    third_unit, third_inv = moments(after_cross)
-    third_all = place.both_cores((third_unit * third_gain + third_shift).astype(jnp.bfloat16))
-
     ff_weight = place.moved_weight(jnp.concatenate([expand_weight, reduce_weight], axis=1))
     hidden_width = expand_weight.shape[1]
     expand_here, reduce_here = ff_weight[:, :hidden_width], ff_weight[:, hidden_width:]
     cot_half = half_rows(place.home(cotangent))
     grad_top = place.both_cores(cot_half)
-    grad_hidden = against(grad_top, reduce_here).astype(jnp.bfloat16)
-
-    pre_act = times(third_all, expand_here)
-    hidden = smooth_gate(pre_act).astype(jnp.bfloat16)
-    grad_expand_in = (grad_hidden.astype(jnp.float32) * smooth_slope(pre_act)).astype(jnp.bfloat16)
-    third_in = place.sum_group_half(against(grad_expand_in, expand_here))
-    back_rows, third_gain_grad, third_shift_grad = normalize_back(
-        third_in, third_unit, third_inv, third_gain
-    )
-    grad_res = cot_half.astype(jnp.float32) + back_rows
-    out_here = quarter_of(after_cross) + place.sum_group_quarter(times(hidden, reduce_here))
-    output = place.home(out_here.astype(jnp.bfloat16))
+
+    after_cross, third_all, hidden, grad_expand_in, grad_res, grad_top2, grad_cmixed, third_grads = hidden_step(
+        cmixed, cross_out_perm, after_self, third_gain, third_shift, expand_here, reduce_here, grad_top, cot_half, 3
+    )
+    third_gain_grad, third_shift_grad = third_grads[0], third_grads[1]
+    out_term = times(hidden, reduce_here).astype(jnp.bfloat16)
     reduce_grad = along_rows(hidden, grad_top)
     expand_grad = along_rows(third_all, grad_expand_in)
 
-    grad_top = place.both_cores(grad_res.astype(jnp.bfloat16))
-    cross_out_grad = along_rows(cmixed, grad_top)
-    grad_cmixed = against(grad_top, cross_out_here).astype(jnp.bfloat16)
+    cross_out_grad = along_rows(cmixed, grad_top2)
     grad_cquery, grad_ckey, grad_cvalue = attend_bwd(
         cquery, ckeyed, cvalued, cmixed, grad_cmixed, cross_logsum, seg_row, cross_keys.T,
         cross_lo, cross_hi, False, block_q, block_k,
@@ -586,32 +1304,40 @@
     grad_cross_in = jnp.concatenate([grad_ckey, grad_cvalue], axis=1)
     cross_grad = along_rows(encoder, grad_cross_in)
     cross_query_grad = along_rows(second_all, grad_cquery)
-    encoder_grad = place.home(
-        place.sum_group_quarter(against(grad_cross_in, cross_weight)).astype(jnp.bfloat16)
-    )
-    second_in = against(place.spread_columns(grad_cquery), cross_query_perm)
-    back_rows, second_gain_grad, second_shift_grad = normalize_back(
-        second_in, second_unit, second_inv, second_gain
-    )
-    grad_res = grad_res + back_rows
-    grad_top = place.both_cores(grad_res.astype(jnp.bfloat16))
+    encoder_term = against(grad_cross_in, cross_weight).astype(jnp.bfloat16)
+    grad_res, grad_top, grad_mixed, second_grads = backward_step(
+        grad_cquery, cross_query_every, after_self, second_gain, grad_res, causal_out_here, 4
+    )
+    second_gain_grad, second_shift_grad = second_grads[0], second_grads[1]
     causal_out_grad = along_rows(mixed, grad_top)
-    grad_mixed = against(grad_top, causal_out_here).astype(jnp.bfloat16)
     grad_query, grad_key, grad_value = attend_bwd(
         query, keyed, valued, mixed, grad_mixed, self_logsum, seg_row, self_keys.T,
         self_lo, self_hi, True, block_q, block_k,
     )
     grad_in = jnp.concatenate([grad_query, grad_key, grad_value], axis=1)
     causal_grad = along_rows(first_all, grad_in)
-    first_in = place.sum_group_quarter(against(grad_in, first_weight))
-    first_unit, first_inv = moments(tokens_here.astype(jnp.float32))
-    back_rows, first_gain_grad, first_shift_grad = normalize_back(
-        first_in, first_unit, first_inv, first_gain
-    )
-    tokens_grad = place.home((quarter_of(grad_res) + back_rows).astype(jnp.bfloat16))
-
+    first_term = (
+        against(grad_query, moved[0]) + against(grad_key, moved[1]) + against(grad_value, moved[2])
+    )
+    first_rows = (first_all.astype(jnp.float32) - first_shift) / first_gain
+    first_gain_grad = jnp.sum(first_term * first_rows, axis=0)
+    first_shift_grad = jnp.sum(first_term, axis=0)
     bf16 = jnp.bfloat16
-    sums = sum_weights(
+    once = (place.side == 0).astype(jnp.float32)
+    none = jnp.zeros_like(first_gain_grad)
+    norm_grads = jnp.stack(
+        [
+            first_gain_grad,
+            first_shift_grad,
+            second_gain_grad * once,
+            second_shift_grad * once,
+            third_gain_grad * once,
+            third_shift_grad * once,
+            none,
+            none,
+        ]
+    )
+    *sums, encoder_grad, output, tokens_grad, norm_grads = sum_all(
         [
             expand_grad.astype(bf16),
             reduce_grad.astype(bf16),
@@ -621,18 +1347,15 @@
             causal_out_grad.astype(bf16),
         ],
         (2, 1, 1),
+        (False, False, False),
+        [encoder_term, out_term, first_term.astype(bf16)],
+        norm_grads,
+        quarter_of(after_cross),
+        tokens_here,
+        quarter_of(grad_res),
+        first_gain,
         0,
     )
-    expand_grad, reduce_grad, cross_grads, causal_grads, cross_out_grad, causal_out_grad = (
-        value.astype(jnp.float32) for value in sums
-    )
-    cross_key_grad, cross_value_grad, cross_query_grad = (
-        cross_grads[:, i * width : (i + 1) * width] for i in range(3)
-    )
-    causal_query_grad, causal_key_grad, causal_value_grad = (
-        causal_grads[:, i * width : (i + 1) * width] for i in range(3)
-    )
-    once = (place.side == 0).astype(jnp.float32)
     (
         first_gain_grad,
         first_shift_grad,
@@ -640,16 +1363,15 @@
         second_shift_grad,
         third_gain_grad,
         third_shift_grad,
-    ) = lax.psum(
-        (
-            first_gain_grad,
-            first_shift_grad,
-            second_gain_grad * once,
-            second_shift_grad * once,
-            third_gain_grad * once,
-            third_shift_grad * once,
-        ),
-        ("dp", "tensor"),
+    ) = (norm_grads[i] for i in range(6))
+    expand_grad, reduce_grad, cross_grads, causal_grads, cross_out_grad, causal_out_grad = (
+        value.astype(jnp.float32) for value in sums
+    )
+    cross_key_grad, cross_value_grad, cross_query_grad = (
+        cross_grads[:, i * width : (i + 1) * width] for i in range(3)
+    )
+    causal_query_grad, causal_key_grad, causal_value_grad = (
+        causal_grads[:, i * width : (i + 1) * width] for i in range(3)
     )
     return (
         output,

time: 694 us -> 578 us (0.83)
  Pallas kernels: 194 us -> 426 us
  waiting for transfers between devices: 216 us -> 23.1 us
  blocking collectives: 43.9 us -> 0 us
  matrix products: 74.2 us -> 33.2 us
  starting transfers between devices: 48.2 us -> 11 us
  other arithmetic: 45.5 us -> 25.7 us
    pallas_call x1 -> x5, Pallas kernels: 139 us -> 357 us  [the longest x1 162 us: sum_all(): pl.pallas_call(functools.partial(sum_kernel, dp, (len(grads), len(parts))...]
    all_gather x3 -> x2, waiting for transfers between devices: 94.2 us -> 0.01 us  [whole_weight(): every = lax.all_gather(piece, ('dp', 'tensor'), axis=0, tiled=False)]
    ppermute x37 -> x8, waiting for transfers between devices: 76.8 us -> 23 us  [swap(): return lax.ppermute(value, ('dp', 'tensor'), pairs)]
    all_gather x3 -> x2, waiting for transfers between devices: 45.1 us -> 0.01 us  [moved_weight(): lax.all_gather(piece, 'dp', axis=0, tiled=True)]
    psum x1 -> x0, blocking collectives: 43.9 us -> none  [on_device(): lax.psum((first_gain_grad, first_shift_grad, second_gain_grad * once, sec...]
    ppermute x37 -> x8, starting transfers between devices: 48 us -> 10.8 us  [swap(): return lax.ppermute(value, ('dp', 'tensor'), pairs)]
    dot_general x7 -> x2, matrix products: 27.7 us -> 6.12 us  [times(): return jnp.dot(left, weight, preferred_element_type=jnp.float32)]
    convert_element_type x9 -> x0, other arithmetic: 11.3 us -> none  [the longest x2 4.38 us: on_device(): grad_top = place.both_cores(grad_res.astype(jnp.bfloat16))]
  transfers between devices with their start and end apart: 43 -> 12, of which waited for: 14 -> 2; matrix products, arithmetic and copies ran while one was open for 21% -> 5% of each run, Pallas kernels for 25% -> 26%
where the time goes in v4:
time: 578 us; the launch traced here: 579 us
  Pallas kernels  426 us (74%)
  local copies, waits for them, and re-layouts  45 us (8%)
  matrix products  33.2 us (6%)
  other arithmetic  25.7 us (4%)
  waiting for transfers between devices  23.1 us (4%)
  between operations  14.8 us (3%)
  starting transfers between devices  11 us (2%)
    pallas_call x1, Pallas kernels, sum_all(): pl.pallas_call(functools.partial(sum_kernel, dp, (len(grads), len(parts))...  162 us
    pallas_call x1, Pallas kernels, start_layer(): pl.pallas_call(start_kernel, out_shape=(shape((2 * rows, wide), bf16), sh...  92.2 us
    pallas_call x1, Pallas kernels, hidden_step(): pl.pallas_call(hidden_kernel, out_shape=(shape((half, wide), f32), shape(...  53.2 us
    pallas_call x2, Pallas kernels, attend_bwd(): pl.pallas_call(functools.partial(bwd_kernel, causal, heads, bq, bk), out_...  38.5 us
    pallas_call x2, Pallas kernels, attend_fwd(): pl.pallas_call(functools.partial(fwd_kernel, causal, heads, bq, bk), out_...  30.6 us
    pallas_call x1, Pallas kernels, forward_step(): pl.pallas_call(forward_kernel, out_shape=(shape((half, wide), jnp.float32...  25.5 us
    pallas_call x1, Pallas kernels, backward_step(): pl.pallas_call(backward_kernel, out_shape=(shape((half, wide), jnp.float3...  23.5 us
    ppermute x8, waiting for transfers between devices, swap(): return lax.ppermute(value, ('dp', 'tensor'), pairs)  23 us
  transfers between devices with their start and end apart: 12, of which 2 were waited for; matrix products, arithmetic and copies ran while one was open for 5% of the time, Pallas kernels for 26%

profile of v4, /device:TPU:1, one launch (start us, length us, event | category | flops | bytes accessed | tf_op | source)
XLA Modules:
  0.0 578.7 jit_solution(10893866614658935561)
XLA Ops:
  7.3 1.2 constant_dynamic-update-slice_fusion.2
  8.5 1.1 constant_dynamic-update-slice_fusion.1
  9.7 3.2 collective-permute-start.3
  12.9 8.8 %collective-permute-done.3 = bf16[128,768]{1,0:T(8,128)(2,1)S(1)} collective-permute-done((bf16[128,768]{1,0:T(8,128)(2,1)S(1)}, bf16[128,768]{1,0:T(8,128)(2,1)S(1)}, u32[]{:S(2)}, u32[]{:S(2)}) %collective-permute-start.3) | collective-permute-done | bytes 196640 | tf_op jit(solution)/shard_map/ppermute | solution.py:243
  23.2 1.3 collective-permute-start
  25.1 3.1 constant_dynamic-update-slice_fusion.4
  28.1 1.5 constant_dynamic-update-slice_fusion.3
  29.6 1.9 constant_dynamic-slice_fusion.8
  31.5 4.5 collective-permute-start.5
  36.8 92.2 %start_layer.1 = (bf16[512,1024]{1,0:T(8,128)(2,1)}, bf16[1024,1024]{1,0:T(8,128)(2,1)}, bf16[1024,256]{1,0:T(8,128)(2,1)}, bf16[1024,256]{1,0:T(8,128)(2,1)}, b...) custom-call(bf16[256,1024]{1,0:T(8,128)(2,1)} %refs_0_.1, ...), custom_call_target="tpu_custom_call" | custom-call | flops 35000000512 | bytes 16000000 | tf_op jit(solution)/shard_map/start_layer/pallas_call | solution.py:802
  129.1 1.9 slice.92.refs_5_
  130.9 1.9 constant_dynamic-slice_fusion.1.refs_11_
  133.7 0.9 broadcast_select_fusion.2
  135.3 14.1 %collective-permute-done.6 = bf16[256,1024]{1,0:T(8,128)(2,1)} collective-permute-done((bf16[256,1024]{1,0:T(8,128)(2,1)}, bf16[256,1024]{1,0:T(8,128)(2,1)}, u32[]{:S(2)}, u32[]{:S(2)}) %collective-permute-start.6) | collective-permute-done | bytes 524320 | tf_op jit(solution)/shard_map/ppermute | solution.py:243
  149.4 2.0 maximum_select_fusion.1.refs_8_
  151.5 1.3 collective-permute-start.7
  152.8 11.0 %attend_fwd.2 = (bf16[1024,256]{1,0:T(8,128)(2,1)S(1)}, f32[8,1024]{1,0:T(8,128)S(1)}) custom-call(s32[4]{0:T(128)S(1)} %and_select_fusion.1.lo_ref, s32[4]{0:T(128)S(1)} %and_select_fusion.hi_ref, bf16[1024,256]{1,0:T(8,128)(2,1)S(1)} %copy-done.14, bf16[1024,256]{1,0:T(8,128)(2,1)S(1)} %copy-done.16, bf16[1024,256]{1,0:T(8,128)(2,1)S(1)} %copy-done.18, ...), custom_call_target="tpu_custom_call" | custom-call | flops 22000001024 | bytes 8000000 | tf_op jit(solution)/shard_map/attend_fwd/pallas_call | solution.py:102
  164.6 2.3 maximum_select_fusion.refs_7_
  166.9 1.7 broadcast_select_fusion.1
  168.7 0.8 slice.112.refs_5_
  169.6 2.4 convolution_convert_fusion.1
  172.2 25.5 %forward_step.1 = (f32[512,1024]{1,0:T(8,128)}, bf16[1024,1024]{1,0:T(8,128)(2,1)}, bf16[1024,256]{1,0:T(8,128)(2,1)}) custom-call(bf16[1024,256]{1,0:T(8,128)(2,1)} %copy-done.2, bf16[1024,1024]{1,0:T(8,128)(2,1)} %get-tuple-element.66.refs_1_, bf16[512,1024]{1,0:T(8,128)(2,1)} %get-tuple-element.67.refs_2_, f32[1,1024]{1,0:T(1,128)} %bitcast.112, ...), custom_call_target="tpu_custom_call" | custom-call | flops 20000000000 | bytes 8000000 | tf_op jit(solution)/shard_map/forward_step/pallas_call | solution.py:932
  197.7 1.0 copy-done.12
  198.7 19.6 %attend_fwd.3 = (bf16[1024,256]{1,0:T(8,128)(2,1)S(1)}, f32[8,1024]{1,0:T(8,128)S(1)}) custom-call(s32[4]{0:T(128)S(1)} %and_select_fusion.3.lo_ref, s32[4]{0:T(128)S(1)} %and_select_fusion.2.hi_ref, bf16[1024,256]{1,0:T(8,128)(2,1)S(1)} %copy-done.12, bf16[2048,256]{1,0:T(8,128)(2,1)S(1)} %get-tuple-element.121.k_ref, ...), custom_call_target="tpu_custom_call" | custom-call | flops 22000001024 | bytes 8000000 | tf_op jit(solution)/shard_map/attend_fwd/pallas_call | solution.py:102
  219.2 3.2 copy.72
  222.3 1.9 copy.75
  224.6 1.2 dynamic-slice_bitcast_fusion.3
  225.9 1.6 pad_maximum_fusion.1.refs_1_
  227.5 2.8 broadcast_select_fusion
  230.3 3.1 fusion.23
  233.4 0.8 copy-done.21
  234.2 53.2 %hidden_step.1 = (f32[512,1024]{1,0:T(8,128)}, bf16[1024,1024]{1,0:T(8,128)(2,1)}, bf16[1024,1024]{1,0:T(8,128)(2,1)}, bf16[1024,1024]{1,0:T(8,128)(2,1)}, f32[5...) custom-call(bf16[1024,256]{1,0:T(8,128)(2,1)} %copy-done.4, ...), custom_call_target="tpu_custom_call" | custom-call | flops 49999998976 | bytes 16000000 | tf_op jit(solution)/shard_map/hidden_step/pallas_call | solution.py:1173
  287.7 1.0 copy-done.13
  288.8 1.0 copy-done.20
  289.8 25.7 %attend_bwd.2 = (bf16[1024,256]{1,0:T(8,128)(2,1)S(1)}, bf16[2048,256]{1,0:T(8,128)(2,1)S(1)}, bf16[2048,256]{1,0:T(8,128)(2,1)S(1)}) custom-call(s32[4]{0:T(128)S(1)} %and_select_fusion.3.lo_ref, s32[4]{0:T(128)S(1)} %and_select_fusion.2.hi_ref, bf16[1024,256]{1,0:T(8,128)(2,1)S(1)} %copy-done.13, bf16[2048,256]{1,0:T(8,128)(2,1)S(1)} %get-tuple-element.121.k_ref, ...), custom_call_target="tpu_custom_call" | custom-call | flops 30000001024 | bytes 8000000 | tf_op jit(solution)/shard_map/attend_bwd/pallas_call | solution.py:167
  315.7 2.2 copy-done.55
  317.9 2.4 convolution_convert_fusion.6
  320.3 4.4 convolution_convert_fusion.refs_6_
  324.7 3.7 convolution_convert_fusion.3.refs_1_
  328.4 3.7 convolution_convert_fusion.2.refs_7_
  332.1 1.5 convolution_convert_fusion.8.refs_4_
  334.5 23.5 %backward_step.1 = (f32[512,1024]{1,0:T(8,128)}, bf16[1024,1024]{1,0:T(8,128)(2,1)}, bf16[1024,256]{1,0:T(8,128)(2,1)}, f32[8,1024]{1,0:T(8,128)}) custom-call(bf16[1024,256]{1,0:T(8,128)(2,1)} %copy-done.10, bf16[4,1024,256]{2,1,0:T(8,128)(2,1)} %pad_maximum_fusion.1.refs_1_, f32[512,1024]{1,0:T(8,128)} %get-tuple-element.71.refs_2_, f32[1,1024]{1,0:T(1,128)} %bitcast.113, ...), custom_call_target="tpu_custom_call" | custom-call | flops 20000000000 | bytes 8000000 | tf_op jit(solution)/shard_map/backward_step/pallas_call | solution.py:1010
  358.1 3.3 convolution_convert_fusion.7.refs_5_
  361.4 12.8 %attend_bwd.3 = (bf16[1024,256]{1,0:T(8,128)(2,1)S(1)}, bf16[1024,256]{1,0:T(8,128)(2,1)S(1)}, bf16[1024,256]{1,0:T(8,128)(2,1)S(1)}) custom-call(s32[4]{0:T(128)S(1)} %copy-done.7, s32[4]{0:T(128)S(1)} %copy-done.9, bf16[1024,256]{1,0:T(8,128)(2,1)S(1)} %copy-done.15, bf16[1024,256]{1,0:T(8,128)(2,1)S(1)} %copy-done.17, bf16[1024,256]{1,0:T(8,128)(2,1)S(1)} %copy-done.19, ...), custom_call_target="tpu_custom_call" | custom-call | flops 30000001024 | bytes 8000000 | tf_op jit(solution)/shard_map/attend_bwd/pallas_call | solution.py:167
  375.7 1.2 slice_multiply_fusion.2
  376.9 0.8 slice_multiply_fusion
  377.7 1.0 constant_dynamic-slice_fusion.2.refs_10_
  378.8 1.0 constant_dynamic-slice_fusion.refs_12_
  379.8 3.8 convolution_convert_fusion.4.refs_0_
  383.6 1.3 pad_maximum_fusion.2.refs_2_
  384.9 0.8 copy-done.57
  385.8 3.1 convolution_convert_fusion.5.refs_3_
  388.8 2.8 fusion.22
  392.3 162.4 %sum_all.1 = (bf16[1024,1024]{1,0:T(8,128)(2,1)}, bf16[1024,1024]{1,0:T(8,128)(2,1)}, bf16[1024,768]{1,0:T(8,128)(2,1)}, bf16[1024,768]{1,0:T(8,128)(2,1)}, bf16...) custom-call(bf16[1024,1024]{1,0:T(8,128)(2,1)} %convolution_convert_, ...), custom_call_target="tpu_custom_call" | custom-call | flops 99999997952 | bytes 16000000 | tf_op jit(solution)/shard_map/sum_all/pallas_call | solution.py:595
  554.7 1.7 fusion.27
  556.4 3.2 fusion.26
  559.5 1.1 convert_element_type.75
  561.3 1.7 fusion.25
  563.1 1.1 convert_element_type.77
  564.4 2.5 convert_element_type.78
  566.8 2.5 convert_element_type.79
  569.3 0.8 copy.86
  570.1 0.8 copy.87
  570.9 1.0 copy.88
  (172 shorter events, 11.2 us)
Async XLA Ops:
  7.2 15.3 %copy-start = (bf16[256,1024]{1,0:T(8,128)(2,1)S(1)}, bf16[256,1024]{1,0:T(8,128)(2,1)}, u32[]{:S(2)}) copy-start(bf16[256,1024]{1,0:T(8,128)(2,1)} %param.38) | copy-start | bytes 1572868
  7.2 2.4 copy-start.40
  7.2 16.0 %copy-start.50 = (s32[1,4]{1,0:T(1,128)S(1)}, s32[1,4]{1,0:T(1,128)}, u32[]{:S(2)}) copy-start(s32[1,4]{1,0:T(1,128)} %param.24) | copy-start | bytes 52
  7.2 17.3 %copy-start.51 = (s32[1,4]{1,0:T(1,128)S(1)}, s32[1,4]{1,0:T(1,128)}, u32[]{:S(2)}) copy-start(s32[1,4]{1,0:T(1,128)} %param.25) | copy-start | bytes 52
  7.2 17.4 %copy-start.49 = (s32[1024]{0:T(1024)S(1)}, s32[1024]{0:T(1024)}, u32[]{:S(2)}) copy-start(s32[1024]{0:T(1024)} %param.26) | copy-start | bytes 12292
  7.2 159.7 %all-gather.7.cloned.1.call-start = ((), (), s32[]{:S(2)}) async-start(), calls=%async_computation | async-start | bytes 1769472 | tf_op jit(solution)/shard_map/all_gather | solution.py:284
  9.6 18.5 %copy-start.26 = (bf16[1024,768]{1,0:T(8,128)(2,1)}, bf16[1024,768]{1,0:T(8,128)(2,1)S(1)}, u32[]{:S(2)}) copy-start(bf16[1024,768]{1,0:T(8,128)(2,1)S(1)} %constant_dynamic-update-slice_fusion) | copy-start | bytes 4718596
  9.7 12.0 %collective-permute-start.3 = (bf16[128,768]{1,0:T(8,128)(2,1)S(1)}, bf16[128,768]{1,0:T(8,128)(2,1)S(1)}, u32[]{:S(2)}, u32[]{:S(2)}) collective-permute-start(bf16[128,768]{1,0:T(8,128)(2,1)S(1)} %constant_dynamic-slice_fusion.10), channel_id=1, source_target_pairs={{0,2},{1,3},{2,0},{3,1},{4,6},{5,7},{6,4},{7,5},{8,10},{9,11},{10,... | collective-permute-start | bytes 589832 | tf_op jit(solution)/shard_map/ppermute | solution.py:243
  22.4 196.7 %all-gather.11.cloned.1.call-start = ((), (), s32[]{:S(2)}) async-start(), calls=%async_computation.2 | async-start | bytes 2162688 | tf_op jit(solution)/shard_map/all_gather | solution.py:288
  23.2 199.2 %all-gather.13.cloned.1.call-start = ((), (), s32[]{:S(2)}) async-start(), calls=%async_computation.3 | async-start | bytes 2162688 | tf_op jit(solution)/shard_map/all_gather | solution.py:288
  23.2 4.9 copy-start.33
  23.2 109.6 %collective-permute-start = (s32[1,4]{1,0:T(1,128)S(1)}, s32[1,4]{1,0:T(1,128)S(1)}, u32[]{:S(2)}, u32[]{:S(2)}) collective-permute-start(s32[1,4]{1,0:T(1,128)S(1)} %copy-done.50), channel_id=1, source_target_pairs={{0,4},{1,5},{2,6},{3,7},{4,0},{5,1},{6,2},{7,3},{8,12},{9,13},{10,... | collective-permute-start | bytes 56 | tf_op jit(solution)/shard_map/ppermute | solution.py:243
  24.5 108.7 %collective-permute-start.1 = (s32[1,4]{1,0:T(1,128)S(1)}, s32[1,4]{1,0:T(1,128)S(1)}, u32[]{:S(2)}, u32[]{:S(2)}) collective-permute-start(s32[1,4]{1,0:T(1,128)S(1)} %copy-done.51), channel_id=1, source_target_pairs={{0,4},{1,5},{2,6},{3,7},{4,0},{5,1},{6,2},{7,3},{8,12},{9,13},{10,... | collective-permute-start | bytes 56 | tf_op jit(solution)/shard_map/ppermute | solution.py:243
  24.6 110.4 %collective-permute-start.2 = (s32[1024]{0:T(1024)S(1)}, s32[1024]{0:T(1024)S(1)}, u32[]{:S(2)}, u32[]{:S(2)}) collective-permute-start(s32[1024]{0:T(1024)S(1)} %copy-done.49), channel_id=1, source_target_pairs={{0,4},{1,5},{2,6},{3,7},{4,0},{5,1},{6,2},{7,3},{8,12},{9,13},{10,... | collective-permute-start | bytes 12296 | tf_op jit(solution)/shard_map/ppermute | solution.py:243
  28.1 3.4 copy-start.45
  31.5 103.8 %collective-permute-start.4 = (bf16[128,2048]{1,0:T(8,128)(2,1)}, bf16[128,2048]{1,0:T(8,128)(2,1)}, u32[]{:S(2)}, u32[]{:S(2)}) collective-permute-start(bf16[128,2048]{1,0:T(8,128)(2,1)} %constant_dynamic-slice_fusion.8), channel_id=1, source_target_pairs={{0,2},{1,3},{2,0},{3,1},{4,6},{5,7},{6,4},{7,5},{8,10},{9,11},{10,... | collective-permute-start | bytes 1572872 | tf_op jit(solution)/shard_map/ppermute | solution.py:243
  31.5 102.2 %collective-permute-start.5 = (bf16[256,1024]{1,0:T(8,128)(2,1)S(1)}, bf16[256,1024]{1,0:T(8,128)(2,1)S(1)}, u32[]{:S(2)}, u32[]{:S(2)}) collective-permute-start(bf16[256,1024]{1,0:T(8,128)(2,1)S(1)} %copy-done.45), channel_id=1, source_target_pairs={{2,4},{3,5},{4,2},{5,3},{10,12},{11,13},{12,10},{13,11},{18,20},{1... | collective-permute-start | bytes 1572872 | tf_op jit(solution)/shard_map/ppermute | solution.py:243
  36.7 190.8 %all-gather.9.cloned.1.call-start = ((), (), s32[]{:S(2)}) async-start(), calls=%async_computation.1 | async-start | bytes 4718592 | tf_op jit(solution)/shard_map/all_gather | solution.py:284
  130.9 21.8 %copy-start.8 = (s32[4]{0:T(128)}, s32[4]{0:T(128)S(1)}, u32[]{:S(2)}) copy-start(s32[4]{0:T(128)S(1)} %and_select_fusion.hi_ref) | copy-start | bytes 52
  134.6 18.2 %copy-start.14 = (bf16[1024,256]{1,0:T(8,128)(2,1)S(1)}, bf16[1024,256]{1,0:T(8,128)(2,1)}, u32[]{:S(2)}) copy-start(bf16[1024,256]{1,0:T(8,128)(2,1)} %get-tuple-element.62.q_ref) | copy-start | bytes 1572868
  134.6 18.2 %copy-start.16 = (bf16[1024,256]{1,0:T(8,128)(2,1)S(1)}, bf16[1024,256]{1,0:T(8,128)(2,1)}, u32[]{:S(2)}) copy-start(bf16[1024,256]{1,0:T(8,128)(2,1)} %get-tuple-element.63.k_ref) | copy-start | bytes 1572868
  134.6 18.2 %copy-start.18 = (bf16[1024,256]{1,0:T(8,128)(2,1)S(1)}, bf16[1024,256]{1,0:T(8,128)(2,1)}, u32[]{:S(2)}) copy-start(bf16[1024,256]{1,0:T(8,128)(2,1)} %get-tuple-element.64.v_ref) | copy-start | bytes 1572868
  134.6 14.8 %collective-permute-start.6 = (bf16[256,1024]{1,0:T(8,128)(2,1)}, bf16[256,1024]{1,0:T(8,128)(2,1)}, u32[]{:S(2)}, u32[]{:S(2)}) collective-permute-start(bf16[256,1024]{1,0:T(8,128)(2,1)} %broadcast_select_fusion.2), channel_id=1, source_target_pairs={{0,1},{1,0},{2,3},{3,2},{4,5},{5,4},{6,7},{7,6},{8,9},{9,8},{10,11... | collective-permute-start | bytes 1572872 | tf_op jit(solution)/shard_map/ppermute | solution.py:243
  134.6 29.1 %copy-start.6 = (s32[4]{0:T(128)}, s32[4]{0:T(128)S(1)}, u32[]{:S(2)}) copy-start(s32[4]{0:T(128)S(1)} %and_select_fusion.1.lo_ref) | copy-start | bytes 52
  151.5 13.1 %copy-start.25 = (bf16[512,1024]{1,0:T(8,128)(2,1)}, bf16[512,1024]{1,0:T(8,128)(2,1)S(1)}, u32[]{:S(2)}) copy-start(bf16[512,1024]{1,0:T(8,128)(2,1)S(1)} %maximum_select_fusion.1.refs_8_) | copy-start | bytes 3145732
  151.5 13.1 %collective-permute-start.7 = (bf16[512,1024]{1,0:T(8,128)(2,1)S(1)}, bf16[512,1024]{1,0:T(8,128)(2,1)S(1)}, u32[]{:S(2)}, u32[]{:S(2)}) collective-permute-start(bf16[512,1024]{1,0:T(8,128)(2,1)S(1)} %maximum_select_fusion.1.refs_8_), channel_id=1, source_target_pairs={{0,4},{1,5},{2,6},{3,7},{4,0},{5,1},{6,2},{7,3},{8,12},{9,13},{10,... | collective-permute-start | bytes 3145736 | tf_op jit(solution)/shard_map/ppermute | solution.py:243
  164.6 2.4 copy-start.27
  166.9 2.7 copy-start.54
  168.7 3.4 copy-start.28
  222.3 2.3 copy-start.23
  227.5 2.8 copy-start.35
  227.5 2.8 copy-start.36
  227.5 2.8 copy-start.37
  230.3 3.9 copy-start.21
  234.2 53.5 %copy-start.5 = (bf16[1024,256]{1,0:T(8,128)(2,1)S(1)}, bf16[1024,256]{1,0:T(8,128)(2,1)}, u32[]{:S(2)}) copy-start(bf16[1024,256]{1,0:T(8,128)(2,1)} %copy-done.4) | copy-start | bytes 1572868
  315.5 18.2 %copy-start.10 = (bf16[1024,256]{1,0:T(8,128)(2,1)}, bf16[1024,256]{1,0:T(8,128)(2,1)S(1)}, u32[]{:S(2)}) copy-start(bf16[1024,256]{1,0:T(8,128)(2,1)S(1)} %get-tuple-element.80.refs_0_) | copy-start | bytes 1572868
  315.5 2.4 copy-start.55
  317.9 2.4 copy-start.29
  320.3 4.4 copy-start.34
  320.3 4.4 copy-start.58
  324.7 3.7 copy-start.22
  328.4 3.7 copy-start.32
  334.5 23.6 %copy-start.3 = (bf16[1024,256]{1,0:T(8,128)(2,1)S(1)}, bf16[1024,256]{1,0:T(8,128)(2,1)}, u32[]{:S(2)}) copy-start(bf16[1024,256]{1,0:T(8,128)(2,1)} %copy-done.2) | copy-start | bytes 1572868
  358.0 3.3 copy-start.7
  358.0 3.3 copy-start.9
  358.0 3.3 copy-start.11
  358.0 3.3 copy-start.15
  358.0 3.3 copy-start.17
  358.0 3.3 copy-start.19
  361.4 12.8 %copy-start.39 = (bf16[3,1024,256]{2,1,0:T(8,128)(2,1)S(1)}, bf16[3,1024,256]{2,1,0:T(8,128)(2,1)}, u32[]{:S(2)}) copy-start(bf16[3,1024,256]{2,1,0:T(8,128)(2,1)} %get-tuple-element.90) | copy-start | bytes 4718596
  374.9 2.8 copy-start.43
  374.9 4.9 copy-start.60
  375.7 3.1 copy-start.44
  377.7 2.1 copy-start.59
  383.6 2.2 copy-start.57
  385.8 3.1 copy-start.52
  385.8 3.1 copy-start.53
  556.4 3.2 copy-start.42
  559.5 1.8 copy-start.24
  561.3 3.0 copy-start.31
  564.4 2.5 copy-start.30
  566.8 2.5 copy-start.47
  566.8 3.3 copy-start.46
  569.3 2.6 copy-start.1
  (9 other events, 10.3 us)
Sparse Core Ops, SparseCore 0:
  22.5 28.8 all-gather.6
  54.9 71.5 all-gather.10
  130.1 56.6 all-gather.12
  188.5 36.0 all-gather.8
